TPU v7x, 512 devices: a whole 4x8x8 slice. The times are simulated.
512 devices in a mesh: dp: 8 (over y), ta: 16 (over z_lo, x), ha: 4 (over z_hi, core).
Axes of the slice: x: 4, y: 8, z: 8 (z_hi: 2, z_lo: 4; z = z_hi * 4 + z_lo), core: 2. Of those that a mesh axis runs over, the one named last changes fastest.
Arguments:
- decoder_feature_rows: bfloat16 [32768, 768], P(('dp', 'ta', 'ha')), parts along dimension 0, may hold values from -12 to 12
- slot_row_index: int32 [32768], P('dp'), parts along dimension 0, may hold values from 0 to 4095, as said below
- latent_frame_count: int32 [48], P('dp'), parts along dimension 0, may hold values from 1 to 81, 256 in all
- first_norm_gain: float32 [384], replicated, may hold values from 0.1 to 1.9
- first_norm_bias: float32 [384], replicated, may hold values from -3 to 3
- first_convolution_weight: bfloat16 [3, 3, 3, 384, 384], P(None, None, None, 'ha'), may hold values from -0.0625 to 0.0625
- first_convolution_bias: float32 [384], replicated, may hold values from -3 to 3
- second_norm_gain: float32 [384], replicated, may hold values from 0.1 to 1.9
- second_norm_bias: float32 [384], replicated, may hold values from -3 to 3
- second_convolution_weight: bfloat16 [3, 3, 3, 384, 384], P(None, None, None, 'ha'), may hold values from -0.0625 to 0.0625
- second_convolution_bias: float32 [384], replicated, may hold values from -3 to 3
Outputs:
- decoded: bfloat16 [2048, 16, 2, 384], P(('dp', 'ta'), 'ha'), parts along dimension 0
There are 8 independent parts, one for each index of `dp`. A program takes and returns all parts, laid end to end along the dimension named above; an argument that names none is the same for every part. Nothing has to cross between parts.
Inputs may be any that keep to these rules, and one draw needn't show every extreme that they name: `slot_row_index`: A permutation of 0 to 4095. Slot i lies on the device of flat index i // 64 over ta+ha; row g is owned by the device of ta index (g // 16) // 16 and ha index (g % 16) // 4. The slots of one device hold at most 2 rows of any one owner, and exactly 2 of some owner.
All inputs are finite; a program needn't handle non-finite values.
Results may differ from a plain program's by a relative error of at most 0.0042.
Values may be sent and summed in bfloat16 or wider, within the bound.
No kernel may reach another device: no remote copies, remote signals or barrier semaphores. Data moves between devices by JAX's collectives and lax.ppermute only.
A program may use at most 64 MiB of HBM per device.

v0:
```python
import jax
import jax.numpy as jnp
from jax import lax
from jax.sharding import PartitionSpec as P

CH = 384
GROUPS = 32
F_DEV = 16
R_DEV = 4
COLS = 2


def from_behind(value, axis, by):
    length = lax.axis_size(axis)
    pairs = [(i, i + by) for i in range(length) if 0 <= i + by < length]
    return lax.ppermute(value, axis, pairs)


def group_sums(values, groups):
    extent = values.shape
    grouped = values.reshape(extent[0], extent[1] * extent[2], groups, extent[3] // groups)
    return (jnp.sum(grouped, axis=(1, 3)), jnp.sum(grouped * grouped, axis=(1, 3)))


def normalize(values, totals, squares, entries, gain_vec, offset, groups):
    average = totals / entries
    spread = squares / entries - average * average
    inverse = lax.rsqrt(spread + 1e-06)
    extent = values.shape
    grouped = values.reshape(extent[0], extent[1], extent[2], groups, extent[3] // groups)
    centred = (grouped - average[:, None, None, :, None]) * inverse[:, None, None, :, None]
    scaled = centred.reshape(extent) * gain_vec + offset
    return jax.nn.silu(scaled).astype(jnp.bfloat16)


def extend_frames(values):
    earlier = from_behind(values[-2:], "ta", 1)
    return jnp.concatenate([earlier, values], axis=0)


def whole_rows(values):
    return lax.all_gather(values, "ha", axis=1, tiled=True)


def shared_norm(values, gain_vec, offset, entries):
    part_sums, part_squares = group_sums(values, GROUPS)
    totals, squares = lax.psum((part_sums, part_squares), "ha")
    return normalize(values, totals, squares, entries, gain_vec, offset, GROUPS)


def causal_conv(extended, weight, masks):
    frames = extended.shape[0] - 2
    image_height = extended.shape[1]
    columns = extended.shape[2]
    channels = extended.shape[3]
    outputs = weight.shape[3]
    padded = jnp.pad(extended, ((0, 0), (1, 1), (1, 1), (0, 0)))
    stacked = jnp.concatenate(
        [
            padded[time_tap : time_tap + frames] * masks[time_tap][:, None, None, None]
            for time_tap in range(3)
        ],
        axis=3,
    )
    kernel = jnp.transpose(weight, (0, 4, 1, 2, 3)).reshape(3 * channels, 9 * outputs)
    taps = jnp.dot(stacked.reshape(-1, 3 * channels), kernel, preferred_element_type=jnp.float32)
    taps = taps.reshape(frames, image_height + 2, columns + 2, 9, outputs)
    total = jnp.zeros((frames, image_height, columns, outputs), jnp.float32)
    for row_tap in range(3):
        for col_tap in range(3):
            total = (
                total
                + taps[
                    :,
                    row_tap : row_tap + image_height,
                    col_tap : col_tap + columns,
                    3 * row_tap + col_tap,
                ]
            )
    return total


def rearrange_rows(decoder_feature_rows, slot_row_index, image_height):
    devices = lax.axis_size(("ta", "ha"))
    ha_count = lax.axis_size("ha")
    number_of_slots = decoder_feature_rows.shape[0]
    capacity = number_of_slots // devices + 1
    own_index = lax.axis_index(("ta", "ha"))
    plan_grid = slot_row_index.reshape(devices, number_of_slots)
    frame_of = plan_grid // image_height
    row_in = plan_grid % image_height
    owners = frame_of // F_DEV * ha_count + row_in // R_DEV
    places = frame_of % F_DEV * R_DEV + row_in % R_DEV
    my_owners = lax.dynamic_slice_in_dim(owners, own_index, 1, 0)[0]
    matches = (my_owners[:, None] == jnp.arange(devices, dtype=jnp.int32)[None, :]).astype(
        jnp.int32
    )
    ranking = jnp.sum((jnp.cumsum(matches, axis=0) - 1) * matches, axis=1)
    position = my_owners * capacity + ranking
    row_packing = (
        jnp.arange(devices * capacity, dtype=jnp.int32)[:, None] == position[None, :]
    ).astype(jnp.bfloat16)
    departing_rows = jnp.dot(
        row_packing, decoder_feature_rows, preferred_element_type=jnp.float32
    ).astype(jnp.bfloat16)
    incoming = lax.all_to_all(
        departing_rows.reshape(devices, capacity, -1),
        ("ta", "ha"),
        split_axis=0,
        concat_axis=0,
        tiled=True,
    )
    arrivals = (owners == own_index).astype(jnp.int32)
    order_in = jnp.cumsum(arrivals, axis=1) - 1
    chosen = arrivals[:, None, :] * (
        order_in[:, None, :] == jnp.arange(capacity, dtype=jnp.int32)[None, :, None]
    ).astype(jnp.int32)
    filled = jnp.sum(chosen, axis=2)
    target = jnp.sum(chosen * places[:, None, :], axis=2) + filled - 1
    unpack = (
        jnp.arange(number_of_slots, dtype=jnp.int32)[:, None] == target.reshape(1, -1)
    ).astype(jnp.bfloat16)
    placed = jnp.dot(
        unpack, incoming.reshape(devices * capacity, -1), preferred_element_type=jnp.float32
    )
    return placed.astype(jnp.bfloat16).reshape(F_DEV, R_DEV, COLS, CH)


def local(
    decoder_feature_rows,
    slot_row_index,
    latent_frame_count,
    first_norm_gain,
    first_norm_bias,
    first_convolution_weight,
    first_convolution_bias,
    second_norm_gain,
    second_norm_bias,
    second_convolution_weight,
    second_convolution_bias,
):
    ha_count = lax.axis_size("ha")
    ha_index = lax.axis_index("ha")
    image_height = R_DEV * ha_count
    out_width = CH // ha_count
    latent_row_list = rearrange_rows(decoder_feature_rows, slot_row_index, image_height)
    frame_ids = lax.axis_index("ta") * F_DEV + jnp.arange(F_DEV, dtype=jnp.int32)
    video_ends = jnp.cumsum(latent_frame_count)
    starts = jnp.sum(
        jnp.where(video_ends[None, :] <= frame_ids[:, None], latent_frame_count[None, :], 0), axis=1
    )
    masks = jnp.stack([frame_ids - 2 + time_tap >= starts for time_tap in range(3)]).astype(
        jnp.bfloat16
    )
    bias_first = lax.dynamic_slice_in_dim(first_convolution_bias, ha_index * out_width, out_width)
    bias_second = lax.dynamic_slice_in_dim(second_convolution_bias, ha_index * out_width, out_width)
    entries = image_height * COLS * (CH // GROUPS)
    latent_float = latent_row_list.astype(jnp.float32)
    first_act = shared_norm(latent_float, first_norm_gain, first_norm_bias, entries)
    hidden = (
        causal_conv(whole_rows(extend_frames(first_act)), first_convolution_weight, masks)
        + bias_first
    ).astype(jnp.bfloat16)
    hidden_rows = lax.all_to_all(hidden, "ha", split_axis=1, concat_axis=3, tiled=True)
    second_act = shared_norm(
        hidden_rows.astype(jnp.float32), second_norm_gain, second_norm_bias, entries
    )
    result = (
        causal_conv(whole_rows(extend_frames(second_act)), second_convolution_weight, masks)
        + bias_second
    )
    output_rows = lax.all_to_all(result, "ha", split_axis=1, concat_axis=3, tiled=True)
    return (output_rows + latent_float).astype(jnp.bfloat16)


def solution(mesh):
    in_specs = (
        P(("dp", "ta", "ha"), None),
        P("dp"),
        P("dp"),
        P(),
        P(),
        P(None, None, None, "ha", None),
        P(),
        P(),
        P(),
        P(None, None, None, "ha", None),
        P(),
    )
    out_specs = P(("dp", "ta"), "ha", None, None)
    return jax.shard_map(local, mesh=mesh, in_specs=in_specs, out_specs=out_specs, check_vma=False)
```

profile of v0, /device:TPU:112, one launch (start us, length us, event | category | flops | bytes accessed | tf_op | source)
XLA Modules:
  0.0 152.8 jit_solution(9828036770972007920)
XLA Ops:
  0.0 0.8 reshape.350
  1.5 0.8 reshape.351
  2.2 13.0 %all-to-all-start = ((bf16[64,2,768]{2,1,0:T(2,128)(2,1)}), bf16[64,2,768]{2,1,0:T(2,128)(2,1)S(1)}, u32[]{:S(2)}, u32[]{:S(2)}) async-start(bf16[64,2,768]{2,1,0:T(2,128)(2,1)} %reshape.351), calls=%async_computation | async-start | bytes 393216 | tf_op jit(solution)/shard_map/all_to_all | solution.py:106
  15.2 0.2 reduce_window_sum.29
  15.6 0.8 reduce-window.8
  16.5 0.7 select_reduce_fusion.2
  17.6 9.4 %all-to-all-done = bf16[64,2,768]{2,1,0:T(2,128)(2,1)S(1)} async-done(((bf16[64,2,768]{2,1,0:T(2,128)(2,1)}), bf16[64,2,768]{2,1,0:T(2,128)(2,1)S(1)}, u32[]{:S(2)}, u32[]{:S(2)}) %all-to-all-start) | async-done | bytes 196640 | tf_op jit(solution)/shard_map/all_to_all | solution.py:106
  27.2 2.3 %reshape.358 = f32[16,8,32,12]{3,2,1,0:T(8,128)S(1)} reshape(f32[64,768]{1,0:T(8,128)S(1)} %fusion.16) | data formatting | bytes 393216 | tf_op jit(solution)/shard_map/convert_element_type | solution.py:158
  29.7 0.4 fusion.44
  30.1 19.1 %all-reduce.3 = (f32[16,32]{1,0:T(8,128)S(1)}, f32[16,32]{1,0:T(8,128)S(1)}) all-reduce(f32[16,32]{1,0:T(8,128)S(1)} %get-tuple-element.6, f32[16,32]{1,0:T(8,128)S(1)} %get-tuple-element.5), channel_id=1, replica_groups=mesh['dp'=8,'ta'=16,'ha'=4] {'ha'}, use_global_device_ids=true, to_apply=%region_8.9 | all-reduce | flops 1024 | bytes 8192 | tf_op jit(solution)/shard_map/psum | solution.py:47
  49.9 2.4 %collective-permute-start = (bf16[2,4,2,384]{3,0,2,1:T(2,128)(2,1)S(1)}, bf16[2,4,2,384]{3,0,2,1:T(2,128)(2,1)S(1)}, u32[]{:S(2)}, u32[]{:S(2)}) collective-permute-start(bf16[2,4,2,384]{3,0,2,1:T(2,128)(2,1)S(1)} %slice.119), channel_id=1, source_target_pairs={{0,4},{4,8},{8,12},{12,16},{16,20},{20,24},{24,28},{28,32},{32,36}... | collective-permute-start | bytes 36872 | tf_op jit(solution)/shard_map/ppermute | solution.py:16
  52.4 2.9 %copy.55 = bf16[3,384,3,3,96]{1,0,4,3,2:T(4,128)(2,1)S(1)} copy(bf16[3,384,3,3,96]{1,4,3,2,0:T(8,128)(2,1)} %bitcast.90) | data formatting | bytes 3981312 | tf_op jit(solution)/shard_map/transpose | solution.py:65
  55.3 0.4 copy.67
  55.7 0.8 dynamic_slice.10
  56.5 1.2 collective-permute-done
  57.8 11.8 %all_gather.6 = bf16[18,16,2,384]{3,2,0,1:T(2,128)(2,1)S(1)} all-gather(bf16[18,4,2,384]{3,2,0,1:T(2,128)(2,1)S(1)} %copy.53), channel_id=1, replica_groups=mesh['dp'=8,'ta'=16,'ha'=4] {'ha'}, dimensions={1}, use_global_device_ids=true | all-gather | bytes 552960 | tf_op jit(solution)/shard_map/all_gather | solution.py:42
  69.6 0.4 fusion.10
  70.0 5.5 %fusion = f32[16,18,4,9,96]{4,1,3,2,0:T(8,128)S(1)} fusion(bf16[9,96,1152,1,1]{2,1,0,4,3:T(8,128)(2,1)S(1)} %bitcast.92, bf16[16,18,4,384]{3,1,2,0:T(8,128)(2,1)S(1)} %get-tuple-element.22, bf16[16,18,4,384]{3,1,2,0:T(8,128)(2,1)S(1)} %get-tuple-element.21, bf16[16,18,4,384]{3,1,2,0:T(8,128)(2,1)S(1)} %get-tuple-element.20), kind=kOutput, calls=%fused_computation.1 | convolution fusion | flops 2301198336 | bytes 8626176 | tf_op jit(solution)/shard_map/dot_general | solution.py:66
  75.8 12.6 %all_to_all.32 = bf16[16,16,2,96]{3,2,0,1:T(2,128)(2,1)S(1)} all-to-all(bf16[16,16,2,96]{3,2,0,1:T(2,128)(2,1)S(1)} %copy.56), channel_id=1, replica_groups=mesh['dp'=8,'ta'=16,'ha'=4] {'ha'}, dimensions={1} | all-to-all | bytes 196608 | tf_op jit(solution)/shard_map/all_to_all | solution.py:164
  88.6 0.3 fusion.43
  89.6 18.0 %all-reduce.2 = (f32[16,32]{1,0:T(8,128)S(1)}, f32[16,32]{1,0:T(8,128)S(1)}) all-reduce(f32[16,32]{1,0:T(8,128)S(1)} %reduce_sum.103, f32[16,32]{1,0:T(8,128)S(1)} %reduce_sum.100), channel_id=1, replica_groups=mesh['dp'=8,'ta'=16,'ha'=4] {'ha'}, use_global_device_ids=true, to_apply=%region_16.17 | all-reduce | flops 1024 | bytes 8192 | tf_op jit(solution)/shard_map/psum | solution.py:47
  108.5 1.9 %collective-permute-start.1 = (bf16[2,4,2,384]{3,0,2,1:T(2,128)(2,1)S(1)}, bf16[2,4,2,384]{3,0,2,1:T(2,128)(2,1)S(1)}, u32[]{:S(2)}, u32[]{:S(2)}) collective-permute-start(bf16[2,4,2,384]{3,0,2,1:T(2,128)(2,1)S(1)} %slice.129), channel_id=1, source_target_pairs={{0,4},{4,8},{8,12},{12,16},{16,20},{20,24},{24,28},{28,32},{32,36}... | collective-permute-start | bytes 36872 | tf_op jit(solution)/shard_map/ppermute | solution.py:16
  110.4 1.4 copy.60
  111.8 0.4 copy.68
  112.2 0.8 dynamic_slice.11
  112.9 3.2 %collective-permute-done.1 = bf16[2,4,2,384]{3,0,2,1:T(2,128)(2,1)S(1)} collective-permute-done((bf16[2,4,2,384]{3,0,2,1:T(2,128)(2,1)S(1)}, bf16[2,4,2,384]{3,0,2,1:T(2,128)(2,1)S(1)}, u32[]{:S(2)}, u32[]{:S(2)}) %collective-permute-start.1) | collective-permute-done | bytes 12320 | tf_op jit(solution)/shard_map/ppermute | solution.py:16
  116.3 12.8 %all_gather.7 = bf16[18,16,2,384]{3,2,0,1:T(2,128)(2,1)S(1)} all-gather(bf16[18,4,2,384]{3,2,0,1:T(2,128)(2,1)S(1)} %copy.58), channel_id=1, replica_groups=mesh['dp'=8,'ta'=16,'ha'=4] {'ha'}, dimensions={1}, use_global_device_ids=true | all-gather | bytes 552960 | tf_op jit(solution)/shard_map/all_gather | solution.py:42
  129.2 0.4 fusion.13
  129.6 5.4 %fusion.5 = f32[16,18,4,9,96]{4,1,3,2,0:T(8,128)S(1)} fusion(bf16[9,96,1152,1,1]{2,1,0,4,3:T(8,128)(2,1)S(1)} %bitcast.93, bf16[16,18,4,384]{3,1,2,0:T(8,128)(2,1)S(1)} %get-tuple-element.19, bf16[16,18,4,384]{3,1,2,0:T(8,128)(2,1)S(1)} %get-tuple-element.18, bf16[16,18,4,384]{3,1,2,0:T(8,128)(2,1)S(1)} %get-tuple-element.17), kind=kOutput, calls=%fused_computation.7 | convolution fusion | flops 2301198336 | bytes 8626176 | tf_op jit(solution)/shard_map/dot_general | solution.py:66
  135.3 16.3 %all_to_all.33 = f32[16,16,2,96]{3,2,0,1:T(2,128)S(1)} all-to-all(f32[16,16,2,96]{3,2,0,1:T(2,128)S(1)} %copy.61), channel_id=1, replica_groups=mesh['dp'=8,'ta'=16,'ha'=4] {'ha'}, dimensions={1} | all-to-all | bytes 393216 | tf_op jit(solution)/shard_map/all_to_all | solution.py:172
  151.7 0.3 all_to_all.28
  152.1 0.7 add_convert_fusion
  (63 shorter events, 5.0 us)
Async XLA Ops:
  0.0 1.3 copy-start
  2.2 24.7 %all-to-all-start = ((bf16[64,2,768]{2,1,0:T(2,128)(2,1)}), bf16[64,2,768]{2,1,0:T(2,128)(2,1)S(1)}, u32[]{:S(2)}, u32[]{:S(2)}) async-start(bf16[64,2,768]{2,1,0:T(2,128)(2,1)} %reshape.351), calls=%async_computation | async-start | bytes 393216 | tf_op jit(solution)/shard_map/all_to_all | solution.py:106
  29.5 20.3 %copy-start.2 = (f32[384]{0:T(512)S(1)}, f32[384]{0:T(512)}, u32[]{:S(2)}) copy-start(f32[384]{0:T(512)} %param.15) | copy-start | bytes 4612
  29.5 20.3 %copy-start.3 = (f32[384]{0:T(512)S(1)}, f32[384]{0:T(512)}, u32[]{:S(2)}) copy-start(f32[384]{0:T(512)} %param.14) | copy-start | bytes 4612
  49.9 7.7 %collective-permute-start = (bf16[2,4,2,384]{3,0,2,1:T(2,128)(2,1)S(1)}, bf16[2,4,2,384]{3,0,2,1:T(2,128)(2,1)S(1)}, u32[]{:S(2)}, u32[]{:S(2)}) collective-permute-start(bf16[2,4,2,384]{3,0,2,1:T(2,128)(2,1)S(1)} %slice.119), channel_id=1, source_target_pairs={{0,4},{4,8},{8,12},{12,16},{16,20},{20,24},{24,28},{28,32},{32,36}... | collective-permute-start | bytes 36872 | tf_op jit(solution)/shard_map/ppermute | solution.py:16
  88.4 19.9 %copy-start.4 = (f32[384]{0:T(512)S(1)}, f32[384]{0:T(512)}, u32[]{:S(2)}) copy-start(f32[384]{0:T(512)} %param.19) | copy-start | bytes 4612
  88.4 19.9 %copy-start.5 = (f32[384]{0:T(512)S(1)}, f32[384]{0:T(512)}, u32[]{:S(2)}) copy-start(f32[384]{0:T(512)} %param.18) | copy-start | bytes 4612
  88.6 21.8 %copy-start.1 = (bf16[3,3,3,96,384]{4,3,2,1,0:T(8,128)(2,1)S(1)}, bf16[3,3,3,96,384]{4,3,2,1,0:T(8,128)(2,1)}, u32[]{:S(2)}) copy-start(bf16[3,3,3,96,384]{4,3,2,1,0:T(8,128)(2,1)} %param.20) | copy-start | bytes 5971972
  108.5 7.7 %collective-permute-start.1 = (bf16[2,4,2,384]{3,0,2,1:T(2,128)(2,1)S(1)}, bf16[2,4,2,384]{3,0,2,1:T(2,128)(2,1)S(1)}, u32[]{:S(2)}, u32[]{:S(2)}) collective-permute-start(bf16[2,4,2,384]{3,0,2,1:T(2,128)(2,1)S(1)} %slice.129), channel_id=1, source_target_pairs={{0,4},{4,8},{8,12},{12,16},{16,20},{20,24},{24,28},{28,32},{32,36}... | collective-permute-start | bytes 36872 | tf_op jit(solution)/shard_map/ppermute | solution.py:16
where the time goes:
time: 153 us
  blocking collectives  90.5 us (59%)
  starting transfers between devices  17.4 us (11%)
  waiting for transfers between devices  13.8 us (9%)
  local copies, waits for them, and re-layouts  13.7 us (9%)
  matrix products  11.2 us (7%)
  other arithmetic  5.8 us (4%)
    psum x2, blocking collectives, shared_norm(): totals, squares = lax.psum((part_sums, part_squares), 'ha')  37 us
    all_gather x2, blocking collectives, whole_rows(): return lax.all_gather(values, 'ha', axis=1, tiled=True)  24.6 us
    all_to_all x1, blocking collectives, local(): lax.all_to_all(result, 'ha', split_axis=1, concat_axis=3, tiled=True)  16.3 us
    all_to_all x1, starting transfers between devices, rearrange_rows(): lax.all_to_all(departing_rows.reshape(devices, capacity, -1), ('ta', 'ha'...  13 us
    all_to_all x1, blocking collectives, local(): lax.all_to_all(hidden, 'ha', split_axis=1, concat_axis=3, tiled=True)  12.6 us
    dot_general x2, matrix products, causal_conv(): jnp.dot(stacked.reshape(-1, 3 * channels), kernel, preferred_element_type...  10.8 us
    all_to_all x1, waiting for transfers between devices, rearrange_rows(): lax.all_to_all(departing_rows.reshape(devices, capacity, -1), ('ta', 'ha'...  9.42 us
    ppermute x2, waiting for transfers between devices, from_behind(): return lax.ppermute(value, axis, pairs)  4.42 us
  transfers between devices with their start and end apart: 3, of which 3 were waited for; matrix products, arithmetic and copies ran while one was open for 6% of the time, Pallas kernels for 0%

commit v1 on v0

v1 whole, which is shorter than its diff:
```python
import functools

import jax
import jax.numpy as jnp
from jax import lax
from jax.experimental import pallas as pl
from jax.experimental.pallas import tpu as pltpu
from jax.sharding import PartitionSpec as P

CH = 384
WIDE = 768
GROUP = 12
ROWS = 16
OWN = 96
PAIR = 192
F_DEV = 16
BLOCK = 256
SLOTS = 64
CAP = 8
VIDEOS = 6
F32, BF16, I32 = jnp.float32, jnp.bfloat16, jnp.int32
VMEM_LIMIT = 24 * 2**20


def dot(a, b):
    return jnp.dot(a, b, preferred_element_type=F32)


def dot_nt(a, b):
    return lax.dot_general(a, b, (((1,), (1,)), ((), ())), preferred_element_type=F32)


def iota(shape, axis):
    return lax.broadcasted_iota(I32, shape, axis)


def twelfth(v):
    return (v * 43691) >> 19


def three(v):
    high = v.astype(BF16)
    rest = v - high.astype(F32)
    middle = rest.astype(BF16)
    low = (rest - middle.astype(F32)).astype(BF16)
    return high, middle, low


def pack_kernel(at_ref, plan_ref, rows_ref, out_ref):
    own = at_ref[0] * 4 + at_ref[1]
    ids = plan_ref[pl.ds(own // 2, 1), :]
    ids = jnp.where(own % 2 == 1, pltpu.roll(ids, 64, 1), ids)
    block = ids >> 8
    hit = iota((16, 128), 0) == block
    before = dot(hit.astype(BF16), (iota((128, 128), 0) < iota((128, 128), 1)).astype(BF16))
    rank = jnp.sum(jnp.where(hit, before, 0.0), axis=0, keepdims=True)
    position = block * CAP + rank.astype(I32)
    place = iota((256, 128), 0)
    hot = ((place >> 4) * CAP + (place & 7) == position).astype(BF16)
    out_ref[...] = dot(hot[:, :SLOTS], rows_ref[...]).astype(BF16)


def table_kernel(at_ref, plan_ref, out_ref):
    plan = plan_ref[...]
    match = (plan >> 8) == at_ref[0]
    i, j = iota((128, 128), 0), iota((128, 128), 1)
    before = dot(match.astype(BF16), ((i < j) & ((i >> 6) == (j >> 6))).astype(BF16))
    value = jnp.where(match, (plan & 255) + 1, 0).astype(F32)
    ranked = jnp.concatenate([jnp.where(before == k, value, 0.0) for k in range(CAP)], axis=0)
    half = ((iota((8, 128), 1) >> 6) == iota((8, 128), 0)).astype(BF16)
    held = dot_nt(half, ranked.astype(BF16))
    q, p = iota((256, 256), 0), iota((256, 256), 1)
    held = dot(held.astype(BF16), (q == (p & 7) * 32 + (p >> 3)).astype(BF16))
    want = (q + 1).astype(F32)
    out_ref[:, 0:256] = (held[0:1] == want).astype(BF16)
    out_ref[:, 256:512] = (held[1:2] == want).astype(BF16)


def unpack_kernel(table_ref, packed_ref, out_ref, tail_ref):
    rows = dot(table_ref[...], packed_ref[...]).astype(BF16)
    out_ref[...] = rows
    tail_ref[...] = rows[BLOCK - 64 :]


def frame_stats(values, width):
    rows = values.shape[0]
    pick = ((iota((16, rows), 1) >> 4) == iota((16, rows), 0)).astype(BF16)
    wide = values.astype(F32)
    square = wide * wide
    high = square.astype(BF16)
    low = (square - high.astype(F32)).astype(BF16)
    sums = dot(pick, values)
    squares = dot(pick, high) + dot(pick, low)
    if width == WIDE:
        sums = sums[:, :CH] + sums[:, CH:]
        squares = squares[:, :CH] + squares[:, CH:]
        lanes = CH
        first, second = iota((CH, CH), 0), iota((CH, CH), 1)
    else:
        lanes = PAIR
        first, second = iota((PAIR, PAIR), 0), iota((PAIR, PAIR), 1)
        first = jnp.where(first >= OWN, first - OWN, first)
        second = jnp.where(second >= OWN, second - OWN, second)
    same = (twelfth(first) == twelfth(second)).astype(BF16)
    both = jnp.concatenate([sums, squares], axis=0)
    total = sum(dot(part, same) for part in three(both))
    entries = ROWS * 2 * GROUP
    mean = total[0:16] / entries
    var = total[16:32] / entries - mean * mean
    return mean, lax.rsqrt(var + 1e-06)


def silu(v):
    return v / (1.0 + jnp.exp(-v))


def store_taps(taps_ref, at, act):
    row = iota((ROWS, WIDE), 0)
    taps_ref[0, at : at + ROWS, :] = jnp.where(row == 0, 0.0, pltpu.roll(act, 1, 0)).astype(BF16)
    taps_ref[1, at : at + ROWS, :] = act.astype(BF16)
    taps_ref[2, at : at + ROWS, :] = jnp.where(row == ROWS - 1, 0.0, pltpu.roll(act, ROWS - 1, 0)).astype(BF16)


def norm_first(rows_ref, gain, bias, taps_ref, at):
    frames = rows_ref.shape[0] // ROWS
    mean, inverse = frame_stats(rows_ref[...], WIDE)
    for f in range(frames):
        value = rows_ref[f * ROWS : (f + 1) * ROWS, :].astype(F32)
        m, s = mean[f : f + 1], inverse[f : f + 1]
        halves = [
            silu((value[:, c * CH : (c + 1) * CH] - m) * s * gain + bias) for c in range(2)
        ]
        store_taps(taps_ref, at + f * ROWS, jnp.concatenate(halves, axis=1))


def convolve(taps_ref, weight_ref, rows, first_frame, count_ref):
    totals = []
    for a in range(3):
        acc = None
        for b in range(3):
            for c in range(2):
                part = dot_nt(
                    taps_ref[b, a * ROWS : a * ROWS + rows, c * CH : (c + 1) * CH],
                    weight_ref[3 * a + b, c * OWN : c * OWN + PAIR, :],
                )
                acc = part if acc is None else acc + part
        totals.append(acc)
    frame = first_frame + (iota((rows, 1), 0) >> 4)
    start = jnp.zeros((rows, 1), I32)
    end = jnp.int32(0)
    for v in range(VIDEOS):
        count = count_ref[v]
        end = end + count
        start = start + jnp.where(frame >= end, count, 0)
    total = totals[2]
    for a in range(2):
        total = total + totals[a] * jnp.where(frame - 2 + a >= start, 1.0, 0.0)
    return total


def norm_second(hidden, gain, bias, out_ref, at):
    mean, inverse = frame_stats(hidden, PAIR)
    for f in range(hidden.shape[0] // ROWS):
        value = hidden[f * ROWS : (f + 1) * ROWS].astype(F32)
        act = silu((value - mean[f : f + 1]) * inverse[f : f + 1] * gain + bias)
        out_ref[at + f * ROWS : at + (f + 1) * ROWS, :] = act.astype(BF16)


def main_kernel(at_ref, count_ref, rows_ref, wide_ref, own_ref, weight_ref, act_ref, rest_ref, taps_ref):
    base = at_ref[0] * F_DEV
    norm_first(rows_ref, wide_ref[0:1], wide_ref[1:2], taps_ref, 0)
    rows = BLOCK - 2 * ROWS
    hidden = convolve(taps_ref, weight_ref, rows, base + 2, count_ref) + own_ref[0:1]
    norm_second(hidden.astype(BF16), own_ref[1:2], own_ref[2:3], act_ref, 0)
    lane = iota((WIDE, PAIR), 1)
    source = at_ref[1] * OWN + jnp.where(lane < OWN, CH + lane, lane - OWN)
    own = (iota((WIDE, PAIR), 0) == source).astype(BF16)
    rest_ref[...] = dot(rows_ref[...], own).astype(BF16)


def halo_kernel(at_ref, count_ref, earlier_ref, rows_ref, wide_ref, own_ref, weight_ref, main_ref, act_ref, taps_ref, join_ref):
    base = at_ref[0] * F_DEV
    join_ref[0:64, :] = earlier_ref[...]
    join_ref[64:96, :] = rows_ref[0:32, :]
    norm_first(join_ref, wide_ref[0:1], wide_ref[1:2], taps_ref, 0)
    hidden = convolve(taps_ref, weight_ref, 64, base - 2, count_ref) + own_ref[0:1]
    norm_second(hidden.astype(BF16), own_ref[1:2], own_ref[2:3], act_ref, 0)
    act_ref[64:288, :] = main_ref[...]


def last_kernel(at_ref, count_ref, act_ref, rest_ref, own_ref, weight_ref, out_ref, taps_ref):
    for f in range(F_DEV + 2):
        parts = [act_ref[h, f * ROWS : (f + 1) * ROWS, :].astype(F32) for h in range(4)]
        whole = jnp.concatenate([p[:, OWN:] for p in parts] + [p[:, :OWN] for p in parts], axis=1)
        store_taps(taps_ref, f * ROWS, whole)
    total = convolve(taps_ref, weight_ref, BLOCK, at_ref[0] * F_DEV, count_ref)
    total = (total + own_ref[3:4] + rest_ref[...].astype(F32)).astype(BF16)
    to, at = iota((BLOCK, BLOCK), 0), iota((BLOCK, BLOCK), 1)
    order = (((to >> 2) & 15) * ROWS + (to >> 6) * 4 + (to & 3) == at).astype(BF16)
    out_ref[...] = dot(order, total).astype(BF16)


def join_kernel(parts_ref, out_ref):
    parts = [parts_ref[h].astype(F32) for h in range(4)]
    zero = jnp.concatenate([p[:, OWN:] for p in parts], axis=1)
    one = jnp.concatenate([p[:, :OWN] for p in parts], axis=1)
    out_ref[...] = jnp.stack([zero, one], axis=1).astype(BF16).reshape(F_DEV, 4, 2, CH)


def call(kernel, shapes, n_scalars, n_arrays, scratch=(), flops=0, **more):
    many = isinstance(shapes, (list, tuple))
    out_shape = [jax.ShapeDtypeStruct(s, BF16) for s in shapes] if many else shapes
    return pl.pallas_call(
        kernel,
        out_shape=out_shape,
        in_specs=[pl.BlockSpec(memory_space=pltpu.SMEM)] * n_scalars
        + [pl.BlockSpec(memory_space=pltpu.VMEM)] * n_arrays,
        out_specs=[pl.BlockSpec(memory_space=pltpu.VMEM)] * len(out_shape),
        scratch_shapes=[pltpu.VMEM(s, BF16) for s in scratch],
        compiler_params=pltpu.CompilerParams(vmem_limit_bytes=VMEM_LIMIT),
        cost_estimate=pl.CostEstimate(flops=flops, bytes_accessed=2**20, transcendentals=0),
        **more,
    )


def local(
    decoder_feature_rows,
    slot_row_index,
    latent_frame_count,
    first_norm_gain,
    first_norm_bias,
    first_convolution_weight,
    first_convolution_bias,
    second_norm_gain,
    second_norm_bias,
    second_convolution_weight,
    second_convolution_bias,
):
    ta, ha = lax.axis_index("ta"), lax.axis_index("ha")
    at = jnp.stack([ta, ha]).astype(I32)
    plan = slot_row_index.reshape(32, 128)
    n_ta = lax.axis_size("ta")
    same_core = [[t * 4 + z * 2 + c for t in range(n_ta) for z in range(2)] for c in range(2)]
    chips = [[0, 1], [2, 3]]

    [packed] = call(pack_kernel, [(256, WIDE)], 1, 2, flops=10**7)(at, plan, decoder_feature_rows)
    arrived = lax.all_to_all(
        packed.reshape(32, CAP, WIDE), ("ta", "ha"), 0, 0, axis_index_groups=same_core, tiled=True
    ).reshape(256, WIDE)
    [table] = call(table_kernel, [(BLOCK, 512)], 1, 1, flops=10**7)(at, plan)
    wide = jnp.stack([first_norm_gain, first_norm_bias])
    own = jnp.stack([first_convolution_bias, second_norm_gain, second_norm_bias, second_convolution_bias])
    own = lax.dynamic_slice_in_dim(own, ha * OWN, OWN, 1)
    own = jnp.concatenate([own, own], axis=1)
    first = first_convolution_weight.reshape(9, 3 * OWN, CH)
    second = second_convolution_weight.reshape(9, 3 * OWN, CH)
    both = lax.all_gather(arrived, "ha", axis=0, axis_index_groups=chips, tiled=True)
    rows, tail = call(unpack_kernel, [(BLOCK, WIDE), (64, WIDE)], 0, 2, flops=10**8)(table, both)
    earlier = lax.ppermute(tail, "ta", [(i, i + 1) for i in range(n_ta - 1)])
    act, rest = call(
        main_kernel, [(224, PAIR), (BLOCK, PAIR)], 2, 4, [(3, BLOCK, WIDE)], flops=2 * 10**9
    )(at, latent_frame_count, rows, wide, own, first)
    [act] = call(
        halo_kernel, [(288, PAIR)], 2, 6, [(3, 96, WIDE), (96, WIDE)], flops=10**9
    )(at, latent_frame_count, earlier, rows, wide, own, first, act)
    acts = lax.all_gather(act, "ha", axis=0, tiled=False)
    [out] = call(last_kernel, [(BLOCK, PAIR)], 2, 4, [(3, 288, WIDE)], flops=2 * 10**9)(
        at, latent_frame_count, acts, rest, own, second
    )
    parts = lax.all_to_all(out.reshape(4, 64, PAIR), "ha", 0, 0, tiled=True)
    [joined] = call(join_kernel, [(F_DEV, 4, 2, CH)], 0, 1)(parts)
    return joined


def solution(mesh):
    in_specs = (
        P(("dp", "ta", "ha"), None),
        P("dp"),
        P("dp"),
        P(),
        P(),
        P(None, None, None, "ha", None),
        P(),
        P(),
        P(),
        P(None, None, None, "ha", None),
        P(),
    )
    out_specs = P(("dp", "ta"), "ha", None, None)
    return jax.shard_map(local, mesh=mesh, in_specs=in_specs, out_specs=out_specs, check_vma=False)
```

time: 153 us -> 74.3 us (0.49)
  the two profiles are of different devices: /device:TPU:112 before, /device:TPU:96 now
where the time goes in v1:
time: 74.3 us; the launch traced here: 73.7 us
  blocking collectives  27.2 us (37%)
  starting transfers between devices  15.1 us (20%)
  Pallas kernels  12.4 us (17%)
  waiting for transfers between devices  12.2 us (16%)
  local copies, waits for them, and re-layouts  6.44 us (9%)
    all_gather x1, blocking collectives, local(): acts = lax.all_gather(act, 'ha', axis=0, tiled=False)  13.2 us
    all_to_all x1, starting transfers between devices, local(): lax.all_to_all(packed.reshape(32, CAP, WIDE), ('ta', 'ha'), 0, 0, axis_in...  12.6 us
    all_to_all x1, blocking collectives, local(): parts = lax.all_to_all(out.reshape(4, 64, PAIR), 'ha', 0, 0, tiled=True)  11.7 us
    all_to_all x1, waiting for transfers between devices, local(): lax.all_to_all(packed.reshape(32, CAP, WIDE), ('ta', 'ha'), 0, 0, axis_in...  9.4 us
    pallas_call x1, Pallas kernels, local(): call(main_kernel, [(224, PAIR), (BLOCK, PAIR)], 2, 4, [(3, BLOCK, WIDE)],...  3.51 us
    ppermute x1, waiting for transfers between devices, local(): earlier = lax.ppermute(tail, 'ta', [(i, i + 1) for i in range(n_ta - 1)])  2.78 us
    another operation x4, local copies, waits for them, and re-layouts, local(): jnp.stack([first_convolution_bias, second_norm_gain, second_norm_bias, se...  2.73 us
    pallas_call x1, Pallas kernels, local(): call(halo_kernel, [(288, PAIR)], 2, 6, [(3, 96, WIDE), (96, WIDE)], flops...  2.59 us
  transfers between devices with their start and end apart: 2, of which 2 were waited for; matrix products, arithmetic and copies ran while one was open for 6% of the time, Pallas kernels for 6%

profile of v1, /device:TPU:96, one launch (start us, length us, event | category | flops | bytes accessed | tf_op | source)
XLA Modules:
  0.0 73.7 jit_solution(167001304199709717)
XLA Ops:
  0.0 0.0 copy-start.5
  0.0 0.1 pad_add_fusion.at_ref
  0.1 0.0 copy-start
  0.1 0.9 %copy-done = bf16[64,768]{1,0:T(8,128)(2,1)S(1)} copy-done((bf16[64,768]{1,0:T(8,128)(2,1)S(1)}, bf16[64,768]{1,0:T(8,128)(2,1)}, u32[]{:S(2)}) %copy-start) | copy-done | bytes 98328
  1.0 0.0 copy-start.1
  1.0 0.7 copy-done.1
  1.7 1.7 %shard_map.110 = bf16[256,768]{1,0:T(8,128)(2,1)} custom-call(s32[2]{0:T(128)S(1)} %pad_add_fusion.at_ref, s32[32,128]{1,0:T(8,128)S(1)} %bitcast.11, bf16[64,768]{1,0:T(8,128)(2,1)S(1)} %copy-done), custom_call_target="tpu_custom_call" | custom-call | flops 10000000 | bytes 1048576 | tf_op jit(solution)/shard_map/pallas_call | solution.py:246
  3.4 12.6 %all-to-all-start = ((bf16[32,8,768]{2,1,0:T(8,128)(2,1)}), bf16[32,8,768]{2,1,0:T(8,128)(2,1)S(1)}, u32[]{:S(2)}, u32[]{:S(2)}) async-start(bf16[32,8,768]{2,1,0:T(8,128)(2,1)} %bitcast.3), calls=%async_computation | async-start | bytes 786432 | tf_op jit(solution)/shard_map/all_to_all | solution.py:247
  16.0 0.7 stack.39
  16.7 0.7 stack.40
  17.4 0.7 stack.41
  18.1 0.7 stack.42
  18.8 0.7 stack.36
  19.4 0.7 stack.37
  20.1 0.7 copy-done.2
  20.8 1.0 %shard_map.109.table_ref = bf16[256,512]{1,0:T(8,128)(2,1)S(1)} custom-call(s32[2]{0:T(128)S(1)} %pad_add_fusion.at_ref, s32[32,128]{1,0:T(8,128)S(1)} %bitcast.12), custom_call_target="tpu_custom_call" | custom-call | flops 10000000 | bytes 1048576 | tf_op jit(solution)/shard_map/pallas_call | solution.py:250
  21.8 0.1 fusion.2
  21.9 0.1 pad_maximum_fusion.own_ref
  22.0 9.4 %all-to-all-done = bf16[32,8,768]{2,1,0:T(8,128)(2,1)S(1)} async-done(((bf16[32,8,768]{2,1,0:T(8,128)(2,1)}), bf16[32,8,768]{2,1,0:T(8,128)(2,1)S(1)}, u32[]{:S(2)}, u32[]{:S(2)}) %all-to-all-start) | async-done | bytes 393248 | tf_op jit(solution)/shard_map/all_to_all | solution.py:247
  31.4 2.4 %all_gather.9.packed_ref = bf16[512,768]{1,0:T(8,128)(2,1)S(1)} all-gather(bf16[256,768]{1,0:T(8,128)(2,1)S(1)} %bitcast.16), channel_id=1, replica_groups={{0,1},{2,3},{4,5},{6,7},{8,9},{10,11},{12,13},{14,15},{16,17},{18,19},{..., dimensions={0}, use_global_device_ids=true | all-gather | bytes 1179648 | tf_op jit(solution)/shard_map/all_gather | solution.py:257
  33.8 0.4 shard_map.111
  34.1 2.5 %collective-permute-start = (bf16[64,768]{1,0:T(8,128)(2,1)S(1)}, bf16[64,768]{1,0:T(8,128)(2,1)S(1)}, u32[]{:S(2)}, u32[]{:S(2)}) collective-permute-start(bf16[64,768]{1,0:T(8,128)(2,1)S(1)} %get-tuple-element.9), channel_id=1, source_target_pairs={{0,4},{4,8},{8,12},{12,16},{16,20},{20,24},{24,28},{28,32},{32,36}... | collective-permute-start | bytes 294920 | tf_op jit(solution)/shard_map/ppermute | solution.py:259
  36.7 0.0 copy-done.5
  36.7 0.0 copy-done.3
  36.7 3.5 %shard_map.112 = (bf16[224,192]{1,0:T(8,128)(2,1)S(1)}, bf16[256,192]{1,0:T(8,128)(2,1)S(1)}) custom-call(s32[2]{0:T(128)S(1)} %pad_add_fusion.at_ref, s32[6]{0:T(128)S(1)} %copy-done.5, bf16[256,768]{1,0:T(8,128)(2,1)S(1)} %get-tuple-element.10.rows_ref, f32[2,384]{1,0:T(2,128)S(1)} %pad_maximum_fusion.1.wide_ref, f32[4,192]{1,0:T(4,128)S(1)} %pad_maximum_fusion.own_ref, ...), custom_call_target="tpu_custom_call" | custom-call | flops 2000000000 | bytes 1048576 | tf_op jit(solution)/shard_map/pallas_call | solution.py:260
  40.2 2.8 %collective-permute-done.earlier_ref = bf16[64,768]{1,0:T(8,128)(2,1)S(1)} collective-permute-done((bf16[64,768]{1,0:T(8,128)(2,1)S(1)}, bf16[64,768]{1,0:T(8,128)(2,1)S(1)}, u32[]{:S(2)}, u32[]{:S(2)}) %collective-permute-start) | collective-permute-done | bytes 98336 | tf_op jit(solution)/shard_map/ppermute | solution.py:259
  43.0 2.6 %shard_map.113 = bf16[288,192]{1,0:T(8,128)(2,1)S(1)} custom-call(s32[2]{0:T(128)S(1)} %pad_add_fusion.at_ref, s32[6]{0:T(128)S(1)} %copy-done.5, bf16[64,768]{1,0:T(8,128)(2,1)S(1)} %collective-permute-done.earlier_ref, bf16[256,768]{1,0:T(8,128)(2,1)S(1)} %get-tuple-element.10.rows_ref, f32[2,384]{1,0:T(2,128)S(1)} %pad_maximum_fusion.1.wide_ref, ...), custom_call_target="tpu_custom_call" | custom-call | flops 1000000000 | bytes 1048576 | tf_op jit(solution)/shard_map/pallas_call | solution.py:263
  45.6 13.2 %all-gather = bf16[1152,192]{1,0:T(8,128)(2,1)S(1)} all-gather(bf16[288,192]{1,0:T(8,128)(2,1)S(1)} %shard_map.113), channel_id=2, replica_groups=mesh['dp'=8,'ta'=16,'ha'=4] {'ha'}, dimensions={0}, use_global_device_ids=true | all-gather | bytes 552960 | tf_op jit(solution)/shard_map/all_gather | solution.py:266
  58.7 0.0 copy-done.4
  58.7 2.3 %shard_map.114 = bf16[256,192]{1,0:T(8,128)(2,1)S(1)} custom-call(s32[2]{0:T(128)S(1)} %pad_add_fusion.at_ref, s32[6]{0:T(128)S(1)} %copy-done.5, bf16[4,288,192]{2,1,0:T(8,128)(2,1)S(1)} %bitcast.9, bf16[256,192]{1,0:T(8,128)(2,1)S(1)} %get-tuple-element.12.rest_ref, f32[4,192]{1,0:T(4,128)S(1)} %pad_maximum_fusion.own_ref, bf16[9,288,384]{2,1,0:T(8,128)(2,1)S(1)} %bitcast.15), custom_call_target="tpu_custom_call" | custom-call | flops 2000000000 | bytes 1048576 | tf_op jit(solution)/shard_map/pallas_call | solution.py:267
  61.1 11.7 %all_to_all.10.parts_ref = bf16[4,64,192]{2,1,0:T(8,128)(2,1)S(1)} all-to-all(bf16[4,64,192]{2,1,0:T(8,128)(2,1)S(1)} %bitcast.10), channel_id=1, replica_groups=mesh['dp'=8,'ta'=16,'ha'=4] {'ha'}, dimensions={0} | all-to-all | bytes 196608 | tf_op jit(solution)/shard_map/all_to_all | solution.py:270
  72.8 0.9 %shard_map.115 = bf16[16,4,2,384]{3,2,1,0:T(2,128)(2,1)} custom-call(bf16[4,64,192]{2,1,0:T(8,128)(2,1)S(1)} %all_to_all.10.parts_ref), custom_call_target="tpu_custom_call" | custom-call | bytes 1048576 | tf_op jit(solution)/shard_map/pallas_call | solution.py:271
  (4 shorter events, 0.0 us)
Async XLA Ops:
  0.0 36.7 %copy-start.5 = (s32[6]{0:T(128)S(1)}, s32[6]{0:T(128)}, u32[]{:S(2)}) copy-start(s32[6]{0:T(128)} %count_ref.5) | copy-start | bytes 76
  0.1 0.9 %copy-start = (bf16[64,768]{1,0:T(8,128)(2,1)S(1)}, bf16[64,768]{1,0:T(8,128)(2,1)}, u32[]{:S(2)}) copy-start(bf16[64,768]{1,0:T(8,128)(2,1)} %rows_ref.1) | copy-start | bytes 294916
  1.0 0.7 copy-start.1
  3.4 28.0 %all-to-all-start = ((bf16[32,8,768]{2,1,0:T(8,128)(2,1)}), bf16[32,8,768]{2,1,0:T(8,128)(2,1)S(1)}, u32[]{:S(2)}, u32[]{:S(2)}) async-start(bf16[32,8,768]{2,1,0:T(8,128)(2,1)} %bitcast.3), calls=%async_computation | async-start | bytes 786432 | tf_op jit(solution)/shard_map/all_to_all | solution.py:247
  20.1 0.7 copy-start.2
  20.8 15.8 %copy-start.3 = (bf16[3,3,3,96,384]{4,3,2,1,0:T(8,128)(2,1)S(1)}, bf16[3,3,3,96,384]{4,3,2,1,0:T(8,128)(2,1)}, u32[]{:S(2)}) copy-start(bf16[3,3,3,96,384]{4,3,2,1,0:T(8,128)(2,1)} %param.16) | copy-start | bytes 5971972
  34.1 8.8 %collective-permute-start = (bf16[64,768]{1,0:T(8,128)(2,1)S(1)}, bf16[64,768]{1,0:T(8,128)(2,1)S(1)}, u32[]{:S(2)}, u32[]{:S(2)}) collective-permute-start(bf16[64,768]{1,0:T(8,128)(2,1)S(1)} %get-tuple-element.9), channel_id=1, source_target_pairs={{0,4},{4,8},{8,12},{12,16},{16,20},{20,24},{24,28},{28,32},{32,36}... | collective-permute-start | bytes 294920 | tf_op jit(solution)/shard_map/ppermute | solution.py:259
  43.0 15.8 %copy-start.4 = (bf16[3,3,3,96,384]{4,3,2,1,0:T(8,128)(2,1)S(1)}, bf16[3,3,3,96,384]{4,3,2,1,0:T(8,128)(2,1)}, u32[]{:S(2)}) copy-start(bf16[3,3,3,96,384]{4,3,2,1,0:T(8,128)(2,1)} %param.20) | copy-start | bytes 5971972

commit v2 on v1

v2 whole, which is shorter than its diff:
```python
import jax
import jax.numpy as jnp
from jax import lax
from jax.experimental import pallas as pl
from jax.experimental.pallas import tpu as pltpu
from jax.sharding import PartitionSpec as P

CH = 384
WIDE = 768
GROUP = 12
ROWS = 16
OWN = 96
PAIR = 192
F_DEV = 16
BLOCK = 256
SLOTS = 64
CAP = 8
VIDEOS = 6
F32, BF16, I32 = jnp.float32, jnp.bfloat16, jnp.int32
VMEM_LIMIT = 24 * 2**20


def dot(a, b):
    return jnp.dot(a, b, preferred_element_type=F32)


def dot_nt(a, b):
    return lax.dot_general(a, b, (((1,), (1,)), ((), ())), preferred_element_type=F32)


def iota(shape, axis):
    return lax.broadcasted_iota(I32, shape, axis)


def twelfth(v):
    return (v * 43691) >> 19


def three(v):
    high = v.astype(BF16)
    rest = v - high.astype(F32)
    middle = rest.astype(BF16)
    low = (rest - middle.astype(F32)).astype(BF16)
    return high, middle, low


def place():
    return lax.axis_index("ta"), lax.axis_index("ha")


def pack_kernel(plan_hbm, rows_hbm, out_ref, plan_ref, rows_ref, plan_sem, rows_sem):
    plan_copy = pltpu.make_async_copy(plan_hbm, plan_ref, plan_sem)
    rows_copy = pltpu.make_async_copy(rows_hbm, rows_ref, rows_sem)
    plan_copy.start()
    rows_copy.start()
    ta, ha = place()
    own = ta * 4 + ha
    lower = (iota((128, 128), 0) < iota((128, 128), 1)).astype(BF16)
    spot = iota((256, 128), 0)
    spot = (spot >> 4) * CAP + (spot & 7)
    plan_copy.wait()
    ids = plan_ref[pl.ds(own // 2, 1), :]
    ids = jnp.where(own % 2 == 1, pltpu.roll(ids, 64, 1), ids)
    block = ids >> 8
    hit = iota((16, 128), 0) == block
    before = dot(hit.astype(BF16), lower)
    rank = jnp.sum(jnp.where(hit, before, 0.0), axis=0, keepdims=True)
    hot = (spot == block * CAP + rank.astype(I32)).astype(BF16)
    rows_copy.wait()
    out_ref[...] = dot(hot[:, :SLOTS], rows_ref[...]).astype(BF16)


def same_group(lanes, wrap):
    first, second = iota((lanes, lanes), 0), iota((lanes, lanes), 1)
    if wrap < lanes:
        first = jnp.where(first >= wrap, first - wrap, first)
        second = jnp.where(second >= wrap, second - wrap, second)
    return (twelfth(first) == twelfth(second)).astype(BF16)


def side_by_side(weight_ref, out_ref):
    for tap in range(9):
        for c in range(2):
            part = weight_ref[tap, c * OWN : c * OWN + PAIR, :].astype(F32)
            at = tap * WIDE + c * CH
            out_ref[at : at + CH, :] = part.T.astype(BF16)


def prepare_kernel(
    plan_ref, gain_ref, bias_ref, b1_ref, g2_ref, n2_ref, b2_ref, w1_ref, w2_ref,
    table_ref, wide_ref, own_ref, same_wide_ref, same_own_ref, select_ref, first_ref, second_ref,
):
    ta, ha = place()
    wide_ref[0:1] = gain_ref[...].reshape(1, CH)
    wide_ref[1:2] = bias_ref[...].reshape(1, CH)
    for k, ref in enumerate((b1_ref, g2_ref, n2_ref, b2_ref)):
        value = ref[...].reshape(1, CH)
        part = jnp.zeros((1, OWN), F32)
        for h in range(4):
            part = jnp.where(ha == h, value[:, h * OWN : (h + 1) * OWN], part)
        own_ref[k : k + 1] = jnp.concatenate([part, part], axis=1)
    same_wide_ref[...] = same_group(CH, CH)
    same_own_ref[...] = same_group(PAIR, OWN)
    lane = iota((WIDE, PAIR), 1)
    source = ha * OWN + jnp.where(lane < OWN, CH + lane, lane - OWN)
    select_ref[...] = (iota((WIDE, PAIR), 0) == source).astype(BF16)
    side_by_side(w1_ref, first_ref)
    side_by_side(w2_ref, second_ref)
    plan = plan_ref[...]
    match = (plan >> 8) == ta
    i, j = iota((128, 128), 0), iota((128, 128), 1)
    before = dot(match.astype(BF16), ((i < j) & ((i >> 6) == (j >> 6))).astype(BF16))
    value = jnp.where(match, (plan & 255) + 1, 0).astype(F32)
    ranked = jnp.concatenate([jnp.where(before == k, value, 0.0) for k in range(CAP)], axis=0)
    half = ((iota((8, 128), 1) >> 6) == iota((8, 128), 0)).astype(BF16)
    held = dot_nt(half, ranked.astype(BF16))
    q, p = iota((256, 256), 0), iota((256, 256), 1)
    held = dot(held.astype(BF16), (q == (p & 7) * 32 + (p >> 3)).astype(BF16))
    want = (q + 1).astype(F32)
    table_ref[:, 0:256] = (held[0:1] == want).astype(BF16)
    table_ref[:, 256:512] = (held[1:2] == want).astype(BF16)


def unpack_kernel(table_ref, packed_ref, out_ref, tail_ref):
    rows = dot(table_ref[...], packed_ref[...]).astype(BF16)
    out_ref[...] = rows
    tail_ref[...] = rows[BLOCK - 64 :]


def frame_stats(values, same):
    rows, lanes = values.shape
    pick = ((iota((16, rows), 1) >> 4) == iota((16, rows), 0)).astype(BF16)
    wide = values.astype(F32)
    square = wide * wide
    high = square.astype(BF16)
    low = (square - high.astype(F32)).astype(BF16)
    both = jnp.concatenate([dot(pick, values), dot(pick, high) + dot(pick, low)], axis=0)
    if lanes == WIDE:
        both = both[:, :CH] + both[:, CH:]
    total = dot(jnp.concatenate(three(both), axis=0), same)
    total = total[0:32] + total[32:64] + total[64:96]
    entries = ROWS * 2 * GROUP
    mean = total[0:16] / entries
    var = total[16:32] / entries - mean * mean
    return mean, lax.rsqrt(var + 1e-06)


def silu(v):
    return v / (1.0 + jnp.exp(-v))


def store_taps(taps_ref, at, act):
    row = iota((ROWS, WIDE), 0)
    taps_ref[0, at : at + ROWS, :] = jnp.where(row == 0, 0.0, pltpu.roll(act, 1, 0)).astype(BF16)
    taps_ref[1, at : at + ROWS, :] = act.astype(BF16)
    taps_ref[2, at : at + ROWS, :] = jnp.where(row == ROWS - 1, 0.0, pltpu.roll(act, ROWS - 1, 0)).astype(BF16)


def norm_first(rows_ref, wide_ref, same, taps_ref):
    gain, bias = wide_ref[0:1], wide_ref[1:2]
    mean, inverse = frame_stats(rows_ref[...], same)
    for f in range(rows_ref.shape[0] // ROWS):
        value = rows_ref[f * ROWS : (f + 1) * ROWS, :].astype(F32)
        m, s = mean[f : f + 1], inverse[f : f + 1]
        halves = [
            silu((value[:, c * CH : (c + 1) * CH] - m) * s * gain + bias) for c in range(2)
        ]
        store_taps(taps_ref, f * ROWS, jnp.concatenate(halves, axis=1))


def convolve(taps_ref, weight_ref, rows, first_frame, count_ref):
    totals = []
    for a in range(3):
        acc = None
        for b in range(3):
            part = dot(
                taps_ref[b, a * ROWS : a * ROWS + rows, :],
                weight_ref[(3 * a + b) * WIDE : (3 * a + b + 1) * WIDE, :],
            )
            acc = part if acc is None else acc + part
        totals.append(acc)
    frame = first_frame + (iota((rows, 1), 0) >> 4)
    start = jnp.zeros((rows, 1), I32)
    end = jnp.int32(0)
    for v in range(VIDEOS):
        count = count_ref[v]
        end = end + count
        start = start + jnp.where(frame >= end, count, 0)
    total = totals[2]
    for a in range(2):
        total = total + totals[a] * jnp.where(frame - 2 + a >= start, 1.0, 0.0)
    return total


def fold(values):
    half = values.shape[0] // 2
    rest = values[:, 128:]
    return jnp.concatenate([values[:, :128], jnp.concatenate([rest[:half], rest[half:]], axis=1)], axis=0)


def norm_second(hidden, own_ref, same):
    gain, bias = own_ref[1:2], own_ref[2:3]
    mean, inverse = frame_stats(hidden, same)
    acts = []
    for f in range(hidden.shape[0] // ROWS):
        value = hidden[f * ROWS : (f + 1) * ROWS].astype(F32)
        acts.append(silu((value - mean[f : f + 1]) * inverse[f : f + 1] * gain + bias))
    return fold(jnp.concatenate(acts, axis=0)).astype(BF16)


EDGE = 64
INNER = BLOCK - 2 * ROWS
FOLDED = (EDGE + INNER) * 3 // 2
CUT = EDGE * 3 // 2


def main_kernel(
    count_ref, rows_ref, wide_ref, own_ref, same_wide_ref, same_own_ref, select_ref, weight_ref,
    act_ref, rest_ref, head_ref, taps_ref,
):
    ta, _ = place()
    norm_first(rows_ref, wide_ref, same_wide_ref[...], taps_ref)
    hidden = convolve(taps_ref, weight_ref, INNER, ta * F_DEV + 2, count_ref) + own_ref[0:1]
    act_ref[...] = norm_second(hidden.astype(BF16), own_ref, same_own_ref[...])
    rest_ref[...] = dot(rows_ref[...], select_ref[...]).astype(BF16)
    for b in range(3):
        head_ref[b] = taps_ref[b, 0:32, :]


def halo_kernel(
    count_ref, earlier_ref, head_ref, wide_ref, own_ref, same_wide_ref, same_own_ref, weight_ref, main_ref,
    act_ref, taps_ref,
):
    ta, _ = place()
    norm_first(earlier_ref, wide_ref, same_wide_ref[...], taps_ref)
    for b in range(3):
        taps_ref[b, EDGE : EDGE + 32, :] = head_ref[b]
    hidden = convolve(taps_ref, weight_ref, EDGE, ta * F_DEV - 2, count_ref) + own_ref[0:1]
    act_ref[0:CUT, :] = norm_second(hidden.astype(BF16), own_ref, same_own_ref[...])
    act_ref[CUT:FOLDED, :] = main_ref[...]


def unfolded(ref, h, base, frames, f):
    half = frames // 2
    low = base + frames * ROWS + (f % half) * ROWS
    lane = 64 * (f // half)
    return jnp.concatenate(
        [
            ref[h, base + f * ROWS : base + (f + 1) * ROWS, :].astype(F32),
            ref[h, low : low + ROWS, :].astype(F32)[:, lane : lane + 64],
        ],
        axis=1,
    )


def last_kernel(count_ref, act_ref, rest_ref, own_ref, weight_ref, out_ref, taps_ref):
    ta, _ = place()
    for f in range(F_DEV + 2):
        parts = [
            unfolded(act_ref, h, 0, 4, f) if f < 4 else unfolded(act_ref, h, CUT, 14, f - 4) for h in range(4)
        ]
        whole = jnp.concatenate([p[:, OWN:] for p in parts] + [p[:, :OWN] for p in parts], axis=1)
        store_taps(taps_ref, f * ROWS, whole)
    total = convolve(taps_ref, weight_ref, BLOCK, ta * F_DEV, count_ref)
    total = (total + own_ref[3:4] + rest_ref[...].astype(F32)).astype(BF16)
    to, at = iota((BLOCK, BLOCK), 0), iota((BLOCK, BLOCK), 1)
    order = (((to >> 2) & 15) * ROWS + (to >> 6) * 4 + (to & 3) == at).astype(BF16)
    ordered = dot(order, total)
    for h in range(4):
        out_ref[h] = fold(ordered[h * 64 : (h + 1) * 64]).astype(BF16)


def join_kernel(parts_ref, out_ref):
    parts = []
    for h in range(4):
        part = parts_ref[h].astype(F32)
        rest = jnp.concatenate([part[64:96, 0:64], part[64:96, 64:128]], axis=0)
        parts.append(jnp.concatenate([part[0:64], rest], axis=1))
    zero = jnp.concatenate([p[:, OWN:] for p in parts], axis=1)
    one = jnp.concatenate([p[:, :OWN] for p in parts], axis=1)
    out_ref[...] = jnp.stack([zero, one], axis=1).astype(BF16).reshape(F_DEV, 4, 2, CH)


def call(kernel, outs, ins, scratch=(), flops=0):
    return pl.pallas_call(
        kernel,
        out_shape=[jax.ShapeDtypeStruct(s, t) for s, t in outs],
        in_specs=[pl.BlockSpec(memory_space=m) for m in ins],
        out_specs=[pl.BlockSpec(memory_space=pltpu.VMEM)] * len(outs),
        scratch_shapes=list(scratch),
        compiler_params=pltpu.CompilerParams(vmem_limit_bytes=VMEM_LIMIT),
        cost_estimate=pl.CostEstimate(flops=flops, bytes_accessed=2**20, transcendentals=0),
    )


def local(
    decoder_feature_rows,
    slot_row_index,
    latent_frame_count,
    first_norm_gain,
    first_norm_bias,
    first_convolution_weight,
    first_convolution_bias,
    second_norm_gain,
    second_norm_bias,
    second_convolution_weight,
    second_convolution_bias,
):
    plan = slot_row_index.reshape(32, 128)
    n_ta = lax.axis_size("ta")
    same_core = [[t * 4 + z * 2 + c for t in range(n_ta) for z in range(2)] for c in range(2)]
    chips = [[0, 1], [2, 3]]
    vmem, smem, hbm = pltpu.VMEM, pltpu.SMEM, pltpu.HBM

    [packed] = call(
        pack_kernel,
        [((256, WIDE), BF16)],
        [hbm] * 2,
        [pltpu.VMEM((32, 128), I32), pltpu.VMEM((SLOTS, WIDE), BF16)] + [pltpu.SemaphoreType.DMA] * 2,
        flops=10**7,
    )(plan, decoder_feature_rows)
    arrived = lax.all_to_all(
        packed.reshape(32, CAP, WIDE), ("ta", "ha"), 0, 0, axis_index_groups=same_core, tiled=True
    ).reshape(256, WIDE)
    weight = (9 * WIDE, PAIR)
    table, wide, own, same_wide, same_own, select, first, second = call(
        prepare_kernel,
        [
            ((BLOCK, 512), BF16),
            ((2, CH), F32),
            ((4, PAIR), F32),
            ((CH, CH), BF16),
            ((PAIR, PAIR), BF16),
            ((WIDE, PAIR), BF16),
            (weight, BF16),
            (weight, BF16),
        ],
        [vmem] * 9,
        flops=2 * 10**9,
    )(
        plan,
        first_norm_gain,
        first_norm_bias,
        first_convolution_bias,
        second_norm_gain,
        second_norm_bias,
        second_convolution_bias,
        first_convolution_weight.reshape(9, 3 * OWN, CH),
        second_convolution_weight.reshape(9, 3 * OWN, CH),
    )
    both = lax.all_gather(arrived, "ha", axis=0, axis_index_groups=chips, tiled=True)
    rows, tail = call(unpack_kernel, [((BLOCK, WIDE), BF16), ((64, WIDE), BF16)], [vmem] * 2, flops=10**8)(table, both)
    earlier = lax.ppermute(tail, "ta", [(i, i + 1) for i in range(n_ta - 1)])
    act, rest, head = call(
        main_kernel,
        [((FOLDED - CUT, 128), BF16), ((BLOCK, PAIR), BF16), ((3, 32, WIDE), BF16)],
        [smem] + [vmem] * 7,
        [pltpu.VMEM((3, BLOCK, WIDE), BF16)],
        flops=2 * 10**9,
    )(latent_frame_count, rows, wide, own, same_wide, same_own, select, first)
    [act] = call(
        halo_kernel, [((FOLDED, 128), BF16)], [smem] + [vmem] * 8, [pltpu.VMEM((3, EDGE + 32, WIDE), BF16)], flops=10**9
    )(latent_frame_count, earlier, head, wide, own, same_wide, same_own, first, act)
    acts = lax.all_gather(act, "ha", axis=0, tiled=False)
    [out] = call(
        last_kernel,
        [((4, 96, 128), BF16)],
        [smem] + [vmem] * 4,
        [pltpu.VMEM((3, EDGE + INNER, WIDE), BF16)],
        flops=2 * 10**9,
    )(latent_frame_count, acts, rest, own, second)
    parts = lax.all_to_all(out, "ha", 0, 0, tiled=True)
    [joined] = call(join_kernel, [((F_DEV, 4, 2, CH), BF16)], [vmem])(parts)
    return joined


def solution(mesh):
    in_specs = (
        P(("dp", "ta", "ha"), None),
        P("dp"),
        P("dp"),
        P(),
        P(),
        P(None, None, None, "ha", None),
        P(),
        P(),
        P(),
        P(None, None, None, "ha", None),
        P(),
    )
    out_specs = P(("dp", "ta"), "ha", None, None)
    return jax.shard_map(local, mesh=mesh, in_specs=in_specs, out_specs=out_specs, check_vma=False)
```

time: 74.3 us -> 76.7 us (1.032)
  the two profiles are of different devices: /device:TPU:96 before, /device:TPU:40 now
where the time goes in v2:
time: 76.7 us; the launch traced here: 75.9 us
  blocking collectives  29 us (38%)
  local copies, waits for them, and re-layouts  17.9 us (23%)
  starting transfers between devices  16.9 us (22%)
  Pallas kernels  12.1 us (16%)
    unnamed x44, local copies, waits for them, and re-layouts  17.9 us
    all_to_all x1, blocking collectives, local(): parts = lax.all_to_all(out, 'ha', 0, 0, tiled=True)  15.7 us
    all_to_all x1, starting transfers between devices, local(): lax.all_to_all(packed.reshape(32, CAP, WIDE), ('ta', 'ha'), 0, 0, axis_in...  13.3 us
    all_gather x1, blocking collectives, local(): acts = lax.all_gather(act, 'ha', axis=0, tiled=False)  10.7 us
    ppermute x1, starting transfers between devices, local(): earlier = lax.ppermute(tail, 'ta', [(i, i + 1) for i in range(n_ta - 1)])  3.63 us
    pallas_call x1, Pallas kernels, local(): call(main_kernel, [((FOLDED - CUT, 128), BF16), ((BLOCK, PAIR), BF16), ((...  2.88 us
    all_gather x1, blocking collectives, local(): lax.all_gather(arrived, 'ha', axis=0, axis_index_groups=chips, tiled=True)  2.57 us
    pallas_call x1, Pallas kernels, local(): call(prepare_kernel, [((BLOCK, 512), BF16), ((2, CH), F32), ((4, PAIR), F...  2.36 us
  transfers between devices with their start and end apart: 2, of which 0 were waited for; matrix products, arithmetic and copies ran while one was open for 0% of the time, Pallas kernels for 7%

profile of v2, /device:TPU:40, one launch (start us, length us, event | category | flops | bytes accessed | tf_op | source)
XLA Modules:
  0.0 75.9 jit_solution(11248343913719642708)
XLA Ops:
  0.0 0.9 %copy-done.4 = bf16[64,768]{1,0:T(8,128)(2,1)S(1)} copy-done((bf16[64,768]{1,0:T(8,128)(2,1)S(1)}, bf16[64,768]{1,0:T(8,128)(2,1)}, u32[]{:S(2)}) %copy-start.4) | copy-done | bytes 98328
  0.9 0.7 copy-done.7
  1.6 1.4 %shard_map.110 = bf16[256,768]{1,0:T(8,128)(2,1)} custom-call(s32[32,128]{1,0:T(8,128)S(1)} %bitcast.7, bf16[64,768]{1,0:T(8,128)(2,1)S(1)} %copy-done.4), custom_call_target="tpu_custom_call" | custom-call | flops 10000000 | bytes 1048576 | tf_op jit(solution)/shard_map/pallas_call | solution.py:315
  3.0 13.3 %all-to-all-start = ((bf16[32,8,768]{2,1,0:T(8,128)(2,1)}), bf16[32,8,768]{2,1,0:T(8,128)(2,1)}, u32[]{:S(2)}, u32[]{:S(2)}) async-start(bf16[32,8,768]{2,1,0:T(8,128)(2,1)} %bitcast.3), calls=%async_computation | async-start | bytes 786432 | tf_op jit(solution)/shard_map/all_to_all | solution.py:322
  16.3 0.7 copy-done.8
  17.0 1.6 %copy-done.10 = bf16[3,3,3,96,384]{4,3,2,1,0:T(8,128)(2,1)S(1)} copy-done((bf16[3,3,3,96,384]{4,3,2,1,0:T(8,128)(2,1)S(1)}, bf16[3,3,3,96,384]{4,3,2,1,0:T(8,128)(2,1)}, u32[]{:S(2)}) %copy-start.10) | copy-done | bytes 1990680
  18.6 1.6 %copy-done.11 = bf16[3,3,3,96,384]{4,3,2,1,0:T(8,128)(2,1)S(1)} copy-done((bf16[3,3,3,96,384]{4,3,2,1,0:T(8,128)(2,1)S(1)}, bf16[3,3,3,96,384]{4,3,2,1,0:T(8,128)(2,1)}, u32[]{:S(2)}) %copy-start.11) | copy-done | bytes 1990680
  20.1 0.7 copy-done.12
  20.8 0.7 copy-done.13
  21.5 0.7 copy-done.14
  22.2 0.7 copy-done.15
  22.9 0.7 copy-done.16
  23.6 0.7 copy-done.17
  24.2 2.4 %shard_map.109 = (bf16[256,512]{1,0:T(8,128)(2,1)S(1)}, f32[2,384]{1,0:T(2,128)S(1)}, f32[4,192]{1,0:T(4,128)S(1)}, bf16[384,384]{1,0:T(8,128)(2,1)S(1)}, bf16[1...) custom-call(s32[32,128]{1,0:T(8,128)S(1)} %bitcast.8, ...), custom_call_target="tpu_custom_call" | custom-call | flops 2000000000 | bytes 1048576 | tf_op jit(solution)/shard_map/pallas_call | solution.py:326
  26.6 0.7 copy-done
  27.3 0.7 copy-done.2
  28.0 0.6 copy-done.5
  28.7 1.7 %copy-done.18 = bf16[6912,192]{1,0:T(8,128)(2,1)} copy-done((bf16[6912,192]{1,0:T(8,128)(2,1)}, bf16[6912,192]{1,0:T(8,128)(2,1)S(1)}, u32[]{:S(2)}) %copy-start.18) | copy-done | bytes 2654232
  30.4 0.8 %copy-done.20 = bf16[768,192]{1,0:T(8,128)(2,1)} copy-done((bf16[768,192]{1,0:T(8,128)(2,1)}, bf16[768,192]{1,0:T(8,128)(2,1)S(1)}, u32[]{:S(2)}) %copy-start.20) | copy-done | bytes 294936
  31.2 2.6 %all_gather.9.packed_ref = bf16[512,768]{1,0:T(8,128)(2,1)S(1)} all-gather(bf16[256,768]{1,0:T(8,128)(2,1)} %bitcast.4), channel_id=1, replica_groups={{0,1},{2,3},{4,5},{6,7},{8,9},{10,11},{12,13},{14,15},{16,17},{18,19},{..., dimensions={0}, use_global_device_ids=true | all-gather | bytes 1179648 | tf_op jit(solution)/shard_map/all_gather | solution.py:351
  33.8 0.9 %copy-done.3 = bf16[256,512]{1,0:T(8,128)(2,1)S(1)} copy-done((bf16[256,512]{1,0:T(8,128)(2,1)S(1)}, bf16[256,512]{1,0:T(8,128)(2,1)}, u32[]{:S(2)}) %copy-start.3) | copy-done | bytes 262168
  34.7 0.4 shard_map.111
  35.1 3.6 %collective-permute-start = (bf16[64,768]{1,0:T(8,128)(2,1)S(1)}, bf16[64,768]{1,0:T(8,128)(2,1)S(1)}, u32[]{:S(2)}, u32[]{:S(2)}) collective-permute-start(bf16[64,768]{1,0:T(8,128)(2,1)S(1)} %get-tuple-element.19), channel_id=1, source_target_pairs={{0,4},{4,8},{8,12},{12,16},{16,20},{20,24},{24,28},{28,32},{32,36}... | collective-permute-start | bytes 294920 | tf_op jit(solution)/shard_map/ppermute | solution.py:353
  38.7 1.0 %copy-done.1 = bf16[384,384]{1,0:T(8,128)(2,1)S(1)} copy-done((bf16[384,384]{1,0:T(8,128)(2,1)S(1)}, bf16[384,384]{1,0:T(8,128)(2,1)}, u32[]{:S(2)}) %copy-start.1) | copy-done | bytes 294936
  39.7 0.9 %copy-done.6 = bf16[192,192]{1,0:T(8,128)(2,1)S(1)} copy-done((bf16[192,192]{1,0:T(8,128)(2,1)S(1)}, bf16[192,192]{1,0:T(8,128)(2,1)}, u32[]{:S(2)}) %copy-start.6) | copy-done | bytes 73752
  40.6 1.0 %copy-done.21 = bf16[768,192]{1,0:T(8,128)(2,1)S(1)} copy-done((bf16[768,192]{1,0:T(8,128)(2,1)S(1)}, bf16[768,192]{1,0:T(8,128)(2,1)}, u32[]{:S(2)}) %copy-start.21) | copy-done | bytes 294936
  41.6 2.9 %shard_map.112 = (bf16[336,128]{1,0:T(8,128)(2,1)S(1)}, bf16[256,192]{1,0:T(8,128)(2,1)S(1)}, bf16[3,32,768]{2,1,0:T(8,128)(2,1)S(1)}) custom-call(s32[6]{0:T(128)S(1)} %copy-done.9, bf16[256,768]{1,0:T(8,128)(2,1)S(1)} %get-tuple-element.20.rows_ref, f32[2,384]{1,0:T(2,128)S(1)} %get-tuple-element.21.wide_ref, f32[4,192]{1,0:T(4,128)S(1)} %get-tuple-element.22.own_ref, ...), custom_call_target="tpu_custom_call" | custom-call | flops 2000000000 | bytes 1048576 | tf_op jit(solution)/shard_map/pallas_call | solution.py:354
  44.5 2.0 %shard_map.113 = bf16[432,128]{1,0:T(8,128)(2,1)S(1)} custom-call(s32[6]{0:T(128)S(1)} %copy-done.9, bf16[64,768]{1,0:T(8,128)(2,1)S(1)} %collective-permute-done.earlier_ref, bf16[3,32,768]{2,1,0:T(8,128)(2,1)S(1)} %get-tuple-element.27.head_ref, f32[2,384]{1,0:T(2,128)S(1)} %get-tuple-element.21.wide_ref, f32[4,192]{1,0:T(4,128)S(1)} %get-tuple-element.22.own_ref, ...), custom_call_target="tpu_custom_call" | custom-call | flops 1000000000 | bytes 1048576 | tf_op jit(solution)/shard_map/pallas_call | solution.py:361
  46.5 10.7 %all-gather = bf16[1728,128]{1,0:T(8,128)(2,1)S(1)} all-gather(bf16[432,128]{1,0:T(8,128)(2,1)S(1)} %shard_map.113), channel_id=2, replica_groups=mesh['dp'=8,'ta'=16,'ha'=4] {'ha'}, dimensions={0}, use_global_device_ids=true | all-gather | bytes 552960 | tf_op jit(solution)/shard_map/all_gather | solution.py:364
  57.2 2.1 %shard_map.114 = bf16[4,96,128]{2,1,0:T(8,128)(2,1)S(1)} custom-call(s32[6]{0:T(128)S(1)} %copy-done.9, bf16[4,432,128]{2,1,0:T(8,128)(2,1)S(1)} %bitcast.6, bf16[256,192]{1,0:T(8,128)(2,1)S(1)} %get-tuple-element.29.rest_ref, f32[4,192]{1,0:T(4,128)S(1)} %get-tuple-element.22.own_ref, bf16[6912,192]{1,0:T(8,128)(2,1)S(1)} %copy-done.19), custom_call_target="tpu_custom_call" | custom-call | flops 2000000000 | bytes 1048576 | tf_op jit(solution)/shard_map/pallas_call | solution.py:365
  59.3 15.7 %all_to_all.10.parts_ref = bf16[4,96,128]{2,1,0:T(8,128)(2,1)S(1)} all-to-all(bf16[4,96,128]{2,1,0:T(8,128)(2,1)S(1)} %shard_map.114), channel_id=1, replica_groups=mesh['dp'=8,'ta'=16,'ha'=4] {'ha'}, dimensions={0} | all-to-all | bytes 196608 | tf_op jit(solution)/shard_map/all_to_all | solution.py:372
  75.0 0.9 %shard_map.115 = bf16[16,4,2,384]{3,2,1,0:T(2,128)(2,1)} custom-call(bf16[4,96,128]{2,1,0:T(8,128)(2,1)S(1)} %all_to_all.10.parts_ref), custom_call_target="tpu_custom_call" | custom-call | bytes 1048576 | tf_op jit(solution)/shard_map/pallas_call | solution.py:373
  (26 shorter events, 0.0 us)
Async XLA Ops:
  0.0 0.9 %copy-start.4 = (bf16[64,768]{1,0:T(8,128)(2,1)S(1)}, bf16[64,768]{1,0:T(8,128)(2,1)}, u32[]{:S(2)}) copy-start(bf16[64,768]{1,0:T(8,128)(2,1)} %rows_hbm.1) | copy-start | bytes 294916
  0.9 0.7 copy-start.7
  3.0 28.2 %all-to-all-start = ((bf16[32,8,768]{2,1,0:T(8,128)(2,1)}), bf16[32,8,768]{2,1,0:T(8,128)(2,1)}, u32[]{:S(2)}, u32[]{:S(2)}) async-start(bf16[32,8,768]{2,1,0:T(8,128)(2,1)} %bitcast.3), calls=%async_computation | async-start | bytes 786432 | tf_op jit(solution)/shard_map/all_to_all | solution.py:322
  16.3 0.7 copy-start.8
  17.0 1.6 %copy-start.10 = (bf16[3,3,3,96,384]{4,3,2,1,0:T(8,128)(2,1)S(1)}, bf16[3,3,3,96,384]{4,3,2,1,0:T(8,128)(2,1)}, u32[]{:S(2)}) copy-start(bf16[3,3,3,96,384]{4,3,2,1,0:T(8,128)(2,1)} %param.16) | copy-start | bytes 5971972
  18.6 1.6 %copy-start.11 = (bf16[3,3,3,96,384]{4,3,2,1,0:T(8,128)(2,1)S(1)}, bf16[3,3,3,96,384]{4,3,2,1,0:T(8,128)(2,1)}, u32[]{:S(2)}) copy-start(bf16[3,3,3,96,384]{4,3,2,1,0:T(8,128)(2,1)} %param.20) | copy-start | bytes 5971972
  20.1 0.7 copy-start.12
  20.8 0.7 copy-start.13
  21.5 0.7 copy-start.14
  22.2 0.7 copy-start.15
  22.9 0.7 copy-start.16
  23.6 0.7 copy-start.17
  24.2 14.5 %copy-start.9 = (s32[6]{0:T(128)S(1)}, s32[6]{0:T(128)}, u32[]{:S(2)}) copy-start(s32[6]{0:T(128)} %count_ref.5) | copy-start | bytes 76
  26.6 0.7 copy-start
  27.3 0.7 copy-start.2
  28.0 0.6 copy-start.5
  28.7 1.7 %copy-start.18 = (bf16[6912,192]{1,0:T(8,128)(2,1)}, bf16[6912,192]{1,0:T(8,128)(2,1)S(1)}, u32[]{:S(2)}) copy-start(bf16[6912,192]{1,0:T(8,128)(2,1)S(1)} %get-tuple-element.30.weight_ref) | copy-start | bytes 7962628
  30.4 0.8 %copy-start.20 = (bf16[768,192]{1,0:T(8,128)(2,1)}, bf16[768,192]{1,0:T(8,128)(2,1)S(1)}, u32[]{:S(2)}) copy-start(bf16[768,192]{1,0:T(8,128)(2,1)S(1)} %get-tuple-element.25.select_ref) | copy-start | bytes 884740
  33.7 1.0 %copy-start.3 = (bf16[256,512]{1,0:T(8,128)(2,1)S(1)}, bf16[256,512]{1,0:T(8,128)(2,1)}, u32[]{:S(2)}) copy-start(bf16[256,512]{1,0:T(8,128)(2,1)} %copy-done.2) | copy-start | bytes 786436
  35.1 9.4 %collective-permute-start = (bf16[64,768]{1,0:T(8,128)(2,1)S(1)}, bf16[64,768]{1,0:T(8,128)(2,1)S(1)}, u32[]{:S(2)}, u32[]{:S(2)}) collective-permute-start(bf16[64,768]{1,0:T(8,128)(2,1)S(1)} %get-tuple-element.19), channel_id=1, source_target_pairs={{0,4},{4,8},{8,12},{12,16},{16,20},{20,24},{24,28},{28,32},{32,36}... | collective-permute-start | bytes 294920 | tf_op jit(solution)/shard_map/ppermute | solution.py:353
  38.7 1.0 %copy-start.1 = (bf16[384,384]{1,0:T(8,128)(2,1)S(1)}, bf16[384,384]{1,0:T(8,128)(2,1)}, u32[]{:S(2)}) copy-start(bf16[384,384]{1,0:T(8,128)(2,1)} %copy-done) | copy-start | bytes 884740
  39.7 0.9 %copy-start.6 = (bf16[192,192]{1,0:T(8,128)(2,1)S(1)}, bf16[192,192]{1,0:T(8,128)(2,1)}, u32[]{:S(2)}) copy-start(bf16[192,192]{1,0:T(8,128)(2,1)} %copy-done.5) | copy-start | bytes 221188
  40.6 1.0 %copy-start.21 = (bf16[768,192]{1,0:T(8,128)(2,1)S(1)}, bf16[768,192]{1,0:T(8,128)(2,1)}, u32[]{:S(2)}) copy-start(bf16[768,192]{1,0:T(8,128)(2,1)} %copy-done.20) | copy-start | bytes 884740
  44.5 12.8 %copy-start.19 = (bf16[6912,192]{1,0:T(8,128)(2,1)S(1)}, bf16[6912,192]{1,0:T(8,128)(2,1)}, u32[]{:S(2)}) copy-start(bf16[6912,192]{1,0:T(8,128)(2,1)} %copy-done.18) | copy-start | bytes 7962628

commit v3 on v2

--- a/solution.py
+++ b/solution.py
@@ -86,26 +86,31 @@
             out_ref[at : at + CH, :] = part.T.astype(BF16)
 
 
+def side_by_side_dense(weight_ref, out_ref):
+    for tap in range(9):
+        for c in range(2):
+            out_ref[tap, :, c * CH : (c + 1) * CH] = weight_ref[tap, c * OWN : c * OWN + PAIR, :]
+
+
 def prepare_kernel(
-    plan_ref, gain_ref, bias_ref, b1_ref, g2_ref, n2_ref, b2_ref, w1_ref, w2_ref,
+    plan_hbm, gain_hbm, bias_hbm, b1_hbm, g2_hbm, n2_hbm, b2_hbm, w1_hbm, w2_hbm,
     table_ref, wide_ref, own_ref, same_wide_ref, same_own_ref, select_ref, first_ref, second_ref,
+    plan_ref, gain_ref, bias_ref, b1_ref, g2_ref, n2_ref, b2_ref, w1_ref, w2_ref, sems,
 ):
+    pairs = (
+        (plan_hbm, plan_ref), (w1_hbm, w1_ref), (w2_hbm, w2_ref), (gain_hbm, gain_ref), (bias_hbm, bias_ref),
+        (b1_hbm, b1_ref), (g2_hbm, g2_ref), (n2_hbm, n2_ref), (b2_hbm, b2_ref),
+    )
+    copies = [pltpu.make_async_copy(source, to, sems.at[k]) for k, (source, to) in enumerate(pairs)]
+    for copy in copies:
+        copy.start()
     ta, ha = place()
-    wide_ref[0:1] = gain_ref[...].reshape(1, CH)
-    wide_ref[1:2] = bias_ref[...].reshape(1, CH)
-    for k, ref in enumerate((b1_ref, g2_ref, n2_ref, b2_ref)):
-        value = ref[...].reshape(1, CH)
-        part = jnp.zeros((1, OWN), F32)
-        for h in range(4):
-            part = jnp.where(ha == h, value[:, h * OWN : (h + 1) * OWN], part)
-        own_ref[k : k + 1] = jnp.concatenate([part, part], axis=1)
     same_wide_ref[...] = same_group(CH, CH)
     same_own_ref[...] = same_group(PAIR, OWN)
     lane = iota((WIDE, PAIR), 1)
     source = ha * OWN + jnp.where(lane < OWN, CH + lane, lane - OWN)
     select_ref[...] = (iota((WIDE, PAIR), 0) == source).astype(BF16)
-    side_by_side(w1_ref, first_ref)
-    side_by_side(w2_ref, second_ref)
+    copies[0].wait()
     plan = plan_ref[...]
     match = (plan >> 8) == ta
     i, j = iota((128, 128), 0), iota((128, 128), 1)
@@ -119,6 +124,20 @@
     want = (q + 1).astype(F32)
     table_ref[:, 0:256] = (held[0:1] == want).astype(BF16)
     table_ref[:, 256:512] = (held[1:2] == want).astype(BF16)
+    for copy in copies[3:]:
+        copy.wait()
+    wide_ref[0:1] = gain_ref[...].reshape(1, CH)
+    wide_ref[1:2] = bias_ref[...].reshape(1, CH)
+    for k, ref in enumerate((b1_ref, g2_ref, n2_ref, b2_ref)):
+        value = ref[...].reshape(1, CH)
+        part = jnp.zeros((1, OWN), F32)
+        for h in range(4):
+            part = jnp.where(ha == h, value[:, h * OWN : (h + 1) * OWN], part)
+        own_ref[k : k + 1] = jnp.concatenate([part, part], axis=1)
+    copies[1].wait()
+    side_by_side(w1_ref, first_ref)
+    copies[2].wait()
+    side_by_side_dense(w2_ref, second_ref)
 
 
 def unpack_kernel(table_ref, packed_ref, out_ref, tail_ref):
@@ -168,15 +187,12 @@
         store_taps(taps_ref, f * ROWS, jnp.concatenate(halves, axis=1))
 
 
-def convolve(taps_ref, weight_ref, rows, first_frame, count_ref):
+def convolve(taps_ref, product, rows, first_frame, count_ref):
     totals = []
     for a in range(3):
         acc = None
         for b in range(3):
-            part = dot(
-                taps_ref[b, a * ROWS : a * ROWS + rows, :],
-                weight_ref[(3 * a + b) * WIDE : (3 * a + b + 1) * WIDE, :],
-            )
+            part = product(taps_ref[b, a * ROWS : a * ROWS + rows, :], 3 * a + b)
             acc = part if acc is None else acc + part
         totals.append(acc)
     frame = first_frame + (iota((rows, 1), 0) >> 4)
@@ -192,6 +208,14 @@
     return total
 
 
+def with_first(weight_ref):
+    return lambda values, tap: dot(values, weight_ref[tap * WIDE : (tap + 1) * WIDE, :])
+
+
+def with_second(weight_ref):
+    return lambda values, tap: dot_nt(values, weight_ref[tap])
+
+
 def fold(values):
     half = values.shape[0] // 2
     rest = values[:, 128:]
@@ -215,16 +239,19 @@
 
 
 def main_kernel(
-    count_ref, rows_ref, wide_ref, own_ref, same_wide_ref, same_own_ref, select_ref, weight_ref,
-    act_ref, rest_ref, head_ref, taps_ref,
+    count_ref, rows_ref, wide_ref, own_ref, same_wide_ref, same_own_ref, select_ref, weight_hbm,
+    act_ref, rest_ref, head_ref, weight_ref, taps_ref, sem,
 ):
+    copy = pltpu.make_async_copy(weight_hbm, weight_ref, sem)
+    copy.start()
     ta, _ = place()
     norm_first(rows_ref, wide_ref, same_wide_ref[...], taps_ref)
-    hidden = convolve(taps_ref, weight_ref, INNER, ta * F_DEV + 2, count_ref) + own_ref[0:1]
-    act_ref[...] = norm_second(hidden.astype(BF16), own_ref, same_own_ref[...])
     rest_ref[...] = dot(rows_ref[...], select_ref[...]).astype(BF16)
     for b in range(3):
         head_ref[b] = taps_ref[b, 0:32, :]
+    copy.wait()
+    hidden = convolve(taps_ref, with_first(weight_ref), INNER, ta * F_DEV + 2, count_ref) + own_ref[0:1]
+    act_ref[...] = norm_second(hidden.astype(BF16), own_ref, same_own_ref[...])
 
 
 def halo_kernel(
@@ -235,7 +262,7 @@
     norm_first(earlier_ref, wide_ref, same_wide_ref[...], taps_ref)
     for b in range(3):
         taps_ref[b, EDGE : EDGE + 32, :] = head_ref[b]
-    hidden = convolve(taps_ref, weight_ref, EDGE, ta * F_DEV - 2, count_ref) + own_ref[0:1]
+    hidden = convolve(taps_ref, with_first(weight_ref), EDGE, ta * F_DEV - 2, count_ref) + own_ref[0:1]
     act_ref[0:CUT, :] = norm_second(hidden.astype(BF16), own_ref, same_own_ref[...])
     act_ref[CUT:FOLDED, :] = main_ref[...]
 
@@ -261,7 +288,7 @@
         ]
         whole = jnp.concatenate([p[:, OWN:] for p in parts] + [p[:, :OWN] for p in parts], axis=1)
         store_taps(taps_ref, f * ROWS, whole)
-    total = convolve(taps_ref, weight_ref, BLOCK, ta * F_DEV, count_ref)
+    total = convolve(taps_ref, with_second(weight_ref), BLOCK, ta * F_DEV, count_ref)
     total = (total + own_ref[3:4] + rest_ref[...].astype(F32)).astype(BF16)
     to, at = iota((BLOCK, BLOCK), 0), iota((BLOCK, BLOCK), 1)
     order = (((to >> 2) & 15) * ROWS + (to >> 6) * 4 + (to & 3) == at).astype(BF16)
@@ -282,15 +309,22 @@
 
 
 def call(kernel, outs, ins, scratch=(), flops=0):
-    return pl.pallas_call(
+    run = pl.pallas_call(
         kernel,
-        out_shape=[jax.ShapeDtypeStruct(s, t) for s, t in outs],
+        out_shape=[jax.ShapeDtypeStruct(*o) if isinstance(o, tuple) else o for o in outs],
         in_specs=[pl.BlockSpec(memory_space=m) for m in ins],
         out_specs=[pl.BlockSpec(memory_space=pltpu.VMEM)] * len(outs),
         scratch_shapes=list(scratch),
         compiler_params=pltpu.CompilerParams(vmem_limit_bytes=VMEM_LIMIT),
         cost_estimate=pl.CostEstimate(flops=flops, bytes_accessed=2**20, transcendentals=0),
     )
+
+    def pinned(*args):
+        return run(
+            *(pltpu.with_memory_space_constraint(a, pltpu.HBM) if m is pltpu.HBM else a for a, m in zip(args, ins))
+        )
+
+    return pinned
 
 
 def local(
@@ -322,20 +356,21 @@
     arrived = lax.all_to_all(
         packed.reshape(32, CAP, WIDE), ("ta", "ha"), 0, 0, axis_index_groups=same_core, tiled=True
     ).reshape(256, WIDE)
-    weight = (9 * WIDE, PAIR)
+    weight, raw = (9 * WIDE, PAIR), (9, 3 * OWN, CH)
     table, wide, own, same_wide, same_own, select, first, second = call(
         prepare_kernel,
         [
-            ((BLOCK, 512), BF16),
-            ((2, CH), F32),
-            ((4, PAIR), F32),
-            ((CH, CH), BF16),
-            ((PAIR, PAIR), BF16),
-            ((WIDE, PAIR), BF16),
-            (weight, BF16),
-            (weight, BF16),
+            vmem((BLOCK, 512), BF16),
+            vmem((2, CH), F32),
+            vmem((4, PAIR), F32),
+            vmem((CH, CH), BF16),
+            vmem((PAIR, PAIR), BF16),
+            vmem((WIDE, PAIR), BF16),
+            hbm(weight, BF16),
+            hbm((9, PAIR, WIDE), BF16),
         ],
-        [vmem] * 9,
+        [hbm] * 9,
+        [vmem((32, 128), I32)] + [vmem((CH,), F32)] * 6 + [vmem(raw, BF16)] * 2 + [pltpu.SemaphoreType.DMA((9,))],
         flops=2 * 10**9,
     )(
         plan,
@@ -345,22 +380,27 @@
         second_norm_gain,
         second_norm_bias,
         second_convolution_bias,
-        first_convolution_weight.reshape(9, 3 * OWN, CH),
-        second_convolution_weight.reshape(9, 3 * OWN, CH),
+        first_convolution_weight.reshape(raw),
+        second_convolution_weight.reshape(raw),
     )
     both = lax.all_gather(arrived, "ha", axis=0, axis_index_groups=chips, tiled=True)
     rows, tail = call(unpack_kernel, [((BLOCK, WIDE), BF16), ((64, WIDE), BF16)], [vmem] * 2, flops=10**8)(table, both)
     earlier = lax.ppermute(tail, "ta", [(i, i + 1) for i in range(n_ta - 1)])
-    act, rest, head = call(
+    act, rest, head, near = call(
         main_kernel,
-        [((FOLDED - CUT, 128), BF16), ((BLOCK, PAIR), BF16), ((3, 32, WIDE), BF16)],
-        [smem] + [vmem] * 7,
-        [pltpu.VMEM((3, BLOCK, WIDE), BF16)],
+        [
+            vmem((FOLDED - CUT, 128), BF16),
+            vmem((BLOCK, PAIR), BF16),
+            vmem((3, 32, WIDE), BF16),
+            vmem(weight, BF16),
+        ],
+        [smem] + [vmem] * 6 + [hbm],
+        [vmem((3, BLOCK, WIDE), BF16), pltpu.SemaphoreType.DMA],
         flops=2 * 10**9,
     )(latent_frame_count, rows, wide, own, same_wide, same_own, select, first)
     [act] = call(
-        halo_kernel, [((FOLDED, 128), BF16)], [smem] + [vmem] * 8, [pltpu.VMEM((3, EDGE + 32, WIDE), BF16)], flops=10**9
-    )(latent_frame_count, earlier, head, wide, own, same_wide, same_own, first, act)
+        halo_kernel, [((FOLDED, 128), BF16)], [smem] + [vmem] * 8, [vmem((3, EDGE + 32, WIDE), BF16)], flops=10**9
+    )(latent_frame_count, earlier, head, wide, own, same_wide, same_own, near, act)
     acts = lax.all_gather(act, "ha", axis=0, tiled=False)
     [out] = call(
         last_kernel,

time: 76.7 us -> 70.1 us (0.914)
  the two profiles are of different devices: /device:TPU:40 before, /device:TPU:62 now
where the time goes in v3:
time: 70.1 us; the launch traced here: 69.7 us
  blocking collectives  25.9 us (37%)
  starting transfers between devices  17.9 us (26%)
  Pallas kernels  17.5 us (25%)
  waiting for transfers between devices  8.29 us (12%)
    pallas_call x7, Pallas kernels, pinned(): run(*(pltpu.with_memory_space_constraint(a, pltpu.HBM) if m is pltpu.HBM...  17.5 us
    all_to_all x1, starting transfers between devices, local(): lax.all_to_all(packed.reshape(32, CAP, WIDE), ('ta', 'ha'), 0, 0, axis_in...  13.4 us
    all_gather x1, blocking collectives, local(): acts = lax.all_gather(act, 'ha', axis=0, tiled=False)  12.4 us
    all_to_all x1, blocking collectives, local(): parts = lax.all_to_all(out, 'ha', 0, 0, tiled=True)  11.1 us
    all_to_all x1, waiting for transfers between devices, local(): lax.all_to_all(packed.reshape(32, CAP, WIDE), ('ta', 'ha'), 0, 0, axis_in...  8.28 us
    ppermute x1, starting transfers between devices, local(): earlier = lax.ppermute(tail, 'ta', [(i, i + 1) for i in range(n_ta - 1)])  4.49 us
    all_gather x1, blocking collectives, local(): lax.all_gather(arrived, 'ha', axis=0, axis_index_groups=chips, tiled=True)  2.36 us
  transfers between devices with their start and end apart: 2, of which 1 were waited for; matrix products, arithmetic and copies ran while one was open for 0% of the time, Pallas kernels for 15%

profile of v3, /device:TPU:62, one launch (start us, length us, event | category | flops | bytes accessed | tf_op | source)
XLA Modules:
  0.0 69.7 jit_solution(8645655617896211060)
XLA Ops:
  0.0 2.0 %shard_map.110 = bf16[256,768]{1,0:T(8,128)(2,1)} custom-call(s32[32,128]{1,0:T(8,128)} %bitcast.8, bf16[64,768]{1,0:T(8,128)(2,1)} %rows_hbm.1), custom_call_target="tpu_custom_call" | custom-call | flops 10000000 | bytes 1048576 | tf_op jit(solution)/shard_map/pallas_call | solution.py:323
  2.0 13.4 %all-to-all-start = ((bf16[32,8,768]{2,1,0:T(8,128)(2,1)}), bf16[32,8,768]{2,1,0:T(8,128)(2,1)S(1)}, u32[]{:S(2)}, u32[]{:S(2)}) async-start(bf16[32,8,768]{2,1,0:T(8,128)(2,1)} %bitcast.3), calls=%async_computation | async-start | bytes 786432 | tf_op jit(solution)/shard_map/all_to_all | solution.py:356
  15.4 0.0 copy-start
  15.4 6.0 %shard_map.109 = (bf16[256,512]{1,0:T(8,128)(2,1)S(1)}, f32[2,384]{1,0:T(2,128)S(1)}, f32[4,192]{1,0:T(4,128)S(1)}, bf16[384,384]{1,0:T(8,128)(2,1)S(1)}, bf16[1...) custom-call(s32[32,128]{1,0:T(8,128)} %bitcast.9, ...), custom_call_target="tpu_custom_call" | custom-call | flops 2000000000 | bytes 1048576 | tf_op jit(solution)/shard_map/pallas_call | solution.py:323
  21.4 8.3 %all-to-all-done = bf16[32,8,768]{2,1,0:T(8,128)(2,1)S(1)} async-done(((bf16[32,8,768]{2,1,0:T(8,128)(2,1)}), bf16[32,8,768]{2,1,0:T(8,128)(2,1)S(1)}, u32[]{:S(2)}, u32[]{:S(2)}) %all-to-all-start) | async-done | bytes 393248 | tf_op jit(solution)/shard_map/all_to_all | solution.py:356
  29.7 2.4 %all_gather.9.packed_ref = bf16[512,768]{1,0:T(8,128)(2,1)S(1)} all-gather(bf16[256,768]{1,0:T(8,128)(2,1)S(1)} %bitcast.7), channel_id=1, replica_groups={{0,1},{2,3},{4,5},{6,7},{8,9},{10,11},{12,13},{14,15},{16,17},{18,19},{..., dimensions={0}, use_global_device_ids=true | all-gather | bytes 1179648 | tf_op jit(solution)/shard_map/all_gather | solution.py:386
  32.0 0.4 shard_map.111
  32.4 4.5 %collective-permute-start = (bf16[64,768]{1,0:T(8,128)(2,1)S(1)}, bf16[64,768]{1,0:T(8,128)(2,1)S(1)}, u32[]{:S(2)}, u32[]{:S(2)}) collective-permute-start(bf16[64,768]{1,0:T(8,128)(2,1)S(1)} %get-tuple-element.20), channel_id=1, source_target_pairs={{0,4},{4,8},{8,12},{12,16},{16,20},{20,24},{24,28},{28,32},{32,36}... | collective-permute-start | bytes 294920 | tf_op jit(solution)/shard_map/ppermute | solution.py:388
  36.9 0.0 copy-done
  36.9 4.2 %shard_map.112 = (bf16[336,128]{1,0:T(8,128)(2,1)S(1)}, bf16[256,192]{1,0:T(8,128)(2,1)S(1)}, bf16[3,32,768]{2,1,0:T(8,128)(2,1)S(1)}, bf16[6912,192]{1,0:T(8,128)(2,1)S(1)}) custom-call(s32[6]{0:T(128)S(1)} %copy-done, bf16[256,768]{1,0:T(8,128)(2,1)S(1)} %get-tuple-element.21.rows_ref, f32[2,384]{1,0:T(2,128)S(1)} %get-tuple-element.22.wide_ref, ...), custom_call_target="tpu_custom_call" | custom-call | flops 2000000000 | bytes 1048576 | tf_op jit(solution)/shard_map/pallas_call | solution.py:323
  41.1 0.0 copy-start.1
  41.1 0.0 collective-permute-done.earlier_ref
  41.1 2.0 %shard_map.113 = bf16[432,128]{1,0:T(8,128)(2,1)S(1)} custom-call(s32[6]{0:T(128)S(1)} %copy-done, bf16[64,768]{1,0:T(8,128)(2,1)S(1)} %collective-permute-done.earlier_ref, bf16[3,32,768]{2,1,0:T(8,128)(2,1)S(1)} %get-tuple-element.28.head_ref, f32[2,384]{1,0:T(2,128)S(1)} %get-tuple-element.22.wide_ref, f32[4,192]{1,0:T(4,128)S(1)} %get-tuple-element.23.own_ref, ...), custom_call_target="tpu_custom_call" | custom-call | flops 1000000000 | bytes 1048576 | tf_op jit(solution)/shard_map/pallas_call | solution.py:323
  43.2 12.4 %all-gather = bf16[1728,128]{1,0:T(8,128)(2,1)S(1)} all-gather(bf16[432,128]{1,0:T(8,128)(2,1)S(1)} %shard_map.113), channel_id=2, replica_groups=mesh['dp'=8,'ta'=16,'ha'=4] {'ha'}, dimensions={0}, use_global_device_ids=true | all-gather | bytes 552960 | tf_op jit(solution)/shard_map/all_gather | solution.py:404
  55.6 0.0 copy-done.1
  55.6 2.1 %shard_map.114 = bf16[4,96,128]{2,1,0:T(8,128)(2,1)S(1)} custom-call(s32[6]{0:T(128)S(1)} %copy-done, bf16[4,432,128]{2,1,0:T(8,128)(2,1)S(1)} %bitcast.6, bf16[256,192]{1,0:T(8,128)(2,1)S(1)} %get-tuple-element.31.rest_ref, f32[4,192]{1,0:T(4,128)S(1)} %get-tuple-element.23.own_ref, bf16[9,192,768]{2,1,0:T(8,128)(2,1)S(1)} %copy-done.1), custom_call_target="tpu_custom_call" | custom-call | flops 2000000000 | bytes 1048576 | tf_op jit(solution)/shard_map/pallas_call | solution.py:323
  57.7 11.1 %all_to_all.10.parts_ref = bf16[4,96,128]{2,1,0:T(8,128)(2,1)S(1)} all-to-all(bf16[4,96,128]{2,1,0:T(8,128)(2,1)S(1)} %shard_map.114), channel_id=1, replica_groups=mesh['dp'=8,'ta'=16,'ha'=4] {'ha'}, dimensions={0} | all-to-all | bytes 196608 | tf_op jit(solution)/shard_map/all_to_all | solution.py:412
  68.8 0.9 %shard_map.115 = bf16[16,4,2,384]{3,2,1,0:T(2,128)(2,1)} custom-call(bf16[4,96,128]{2,1,0:T(8,128)(2,1)S(1)} %all_to_all.10.parts_ref), custom_call_target="tpu_custom_call" | custom-call | bytes 1048576 | tf_op jit(solution)/shard_map/pallas_call | solution.py:323
Async XLA Ops:
  2.0 27.7 %all-to-all-start = ((bf16[32,8,768]{2,1,0:T(8,128)(2,1)}), bf16[32,8,768]{2,1,0:T(8,128)(2,1)S(1)}, u32[]{:S(2)}, u32[]{:S(2)}) async-start(bf16[32,8,768]{2,1,0:T(8,128)(2,1)} %bitcast.3), calls=%async_computation | async-start | bytes 786432 | tf_op jit(solution)/shard_map/all_to_all | solution.py:356
  15.4 21.5 %copy-start = (s32[6]{0:T(128)S(1)}, s32[6]{0:T(128)}, u32[]{:S(2)}) copy-start(s32[6]{0:T(128)} %count_ref.5) | copy-start | bytes 76
  32.4 8.7 %collective-permute-start = (bf16[64,768]{1,0:T(8,128)(2,1)S(1)}, bf16[64,768]{1,0:T(8,128)(2,1)S(1)}, u32[]{:S(2)}, u32[]{:S(2)}) collective-permute-start(bf16[64,768]{1,0:T(8,128)(2,1)S(1)} %get-tuple-element.20), channel_id=1, source_target_pairs={{0,4},{4,8},{8,12},{12,16},{16,20},{20,24},{24,28},{28,32},{32,36}... | collective-permute-start | bytes 294920 | tf_op jit(solution)/shard_map/ppermute | solution.py:388
  41.1 14.5 %copy-start.1 = (bf16[9,192,768]{2,1,0:T(8,128)(2,1)S(1)}, bf16[9,192,768]{2,1,0:T(8,128)(2,1)}, u32[]{:S(2)}) copy-start(bf16[9,192,768]{2,1,0:T(8,128)(2,1)} %get-tuple-element.32.weight_ref) | copy-start | bytes 7962628

commit v4 on v3

--- a/solution.py
+++ b/solution.py
@@ -81,24 +81,16 @@
 def side_by_side(weight_ref, out_ref):
     for tap in range(9):
         for c in range(2):
-            part = weight_ref[tap, c * OWN : c * OWN + PAIR, :].astype(F32)
-            at = tap * WIDE + c * CH
-            out_ref[at : at + CH, :] = part.T.astype(BF16)
-
-
-def side_by_side_dense(weight_ref, out_ref):
-    for tap in range(9):
-        for c in range(2):
             out_ref[tap, :, c * CH : (c + 1) * CH] = weight_ref[tap, c * OWN : c * OWN + PAIR, :]
 
 
 def prepare_kernel(
-    plan_hbm, gain_hbm, bias_hbm, b1_hbm, g2_hbm, n2_hbm, b2_hbm, w1_hbm, w2_hbm,
-    table_ref, wide_ref, own_ref, same_wide_ref, same_own_ref, select_ref, first_ref, second_ref,
-    plan_ref, gain_ref, bias_ref, b1_ref, g2_ref, n2_ref, b2_ref, w1_ref, w2_ref, sems,
+    plan_hbm, gain_hbm, bias_hbm, b1_hbm, g2_hbm, n2_hbm, b2_hbm, w2_hbm,
+    table_ref, wide_ref, own_ref, same_wide_ref, same_own_ref, select_ref, second_ref,
+    plan_ref, gain_ref, bias_ref, b1_ref, g2_ref, n2_ref, b2_ref, w2_ref, sems,
 ):
     pairs = (
-        (plan_hbm, plan_ref), (w1_hbm, w1_ref), (w2_hbm, w2_ref), (gain_hbm, gain_ref), (bias_hbm, bias_ref),
+        (plan_hbm, plan_ref), (w2_hbm, w2_ref), (gain_hbm, gain_ref), (bias_hbm, bias_ref),
         (b1_hbm, b1_ref), (g2_hbm, g2_ref), (n2_hbm, n2_ref), (b2_hbm, b2_ref),
     )
     copies = [pltpu.make_async_copy(source, to, sems.at[k]) for k, (source, to) in enumerate(pairs)]
@@ -124,7 +116,7 @@
     want = (q + 1).astype(F32)
     table_ref[:, 0:256] = (held[0:1] == want).astype(BF16)
     table_ref[:, 256:512] = (held[1:2] == want).astype(BF16)
-    for copy in copies[3:]:
+    for copy in copies[2:]:
         copy.wait()
     wide_ref[0:1] = gain_ref[...].reshape(1, CH)
     wide_ref[1:2] = bias_ref[...].reshape(1, CH)
@@ -135,15 +127,11 @@
             part = jnp.where(ha == h, value[:, h * OWN : (h + 1) * OWN], part)
         own_ref[k : k + 1] = jnp.concatenate([part, part], axis=1)
     copies[1].wait()
-    side_by_side(w1_ref, first_ref)
-    copies[2].wait()
-    side_by_side_dense(w2_ref, second_ref)
-
-
-def unpack_kernel(table_ref, packed_ref, out_ref, tail_ref):
-    rows = dot(table_ref[...], packed_ref[...]).astype(BF16)
-    out_ref[...] = rows
-    tail_ref[...] = rows[BLOCK - 64 :]
+    side_by_side(w2_ref, second_ref)
+
+
+def tail_kernel(table_ref, packed_ref, tail_ref):
+    tail_ref[...] = dot(table_ref[BLOCK - EDGE :, :], packed_ref[...]).astype(BF16)
 
 
 def frame_stats(values, same):
@@ -208,11 +196,7 @@
     return total
 
 
-def with_first(weight_ref):
-    return lambda values, tap: dot(values, weight_ref[tap * WIDE : (tap + 1) * WIDE, :])
-
-
-def with_second(weight_ref):
+def with_weights(weight_ref):
     return lambda values, tap: dot_nt(values, weight_ref[tap])
 
 
@@ -239,18 +223,17 @@
 
 
 def main_kernel(
-    count_ref, rows_ref, wide_ref, own_ref, same_wide_ref, same_own_ref, select_ref, weight_hbm,
-    act_ref, rest_ref, head_ref, weight_ref, taps_ref, sem,
+    count_ref, table_ref, packed_ref, wide_ref, own_ref, same_wide_ref, same_own_ref, select_ref, raw_ref,
+    act_ref, rest_ref, head_ref, weight_ref, rows_ref, taps_ref,
 ):
-    copy = pltpu.make_async_copy(weight_hbm, weight_ref, sem)
-    copy.start()
     ta, _ = place()
+    rows_ref[...] = dot(table_ref[...], packed_ref[...]).astype(BF16)
+    side_by_side(raw_ref, weight_ref)
     norm_first(rows_ref, wide_ref, same_wide_ref[...], taps_ref)
     rest_ref[...] = dot(rows_ref[...], select_ref[...]).astype(BF16)
     for b in range(3):
         head_ref[b] = taps_ref[b, 0:32, :]
-    copy.wait()
-    hidden = convolve(taps_ref, with_first(weight_ref), INNER, ta * F_DEV + 2, count_ref) + own_ref[0:1]
+    hidden = convolve(taps_ref, with_weights(weight_ref), INNER, ta * F_DEV + 2, count_ref) + own_ref[0:1]
     act_ref[...] = norm_second(hidden.astype(BF16), own_ref, same_own_ref[...])
 
 
@@ -262,7 +245,7 @@
     norm_first(earlier_ref, wide_ref, same_wide_ref[...], taps_ref)
     for b in range(3):
         taps_ref[b, EDGE : EDGE + 32, :] = head_ref[b]
-    hidden = convolve(taps_ref, with_first(weight_ref), EDGE, ta * F_DEV - 2, count_ref) + own_ref[0:1]
+    hidden = convolve(taps_ref, with_weights(weight_ref), EDGE, ta * F_DEV - 2, count_ref) + own_ref[0:1]
     act_ref[0:CUT, :] = norm_second(hidden.astype(BF16), own_ref, same_own_ref[...])
     act_ref[CUT:FOLDED, :] = main_ref[...]
 
@@ -288,7 +271,7 @@
         ]
         whole = jnp.concatenate([p[:, OWN:] for p in parts] + [p[:, :OWN] for p in parts], axis=1)
         store_taps(taps_ref, f * ROWS, whole)
-    total = convolve(taps_ref, with_second(weight_ref), BLOCK, ta * F_DEV, count_ref)
+    total = convolve(taps_ref, with_weights(weight_ref), BLOCK, ta * F_DEV, count_ref)
     total = (total + own_ref[3:4] + rest_ref[...].astype(F32)).astype(BF16)
     to, at = iota((BLOCK, BLOCK), 0), iota((BLOCK, BLOCK), 1)
     order = (((to >> 2) & 15) * ROWS + (to >> 6) * 4 + (to & 3) == at).astype(BF16)
@@ -348,7 +331,7 @@
 
     [packed] = call(
         pack_kernel,
-        [((256, WIDE), BF16)],
+        [vmem((256, WIDE), BF16)],
         [hbm] * 2,
         [pltpu.VMEM((32, 128), I32), pltpu.VMEM((SLOTS, WIDE), BF16)] + [pltpu.SemaphoreType.DMA] * 2,
         flops=10**7,
@@ -356,8 +339,8 @@
     arrived = lax.all_to_all(
         packed.reshape(32, CAP, WIDE), ("ta", "ha"), 0, 0, axis_index_groups=same_core, tiled=True
     ).reshape(256, WIDE)
-    weight, raw = (9 * WIDE, PAIR), (9, 3 * OWN, CH)
-    table, wide, own, same_wide, same_own, select, first, second = call(
+    weight, raw = (9, PAIR, WIDE), (9, 3 * OWN, CH)
+    table, wide, own, same_wide, same_own, select, second = call(
         prepare_kernel,
         [
             vmem((BLOCK, 512), BF16),
@@ -367,10 +350,9 @@
             vmem((PAIR, PAIR), BF16),
             vmem((WIDE, PAIR), BF16),
             hbm(weight, BF16),
-            hbm((9, PAIR, WIDE), BF16),
         ],
-        [hbm] * 9,
-        [vmem((32, 128), I32)] + [vmem((CH,), F32)] * 6 + [vmem(raw, BF16)] * 2 + [pltpu.SemaphoreType.DMA((9,))],
+        [hbm] * 8,
+        [vmem((32, 128), I32)] + [vmem((CH,), F32)] * 6 + [vmem(raw, BF16), pltpu.SemaphoreType.DMA((8,))],
         flops=2 * 10**9,
     )(
         plan,
@@ -380,11 +362,10 @@
         second_norm_gain,
         second_norm_bias,
         second_convolution_bias,
-        first_convolution_weight.reshape(raw),
         second_convolution_weight.reshape(raw),
     )
     both = lax.all_gather(arrived, "ha", axis=0, axis_index_groups=chips, tiled=True)
-    rows, tail = call(unpack_kernel, [((BLOCK, WIDE), BF16), ((64, WIDE), BF16)], [vmem] * 2, flops=10**8)(table, both)
+    [tail] = call(tail_kernel, [((EDGE, WIDE), BF16)], [vmem] * 2, flops=10**8)(table, both)
     earlier = lax.ppermute(tail, "ta", [(i, i + 1) for i in range(n_ta - 1)])
     act, rest, head, near = call(
         main_kernel,
@@ -394,10 +375,10 @@
             vmem((3, 32, WIDE), BF16),
             vmem(weight, BF16),
         ],
-        [smem] + [vmem] * 6 + [hbm],
-        [vmem((3, BLOCK, WIDE), BF16), pltpu.SemaphoreType.DMA],
+        [smem] + [vmem] * 8,
+        [vmem((BLOCK, WIDE), BF16), vmem((3, BLOCK, WIDE), BF16)],
         flops=2 * 10**9,
-    )(latent_frame_count, rows, wide, own, same_wide, same_own, select, first)
+    )(latent_frame_count, table, both, wide, own, same_wide, same_own, select, first_convolution_weight.reshape(raw))
     [act] = call(
         halo_kernel, [((FOLDED, 128), BF16)], [smem] + [vmem] * 8, [vmem((3, EDGE + 32, WIDE), BF16)], flops=10**9
     )(latent_frame_count, earlier, head, wide, own, same_wide, same_own, near, act)

time: 70.1 us -> 70 us (level)
  the two profiles are of different devices: /device:TPU:62 before, /device:TPU:72 now
where the time goes in v4:
time: 70 us; the launch traced here: 69.6 us
  blocking collectives  25.3 us (36%)
  starting transfers between devices  15.1 us (22%)
  waiting for transfers between devices  14.8 us (21%)
  Pallas kernels  14.4 us (21%)
    pallas_call x7, Pallas kernels, pinned(): run(*(pltpu.with_memory_space_constraint(a, pltpu.HBM) if m is pltpu.HBM...  14.4 us
    all_to_all x1, starting transfers between devices, local(): lax.all_to_all(packed.reshape(32, CAP, WIDE), ('ta', 'ha'), 0, 0, axis_in...  12.6 us
    all_to_all x1, waiting for transfers between devices, local(): lax.all_to_all(packed.reshape(32, CAP, WIDE), ('ta', 'ha'), 0, 0, axis_in...  11.8 us
    all_gather x1, blocking collectives, local(): acts = lax.all_gather(act, 'ha', axis=0, tiled=False)  11.6 us
    all_to_all x1, blocking collectives, local(): parts = lax.all_to_all(out, 'ha', 0, 0, tiled=True)  11.4 us
    ppermute x1, waiting for transfers between devices, local(): earlier = lax.ppermute(tail, 'ta', [(i, i + 1) for i in range(n_ta - 1)])  2.99 us
    ppermute x1, starting transfers between devices, local(): earlier = lax.ppermute(tail, 'ta', [(i, i + 1) for i in range(n_ta - 1)])  2.5 us
    all_gather x1, blocking collectives, local(): lax.all_gather(arrived, 'ha', axis=0, axis_index_groups=chips, tiled=True)  2.36 us
  transfers between devices with their start and end apart: 2, of which 2 were waited for; matrix products, arithmetic and copies ran while one was open for 0% of the time, Pallas kernels for 10%

profile of v4, /device:TPU:72, one launch (start us, length us, event | category | flops | bytes accessed | tf_op | source)
XLA Modules:
  0.0 69.6 jit_solution(2302523629802007325)
XLA Ops:
  0.0 2.0 %shard_map.110 = bf16[256,768]{1,0:T(8,128)(2,1)} custom-call(s32[32,128]{1,0:T(8,128)} %bitcast.9, bf16[64,768]{1,0:T(8,128)(2,1)} %rows_hbm.1), custom_call_target="tpu_custom_call" | custom-call | flops 10000000 | bytes 1048576 | tf_op jit(solution)/shard_map/pallas_call | solution.py:306
  2.0 12.6 %all-to-all-start = ((bf16[32,8,768]{2,1,0:T(8,128)(2,1)}), bf16[32,8,768]{2,1,0:T(8,128)(2,1)S(1)}, u32[]{:S(2)}, u32[]{:S(2)}) async-start(bf16[32,8,768]{2,1,0:T(8,128)(2,1)} %bitcast.2), calls=%async_computation | async-start | bytes 786432 | tf_op jit(solution)/shard_map/all_to_all | solution.py:339
  14.6 0.0 copy-start
  14.6 0.0 copy-start.1
  14.6 3.5 %shard_map.109 = (bf16[256,512]{1,0:T(8,128)(2,1)S(1)}, f32[2,384]{1,0:T(2,128)S(1)}, f32[4,192]{1,0:T(4,128)S(1)}, bf16[384,384]{1,0:T(8,128)(2,1)S(1)}, bf16[1...) custom-call(s32[32,128]{1,0:T(8,128)} %bitcast.10, f32[384]{0:T(512)} %gain_hbm.1, ...), custom_call_target="tpu_custom_call" | custom-call | flops 2000000000 | bytes 1048576 | tf_op jit(solution)/shard_map/pallas_call | solution.py:306
  18.1 11.8 %all-to-all-done = bf16[32,8,768]{2,1,0:T(8,128)(2,1)S(1)} async-done(((bf16[32,8,768]{2,1,0:T(8,128)(2,1)}), bf16[32,8,768]{2,1,0:T(8,128)(2,1)S(1)}, u32[]{:S(2)}, u32[]{:S(2)}) %all-to-all-start) | async-done | bytes 393248 | tf_op jit(solution)/shard_map/all_to_all | solution.py:339
  30.0 2.4 %all_gather.9.packed_ref = bf16[512,768]{1,0:T(8,128)(2,1)S(1)} all-gather(bf16[256,768]{1,0:T(8,128)(2,1)S(1)} %bitcast.8), channel_id=1, replica_groups={{0,1},{2,3},{4,5},{6,7},{8,9},{10,11},{12,13},{14,15},{16,17},{18,19},{..., dimensions={0}, use_global_device_ids=true | all-gather | bytes 1179648 | tf_op jit(solution)/shard_map/all_gather | solution.py:367
  32.3 0.3 shard_map.111
  32.6 2.5 %collective-permute-start = (bf16[64,768]{1,0:T(8,128)(2,1)S(1)}, bf16[64,768]{1,0:T(8,128)(2,1)S(1)}, u32[]{:S(2)}, u32[]{:S(2)}) collective-permute-start(bf16[64,768]{1,0:T(8,128)(2,1)S(1)} %shard_map.111), channel_id=1, source_target_pairs={{0,4},{4,8},{8,12},{12,16},{16,20},{20,24},{24,28},{28,32},{32,36}... | collective-permute-start | bytes 294920 | tf_op jit(solution)/shard_map/ppermute | solution.py:369
  35.1 0.0 copy-done
  35.1 0.0 copy-done.1
  35.1 3.3 %shard_map.112 = (bf16[336,128]{1,0:T(8,128)(2,1)S(1)}, bf16[256,192]{1,0:T(8,128)(2,1)S(1)}, bf16[3,32,768]{2,1,0:T(8,128)(2,1)S(1)}, bf16[9,192,768]{2,1,0:T(8,128)(2,1)S(1)}) custom-call(s32[6]{0:T(128)S(1)} %copy-done.1, bf16[256,512]{1,0:T(8,128)(2,1)S(1)} %get-tuple-element.16.table_ref, bf16[512,768]{1,0:T(8,128)(2,1)S(1)} %all_gather.9.packed_ref, ...), custom_call_target="tpu_custom_call" | custom-call | flops 2000000000 | bytes 1048576 | tf_op jit(solution)/shard_map/pallas_call | solution.py:306
  38.4 0.0 copy-start.2
  38.4 3.0 %collective-permute-done.earlier_ref = bf16[64,768]{1,0:T(8,128)(2,1)S(1)} collective-permute-done((bf16[64,768]{1,0:T(8,128)(2,1)S(1)}, bf16[64,768]{1,0:T(8,128)(2,1)S(1)}, u32[]{:S(2)}, u32[]{:S(2)}) %collective-permute-start) | collective-permute-done | bytes 98336 | tf_op jit(solution)/shard_map/ppermute | solution.py:369
  41.4 2.3 %shard_map.113 = bf16[432,128]{1,0:T(8,128)(2,1)S(1)} custom-call(s32[6]{0:T(128)S(1)} %copy-done.1, bf16[64,768]{1,0:T(8,128)(2,1)S(1)} %collective-permute-done.earlier_ref, bf16[3,32,768]{2,1,0:T(8,128)(2,1)S(1)} %get-tuple-element.22.head_ref, f32[2,384]{1,0:T(2,128)S(1)} %get-tuple-element.17.wide_ref, f32[4,192]{1,0:T(4,128)S(1)} %get-tuple-element.18.own_ref, ...), custom_call_target="tpu_custom_call" | custom-call | flops 1000000000 | bytes 1048576 | tf_op jit(solution)/shard_map/pallas_call | solution.py:306
  43.7 11.6 %all-gather = bf16[1728,128]{1,0:T(8,128)(2,1)S(1)} all-gather(bf16[432,128]{1,0:T(8,128)(2,1)S(1)} %shard_map.113), channel_id=2, replica_groups=mesh['dp'=8,'ta'=16,'ha'=4] {'ha'}, dimensions={0}, use_global_device_ids=true | all-gather | bytes 552960 | tf_op jit(solution)/shard_map/all_gather | solution.py:385
  55.2 0.0 copy-done.2
  55.2 2.1 %shard_map.114 = bf16[4,96,128]{2,1,0:T(8,128)(2,1)S(1)} custom-call(s32[6]{0:T(128)S(1)} %copy-done.1, bf16[4,432,128]{2,1,0:T(8,128)(2,1)S(1)} %bitcast.6, bf16[256,192]{1,0:T(8,128)(2,1)S(1)} %get-tuple-element.25.rest_ref, f32[4,192]{1,0:T(4,128)S(1)} %get-tuple-element.18.own_ref, bf16[9,192,768]{2,1,0:T(8,128)(2,1)S(1)} %copy-done.2), custom_call_target="tpu_custom_call" | custom-call | flops 2000000000 | bytes 1048576 | tf_op jit(solution)/shard_map/pallas_call | solution.py:306
  57.3 11.4 %all_to_all.10.parts_ref = bf16[4,96,128]{2,1,0:T(8,128)(2,1)S(1)} all-to-all(bf16[4,96,128]{2,1,0:T(8,128)(2,1)S(1)} %shard_map.114), channel_id=1, replica_groups=mesh['dp'=8,'ta'=16,'ha'=4] {'ha'}, dimensions={0} | all-to-all | bytes 196608 | tf_op jit(solution)/shard_map/all_to_all | solution.py:393
  68.7 0.9 %shard_map.115 = bf16[16,4,2,384]{3,2,1,0:T(2,128)(2,1)} custom-call(bf16[4,96,128]{2,1,0:T(8,128)(2,1)S(1)} %all_to_all.10.parts_ref), custom_call_target="tpu_custom_call" | custom-call | bytes 1048576 | tf_op jit(solution)/shard_map/pallas_call | solution.py:306
Async XLA Ops:
  2.0 28.0 %all-to-all-start = ((bf16[32,8,768]{2,1,0:T(8,128)(2,1)}), bf16[32,8,768]{2,1,0:T(8,128)(2,1)S(1)}, u32[]{:S(2)}, u32[]{:S(2)}) async-start(bf16[32,8,768]{2,1,0:T(8,128)(2,1)} %bitcast.2), calls=%async_computation | async-start | bytes 786432 | tf_op jit(solution)/shard_map/all_to_all | solution.py:339
  14.6 20.5 %copy-start = (bf16[3,3,3,96,384]{4,3,2,1,0:T(8,128)(2,1)S(1)}, bf16[3,3,3,96,384]{4,3,2,1,0:T(8,128)(2,1)}, u32[]{:S(2)}) copy-start(bf16[3,3,3,96,384]{4,3,2,1,0:T(8,128)(2,1)} %param.16) | copy-start | bytes 5971972
  14.6 20.5 %copy-start.1 = (s32[6]{0:T(128)S(1)}, s32[6]{0:T(128)}, u32[]{:S(2)}) copy-start(s32[6]{0:T(128)} %count_ref.5) | copy-start | bytes 76
  32.6 8.8 %collective-permute-start = (bf16[64,768]{1,0:T(8,128)(2,1)S(1)}, bf16[64,768]{1,0:T(8,128)(2,1)S(1)}, u32[]{:S(2)}, u32[]{:S(2)}) collective-permute-start(bf16[64,768]{1,0:T(8,128)(2,1)S(1)} %shard_map.111), channel_id=1, source_target_pairs={{0,4},{4,8},{8,12},{12,16},{16,20},{20,24},{24,28},{28,32},{32,36}... | collective-permute-start | bytes 294920 | tf_op jit(solution)/shard_map/ppermute | solution.py:369
  38.4 16.8 %copy-start.2 = (bf16[9,192,768]{2,1,0:T(8,128)(2,1)S(1)}, bf16[9,192,768]{2,1,0:T(8,128)(2,1)}, u32[]{:S(2)}) copy-start(bf16[9,192,768]{2,1,0:T(8,128)(2,1)} %get-tuple-element.26.weight_ref) | copy-start | bytes 7962628

commit v5 on v4

--- a/solution.py
+++ b/solution.py
@@ -16,6 +16,10 @@
 SLOTS = 64
 CAP = 8
 VIDEOS = 6
+EDGE = 64
+INNER = BLOCK - 2 * ROWS
+FOLDED = (EDGE + INNER) * 3 // 2
+CUT = EDGE * 3 // 2
 F32, BF16, I32 = jnp.float32, jnp.bfloat16, jnp.int32
 VMEM_LIMIT = 24 * 2**20
 
@@ -85,8 +89,8 @@
 
 
 def prepare_kernel(
-    plan_hbm, gain_hbm, bias_hbm, b1_hbm, g2_hbm, n2_hbm, b2_hbm, w2_hbm,
-    table_ref, wide_ref, own_ref, same_wide_ref, same_own_ref, select_ref, second_ref,
+    count_ref, plan_hbm, gain_hbm, bias_hbm, b1_hbm, g2_hbm, n2_hbm, b2_hbm, w2_hbm,
+    table_ref, keep_ref, wide_ref, own_ref, same_wide_ref, same_own_ref, select_ref, second_ref,
     plan_ref, gain_ref, bias_ref, b1_ref, g2_ref, n2_ref, b2_ref, w2_ref, sems,
 ):
     pairs = (
@@ -97,11 +101,19 @@
     for copy in copies:
         copy.start()
     ta, ha = place()
+    frame = ta * F_DEV - 2 + (iota((EDGE + INNER, 2), 0) >> 4)
+    start = jnp.zeros((EDGE + INNER, 2), I32)
+    end = jnp.int32(0)
+    for v in range(VIDEOS):
+        count = count_ref[v]
+        end = end + count
+        start = start + jnp.where(frame >= end, count, 0)
+    keep_ref[...] = jnp.where(frame - 2 + iota((EDGE + INNER, 2), 1) >= start, 1.0, 0.0).astype(BF16)
     same_wide_ref[...] = same_group(CH, CH)
     same_own_ref[...] = same_group(PAIR, OWN)
-    lane = iota((WIDE, PAIR), 1)
+    lane = iota((PAIR, WIDE), 0)
     source = ha * OWN + jnp.where(lane < OWN, CH + lane, lane - OWN)
-    select_ref[...] = (iota((WIDE, PAIR), 0) == source).astype(BF16)
+    select_ref[...] = (iota((PAIR, WIDE), 1) == source).astype(BF16)
     copies[0].wait()
     plan = plan_ref[...]
     match = (plan >> 8) == ta
@@ -134,22 +146,38 @@
     tail_ref[...] = dot(table_ref[BLOCK - EDGE :, :], packed_ref[...]).astype(BF16)
 
 
-def frame_stats(values, same):
-    rows, lanes = values.shape
-    pick = ((iota((16, rows), 1) >> 4) == iota((16, rows), 0)).astype(BF16)
+def squares(values):
     wide = values.astype(F32)
     square = wide * wide
     high = square.astype(BF16)
-    low = (square - high.astype(F32)).astype(BF16)
+    return high, (square - high.astype(F32)).astype(BF16)
+
+
+def moments(total, total_squares):
+    entries = ROWS * 2 * GROUP
+    mean = total / entries
+    return mean, lax.rsqrt(total_squares / entries - mean * mean + 1e-06)
+
+
+def wide_stats(values, same):
+    rows = values.shape[0]
+    pick = ((iota((16, rows), 1) >> 4) == iota((16, rows), 0)).astype(BF16)
+    high, low = squares(values)
     both = jnp.concatenate([dot(pick, values), dot(pick, high) + dot(pick, low)], axis=0)
-    if lanes == WIDE:
-        both = both[:, :CH] + both[:, CH:]
+    both = both[:, :CH] + both[:, CH:]
     total = dot(jnp.concatenate(three(both), axis=0), same)
     total = total[0:32] + total[32:64] + total[64:96]
-    entries = ROWS * 2 * GROUP
-    mean = total[0:16] / entries
-    var = total[16:32] / entries - mean * mean
-    return mean, lax.rsqrt(var + 1e-06)
+    return moments(total[0:16], total[16:32])
+
+
+def own_stats(values, same):
+    rows = values.shape[0]
+    total = dot(jnp.concatenate([values, *squares(values)], axis=0), same)
+    by_frame = [
+        jnp.sum(part.reshape(rows // ROWS, ROWS, PAIR), axis=1)
+        for part in (total[:rows], total[rows : 2 * rows] + total[2 * rows :])
+    ]
+    return moments(*by_frame)
 
 
 def silu(v):
@@ -165,7 +193,7 @@
 
 def norm_first(rows_ref, wide_ref, same, taps_ref):
     gain, bias = wide_ref[0:1], wide_ref[1:2]
-    mean, inverse = frame_stats(rows_ref[...], same)
+    mean, inverse = wide_stats(rows_ref[...], same)
     for f in range(rows_ref.shape[0] // ROWS):
         value = rows_ref[f * ROWS : (f + 1) * ROWS, :].astype(F32)
         m, s = mean[f : f + 1], inverse[f : f + 1]
@@ -175,7 +203,7 @@
         store_taps(taps_ref, f * ROWS, jnp.concatenate(halves, axis=1))
 
 
-def convolve(taps_ref, product, rows, first_frame, count_ref):
+def convolve(taps_ref, product, rows, keep):
     totals = []
     for a in range(3):
         acc = None
@@ -183,17 +211,8 @@
             part = product(taps_ref[b, a * ROWS : a * ROWS + rows, :], 3 * a + b)
             acc = part if acc is None else acc + part
         totals.append(acc)
-    frame = first_frame + (iota((rows, 1), 0) >> 4)
-    start = jnp.zeros((rows, 1), I32)
-    end = jnp.int32(0)
-    for v in range(VIDEOS):
-        count = count_ref[v]
-        end = end + count
-        start = start + jnp.where(frame >= end, count, 0)
-    total = totals[2]
-    for a in range(2):
-        total = total + totals[a] * jnp.where(frame - 2 + a >= start, 1.0, 0.0)
-    return total
+    keep = keep.astype(F32)
+    return totals[2] + totals[0] * keep[:, 0:1] + totals[1] * keep[:, 1:2]
 
 
 def with_weights(weight_ref):
@@ -208,7 +227,7 @@
 
 def norm_second(hidden, own_ref, same):
     gain, bias = own_ref[1:2], own_ref[2:3]
-    mean, inverse = frame_stats(hidden, same)
+    mean, inverse = own_stats(hidden, same)
     acts = []
     for f in range(hidden.shape[0] // ROWS):
         value = hidden[f * ROWS : (f + 1) * ROWS].astype(F32)
@@ -216,36 +235,28 @@
     return fold(jnp.concatenate(acts, axis=0)).astype(BF16)
 
 
-EDGE = 64
-INNER = BLOCK - 2 * ROWS
-FOLDED = (EDGE + INNER) * 3 // 2
-CUT = EDGE * 3 // 2
-
-
 def main_kernel(
-    count_ref, table_ref, packed_ref, wide_ref, own_ref, same_wide_ref, same_own_ref, select_ref, raw_ref,
+    keep_ref, table_ref, packed_ref, wide_ref, own_ref, same_wide_ref, same_own_ref, select_ref, raw_ref,
     act_ref, rest_ref, head_ref, weight_ref, rows_ref, taps_ref,
 ):
-    ta, _ = place()
     rows_ref[...] = dot(table_ref[...], packed_ref[...]).astype(BF16)
     side_by_side(raw_ref, weight_ref)
     norm_first(rows_ref, wide_ref, same_wide_ref[...], taps_ref)
-    rest_ref[...] = dot(rows_ref[...], select_ref[...]).astype(BF16)
+    rest_ref[...] = dot_nt(rows_ref[...], select_ref[...]).astype(BF16)
     for b in range(3):
         head_ref[b] = taps_ref[b, 0:32, :]
-    hidden = convolve(taps_ref, with_weights(weight_ref), INNER, ta * F_DEV + 2, count_ref) + own_ref[0:1]
+    hidden = convolve(taps_ref, with_weights(weight_ref), INNER, keep_ref[EDGE:, :]) + own_ref[0:1]
     act_ref[...] = norm_second(hidden.astype(BF16), own_ref, same_own_ref[...])
 
 
 def halo_kernel(
-    count_ref, earlier_ref, head_ref, wide_ref, own_ref, same_wide_ref, same_own_ref, weight_ref, main_ref,
+    keep_ref, earlier_ref, head_ref, wide_ref, own_ref, same_wide_ref, same_own_ref, weight_ref, main_ref,
     act_ref, taps_ref,
 ):
-    ta, _ = place()
     norm_first(earlier_ref, wide_ref, same_wide_ref[...], taps_ref)
     for b in range(3):
         taps_ref[b, EDGE : EDGE + 32, :] = head_ref[b]
-    hidden = convolve(taps_ref, with_weights(weight_ref), EDGE, ta * F_DEV - 2, count_ref) + own_ref[0:1]
+    hidden = convolve(taps_ref, with_weights(weight_ref), EDGE, keep_ref[0:EDGE, :]) + own_ref[0:1]
     act_ref[0:CUT, :] = norm_second(hidden.astype(BF16), own_ref, same_own_ref[...])
     act_ref[CUT:FOLDED, :] = main_ref[...]
 
@@ -263,15 +274,14 @@
     )
 
 
-def last_kernel(count_ref, act_ref, rest_ref, own_ref, weight_ref, out_ref, taps_ref):
-    ta, _ = place()
+def last_kernel(keep_ref, act_ref, rest_ref, own_ref, weight_ref, out_ref, taps_ref):
     for f in range(F_DEV + 2):
         parts = [
             unfolded(act_ref, h, 0, 4, f) if f < 4 else unfolded(act_ref, h, CUT, 14, f - 4) for h in range(4)
         ]
         whole = jnp.concatenate([p[:, OWN:] for p in parts] + [p[:, :OWN] for p in parts], axis=1)
         store_taps(taps_ref, f * ROWS, whole)
-    total = convolve(taps_ref, with_weights(weight_ref), BLOCK, ta * F_DEV, count_ref)
+    total = convolve(taps_ref, with_weights(weight_ref), BLOCK, keep_ref[2 * ROWS :, :])
     total = (total + own_ref[3:4] + rest_ref[...].astype(F32)).astype(BF16)
     to, at = iota((BLOCK, BLOCK), 0), iota((BLOCK, BLOCK), 1)
     order = (((to >> 2) & 15) * ROWS + (to >> 6) * 4 + (to & 3) == at).astype(BF16)
@@ -340,21 +350,23 @@
         packed.reshape(32, CAP, WIDE), ("ta", "ha"), 0, 0, axis_index_groups=same_core, tiled=True
     ).reshape(256, WIDE)
     weight, raw = (9, PAIR, WIDE), (9, 3 * OWN, CH)
-    table, wide, own, same_wide, same_own, select, second = call(
+    table, keep, wide, own, same_wide, same_own, select, second = call(
         prepare_kernel,
         [
             vmem((BLOCK, 512), BF16),
+            vmem((EDGE + INNER, 2), BF16),
             vmem((2, CH), F32),
             vmem((4, PAIR), F32),
             vmem((CH, CH), BF16),
             vmem((PAIR, PAIR), BF16),
-            vmem((WIDE, PAIR), BF16),
+            vmem((PAIR, WIDE), BF16),
             hbm(weight, BF16),
         ],
-        [hbm] * 8,
+        [smem] + [hbm] * 8,
         [vmem((32, 128), I32)] + [vmem((CH,), F32)] * 6 + [vmem(raw, BF16), pltpu.SemaphoreType.DMA((8,))],
         flops=2 * 10**9,
     )(
+        latent_frame_count,
         plan,
         first_norm_gain,
         first_norm_bias,
@@ -375,21 +387,21 @@
             vmem((3, 32, WIDE), BF16),
             vmem(weight, BF16),
         ],
-        [smem] + [vmem] * 8,
+        [vmem] * 9,
         [vmem((BLOCK, WIDE), BF16), vmem((3, BLOCK, WIDE), BF16)],
         flops=2 * 10**9,
-    )(latent_frame_count, table, both, wide, own, same_wide, same_own, select, first_convolution_weight.reshape(raw))
+    )(keep, table, both, wide, own, same_wide, same_own, select, first_convolution_weight.reshape(raw))
     [act] = call(
-        halo_kernel, [((FOLDED, 128), BF16)], [smem] + [vmem] * 8, [vmem((3, EDGE + 32, WIDE), BF16)], flops=10**9
-    )(latent_frame_count, earlier, head, wide, own, same_wide, same_own, near, act)
+        halo_kernel, [((FOLDED, 128), BF16)], [vmem] * 9, [vmem((3, EDGE + 32, WIDE), BF16)], flops=10**9
+    )(keep, earlier, head, wide, own, same_wide, same_own, near, act)
     acts = lax.all_gather(act, "ha", axis=0, tiled=False)
     [out] = call(
         last_kernel,
         [((4, 96, 128), BF16)],
-        [smem] + [vmem] * 4,
+        [vmem] * 5,
         [pltpu.VMEM((3, EDGE + INNER, WIDE), BF16)],
         flops=2 * 10**9,
-    )(latent_frame_count, acts, rest, own, second)
+    )(keep, acts, rest, own, second)
     parts = lax.all_to_all(out, "ha", 0, 0, tiled=True)
     [joined] = call(join_kernel, [((F_DEV, 4, 2, CH), BF16)], [vmem])(parts)
     return joined

time: 70 us -> 68.8 us (0.983)
  Pallas kernels: 14.4 us -> 13 us
    pallas_call x7, Pallas kernels: 14.4 us -> 13 us  [pinned(): run(*(pltpu.with_memory_space_constraint(a, pltpu.HBM) if m is pltpu.HBM...]
    all_to_all x1, waiting for transfers between devices: 11.8 us -> 10.7 us  [local(): lax.all_to_all(packed.reshape(32, CAP, WIDE), ('ta', 'ha'), 0, 0, axis_in...]
where the time goes in v5:
time: 68.8 us; the launch traced here: 68.4 us
  blocking collectives  25.3 us (37%)
  starting transfers between devices  15.1 us (22%)
  waiting for transfers between devices  14.3 us (21%)
  Pallas kernels  13 us (19%)
    pallas_call x7, Pallas kernels, pinned(): run(*(pltpu.with_memory_space_constraint(a, pltpu.HBM) if m is pltpu.HBM...  13 us
    all_to_all x1, starting transfers between devices, local(): lax.all_to_all(packed.reshape(32, CAP, WIDE), ('ta', 'ha'), 0, 0, axis_in...  12.6 us
    all_gather x1, blocking collectives, local(): acts = lax.all_gather(act, 'ha', axis=0, tiled=False)  11.6 us
    all_to_all x1, blocking collectives, local(): parts = lax.all_to_all(out, 'ha', 0, 0, tiled=True)  11.4 us
    all_to_all x1, waiting for transfers between devices, local(): lax.all_to_all(packed.reshape(32, CAP, WIDE), ('ta', 'ha'), 0, 0, axis_in...  10.7 us
    ppermute x1, waiting for transfers between devices, local(): earlier = lax.ppermute(tail, 'ta', [(i, i + 1) for i in range(n_ta - 1)])  3.63 us
    ppermute x1, starting transfers between devices, local(): earlier = lax.ppermute(tail, 'ta', [(i, i + 1) for i in range(n_ta - 1)])  2.5 us
    all_gather x1, blocking collectives, local(): lax.all_gather(arrived, 'ha', axis=0, axis_index_groups=chips, tiled=True)  2.36 us
  transfers between devices with their start and end apart: 2, of which 2 were waited for; matrix products, arithmetic and copies ran while one was open for 0% of the time, Pallas kernels for 10%

profile of v5, /device:TPU:72, one launch (start us, length us, event | category | flops | bytes accessed | tf_op | source)
XLA Modules:
  0.0 68.4 jit_solution(11117975265516639056)
XLA Ops:
  0.0 2.0 %shard_map.110 = bf16[256,768]{1,0:T(8,128)(2,1)} custom-call(s32[32,128]{1,0:T(8,128)} %bitcast.9, bf16[64,768]{1,0:T(8,128)(2,1)} %rows_hbm.1), custom_call_target="tpu_custom_call" | custom-call | flops 10000000 | bytes 1048576 | tf_op jit(solution)/shard_map/pallas_call | solution.py:316
  2.0 12.6 %all-to-all-start = ((bf16[32,8,768]{2,1,0:T(8,128)(2,1)}), bf16[32,8,768]{2,1,0:T(8,128)(2,1)S(1)}, u32[]{:S(2)}, u32[]{:S(2)}) async-start(bf16[32,8,768]{2,1,0:T(8,128)(2,1)} %bitcast.2), calls=%async_computation | async-start | bytes 786432 | tf_op jit(solution)/shard_map/all_to_all | solution.py:349
  14.6 0.0 copy-start.1
  14.6 0.6 copy-done.1
  15.2 0.0 copy-start
  15.2 4.0 %shard_map.109 = (bf16[256,512]{1,0:T(8,128)(2,1)S(1)}, bf16[288,2]{1,0:T(8,128)(2,1)S(1)}, f32[2,384]{1,0:T(2,128)S(1)}, f32[4,192]{1,0:T(4,128)S(1)}, bf16[384...) custom-call(s32[6]{0:T(128)S(1)} %copy-done.1, ...), custom_call_target="tpu_custom_call" | custom-call | flops 2000000000 | bytes 1048576 | tf_op jit(solution)/shard_map/pallas_call | solution.py:316
  19.2 10.7 %all-to-all-done = bf16[32,8,768]{2,1,0:T(8,128)(2,1)S(1)} async-done(((bf16[32,8,768]{2,1,0:T(8,128)(2,1)}), bf16[32,8,768]{2,1,0:T(8,128)(2,1)S(1)}, u32[]{:S(2)}, u32[]{:S(2)}) %all-to-all-start) | async-done | bytes 393248 | tf_op jit(solution)/shard_map/all_to_all | solution.py:349
  30.0 2.4 %all_gather.9.packed_ref = bf16[512,768]{1,0:T(8,128)(2,1)S(1)} all-gather(bf16[256,768]{1,0:T(8,128)(2,1)S(1)} %bitcast.8), channel_id=1, replica_groups={{0,1},{2,3},{4,5},{6,7},{8,9},{10,11},{12,13},{14,15},{16,17},{18,19},{..., dimensions={0}, use_global_device_ids=true | all-gather | bytes 1179648 | tf_op jit(solution)/shard_map/all_gather | solution.py:379
  32.3 0.3 shard_map.111
  32.6 2.5 %collective-permute-start = (bf16[64,768]{1,0:T(8,128)(2,1)S(1)}, bf16[64,768]{1,0:T(8,128)(2,1)S(1)}, u32[]{:S(2)}, u32[]{:S(2)}) collective-permute-start(bf16[64,768]{1,0:T(8,128)(2,1)S(1)} %shard_map.111), channel_id=1, source_target_pairs={{0,4},{4,8},{8,12},{12,16},{16,20},{20,24},{24,28},{28,32},{32,36}... | collective-permute-start | bytes 294920 | tf_op jit(solution)/shard_map/ppermute | solution.py:381
  35.1 0.0 copy-done
  35.1 2.7 %shard_map.112 = (bf16[336,128]{1,0:T(8,128)(2,1)S(1)}, bf16[256,192]{1,0:T(8,128)(2,1)S(1)}, bf16[3,32,768]{2,1,0:T(8,128)(2,1)S(1)}, bf16[9,192,768]{2,1,0:T(8,128)(2,1)S(1)}) custom-call(bf16[288,2]{1,0:T(8,128)(2,1)S(1)} %get-tuple-element.17.keep_ref, bf16[256,512]{1,0:T(8,128)(2,1)S(1)} %get-tuple-element.18.table_ref, ...), custom_call_target="tpu_custom_call" | custom-call | flops 2000000000 | bytes 1048576 | tf_op jit(solution)/shard_map/pallas_call | solution.py:316
  37.8 0.0 copy-start.2
  37.8 3.6 %collective-permute-done.earlier_ref = bf16[64,768]{1,0:T(8,128)(2,1)S(1)} collective-permute-done((bf16[64,768]{1,0:T(8,128)(2,1)S(1)}, bf16[64,768]{1,0:T(8,128)(2,1)S(1)}, u32[]{:S(2)}, u32[]{:S(2)}) %collective-permute-start) | collective-permute-done | bytes 98336 | tf_op jit(solution)/shard_map/ppermute | solution.py:381
  41.4 1.6 %shard_map.113 = bf16[432,128]{1,0:T(8,128)(2,1)S(1)} custom-call(bf16[288,2]{1,0:T(8,128)(2,1)S(1)} %get-tuple-element.17.keep_ref, bf16[64,768]{1,0:T(8,128)(2,1)S(1)} %collective-permute-done.earlier_ref, bf16[3,32,768]{2,1,0:T(8,128)(2,1)S(1)} %get-tuple-element.24.head_ref, f32[2,384]{1,0:T(2,128)S(1)} %get-tuple-element.19.wide_ref, ...), custom_call_target="tpu_custom_call" | custom-call | flops 1000000000 | bytes 1048576 | tf_op jit(solution)/shard_map/pallas_call | solution.py:316
  43.0 11.6 %all-gather = bf16[1728,128]{1,0:T(8,128)(2,1)S(1)} all-gather(bf16[432,128]{1,0:T(8,128)(2,1)S(1)} %shard_map.113), channel_id=2, replica_groups=mesh['dp'=8,'ta'=16,'ha'=4] {'ha'}, dimensions={0}, use_global_device_ids=true | all-gather | bytes 552960 | tf_op jit(solution)/shard_map/all_gather | solution.py:397
  54.5 0.0 copy-done.2
  54.5 1.6 %shard_map.114 = bf16[4,96,128]{2,1,0:T(8,128)(2,1)S(1)} custom-call(bf16[288,2]{1,0:T(8,128)(2,1)S(1)} %get-tuple-element.17.keep_ref, bf16[4,432,128]{2,1,0:T(8,128)(2,1)S(1)} %bitcast.6, bf16[256,192]{1,0:T(8,128)(2,1)S(1)} %get-tuple-element.27.rest_ref, f32[4,192]{1,0:T(4,128)S(1)} %get-tuple-element.20.own_ref, bf16[9,192,768]{2,1,0:T(8,128)(2,1)S(1)} %copy-done.2), custom_call_target="tpu_custom_call" | custom-call | flops 2000000000 | bytes 1048576 | tf_op jit(solution)/shard_map/pallas_call | solution.py:316
  56.1 11.4 %all_to_all.10.parts_ref = bf16[4,96,128]{2,1,0:T(8,128)(2,1)S(1)} all-to-all(bf16[4,96,128]{2,1,0:T(8,128)(2,1)S(1)} %shard_map.114), channel_id=1, replica_groups=mesh['dp'=8,'ta'=16,'ha'=4] {'ha'}, dimensions={0} | all-to-all | bytes 196608 | tf_op jit(solution)/shard_map/all_to_all | solution.py:405
  67.5 0.9 %shard_map.115 = bf16[16,4,2,384]{3,2,1,0:T(2,128)(2,1)} custom-call(bf16[4,96,128]{2,1,0:T(8,128)(2,1)S(1)} %all_to_all.10.parts_ref), custom_call_target="tpu_custom_call" | custom-call | bytes 1048576 | tf_op jit(solution)/shard_map/pallas_call | solution.py:316
Async XLA Ops:
  2.0 28.0 %all-to-all-start = ((bf16[32,8,768]{2,1,0:T(8,128)(2,1)}), bf16[32,8,768]{2,1,0:T(8,128)(2,1)S(1)}, u32[]{:S(2)}, u32[]{:S(2)}) async-start(bf16[32,8,768]{2,1,0:T(8,128)(2,1)} %bitcast.2), calls=%async_computation | async-start | bytes 786432 | tf_op jit(solution)/shard_map/all_to_all | solution.py:349
  14.6 0.7 copy-start.1
  15.2 19.9 %copy-start = (bf16[3,3,3,96,384]{4,3,2,1,0:T(8,128)(2,1)S(1)}, bf16[3,3,3,96,384]{4,3,2,1,0:T(8,128)(2,1)}, u32[]{:S(2)}) copy-start(bf16[3,3,3,96,384]{4,3,2,1,0:T(8,128)(2,1)} %param.16) | copy-start | bytes 5971972
  32.6 8.8 %collective-permute-start = (bf16[64,768]{1,0:T(8,128)(2,1)S(1)}, bf16[64,768]{1,0:T(8,128)(2,1)S(1)}, u32[]{:S(2)}, u32[]{:S(2)}) collective-permute-start(bf16[64,768]{1,0:T(8,128)(2,1)S(1)} %shard_map.111), channel_id=1, source_target_pairs={{0,4},{4,8},{8,12},{12,16},{16,20},{20,24},{24,28},{28,32},{32,36}... | collective-permute-start | bytes 294920 | tf_op jit(solution)/shard_map/ppermute | solution.py:381
  37.8 16.8 %copy-start.2 = (bf16[9,192,768]{2,1,0:T(8,128)(2,1)S(1)}, bf16[9,192,768]{2,1,0:T(8,128)(2,1)}, u32[]{:S(2)}) copy-start(bf16[9,192,768]{2,1,0:T(8,128)(2,1)} %get-tuple-element.28.weight_ref) | copy-start | bytes 7962628

commit v6 on v5

--- a/solution.py
+++ b/solution.py
@@ -15,11 +15,13 @@
 BLOCK = 256
 SLOTS = 64
 CAP = 8
+PLACES = 2 * CAP
 VIDEOS = 6
 EDGE = 64
 INNER = BLOCK - 2 * ROWS
-FOLDED = (EDGE + INNER) * 3 // 2
-CUT = EDGE * 3 // 2
+HELD = EDGE + BLOCK
+OUT = EDGE + INNER
+FOLDED = OUT * 3 // 2
 F32, BF16, I32 = jnp.float32, jnp.bfloat16, jnp.int32
 VMEM_LIMIT = 24 * 2**20
 
@@ -60,16 +62,22 @@
     ta, ha = place()
     own = ta * 4 + ha
     lower = (iota((128, 128), 0) < iota((128, 128), 1)).astype(BF16)
-    spot = iota((256, 128), 0)
-    spot = (spot >> 4) * CAP + (spot & 7)
+    spot = iota((32 * PLACES, 128), 0)
+    late = (spot & 15) >= CAP
+    spot = ((spot >> 5) - jnp.where(late, 1, 0)) * CAP + (spot & 7)
     plan_copy.wait()
     ids = plan_ref[pl.ds(own // 2, 1), :]
     ids = jnp.where(own % 2 == 1, pltpu.roll(ids, 64, 1), ids)
     block = ids >> 8
-    hit = iota((16, 128), 0) == block
-    before = dot(hit.astype(BF16), lower)
-    rank = jnp.sum(jnp.where(hit, before, 0.0), axis=0, keepdims=True)
-    hot = (spot == block * CAP + rank.astype(I32)).astype(BF16)
+    last = (ids & 255) >= BLOCK - EDGE
+    hit = jnp.where(iota((16, 128), 0) == block, 1.0, 0.0)
+    edge = jnp.where(last, hit, 0.0)
+    before = dot(jnp.concatenate([hit, edge], axis=0).astype(BF16), lower)
+    rank = jnp.sum(hit * before[0:16], axis=0, keepdims=True).astype(I32)
+    edge_rank = jnp.sum(edge * before[16:32], axis=0, keepdims=True).astype(I32)
+    position = block * CAP + rank
+    edge_position = jnp.where(last, block * CAP + edge_rank, -1000)
+    hot = (spot == jnp.where(late, edge_position, position)).astype(BF16)
     rows_copy.wait()
     out_ref[...] = dot(hot[:, :SLOTS], rows_ref[...]).astype(BF16)
 
@@ -101,14 +109,14 @@
     for copy in copies:
         copy.start()
     ta, ha = place()
-    frame = ta * F_DEV - 2 + (iota((EDGE + INNER, 2), 0) >> 4)
-    start = jnp.zeros((EDGE + INNER, 2), I32)
+    frame = ta * F_DEV - 2 + (iota((OUT, 2), 0) >> 4)
+    start = jnp.zeros((OUT, 2), I32)
     end = jnp.int32(0)
     for v in range(VIDEOS):
         count = count_ref[v]
         end = end + count
         start = start + jnp.where(frame >= end, count, 0)
-    keep_ref[...] = jnp.where(frame - 2 + iota((EDGE + INNER, 2), 1) >= start, 1.0, 0.0).astype(BF16)
+    keep_ref[...] = jnp.where(frame - 2 + iota((OUT, 2), 1) >= start, 1.0, 0.0).astype(BF16)
     same_wide_ref[...] = same_group(CH, CH)
     same_own_ref[...] = same_group(PAIR, OWN)
     lane = iota((PAIR, WIDE), 0)
@@ -116,18 +124,23 @@
     select_ref[...] = (iota((PAIR, WIDE), 1) == source).astype(BF16)
     copies[0].wait()
     plan = plan_ref[...]
-    match = (plan >> 8) == ta
     i, j = iota((128, 128), 0), iota((128, 128), 1)
-    before = dot(match.astype(BF16), ((i < j) & ((i >> 6) == (j >> 6))).astype(BF16))
-    value = jnp.where(match, (plan & 255) + 1, 0).astype(F32)
-    ranked = jnp.concatenate([jnp.where(before == k, value, 0.0) for k in range(CAP)], axis=0)
-    half = ((iota((8, 128), 1) >> 6) == iota((8, 128), 0)).astype(BF16)
-    held = dot_nt(half, ranked.astype(BF16))
-    q, p = iota((256, 256), 0), iota((256, 256), 1)
-    held = dot(held.astype(BF16), (q == (p & 7) * 32 + (p >> 3)).astype(BF16))
-    want = (q + 1).astype(F32)
-    table_ref[:, 0:256] = (held[0:1] == want).astype(BF16)
-    table_ref[:, 256:512] = (held[1:2] == want).astype(BF16)
+    earlier = ((i < j) & ((i >> 6) == (j >> 6))).astype(BF16)
+    place_in = plan & 255
+    mine = (plan >> 8) == ta
+    edge = ((plan >> 8) == ta - 1) & (place_in >= BLOCK - EDGE)
+    ranked = []
+    for match, value in ((mine, place_in + 1), (edge, place_in + 1 - (BLOCK - EDGE))):
+        before = dot(match.astype(BF16), earlier)
+        value = jnp.where(match, value, 0).astype(F32)
+        ranked += [jnp.where(before == k, value, 0.0) for k in range(CAP)]
+    half = ((iota((8, 128), 1) >> 6) == ha % 2).astype(BF16)
+    held = dot_nt(half, jnp.concatenate(ranked, axis=0).astype(BF16))
+    q, p = iota((512, 512), 0), iota((512, 512), 1)
+    held = dot(held.astype(BF16), (q == (p & 15) * 32 + (p >> 4)).astype(BF16))[0:1]
+    row, p = iota((HELD, 512), 0), iota((HELD, 512), 1)
+    want = (row + 1 - jnp.where((p & 15) < CAP, EDGE, 0)).astype(F32)
+    table_ref[...] = ((held == want) & (held > 0.0)).astype(BF16)
     for copy in copies[2:]:
         copy.wait()
     wide_ref[0:1] = gain_ref[...].reshape(1, CH)
@@ -142,8 +155,8 @@
     side_by_side(w2_ref, second_ref)
 
 
-def tail_kernel(table_ref, packed_ref, tail_ref):
-    tail_ref[...] = dot(table_ref[BLOCK - EDGE :, :], packed_ref[...]).astype(BF16)
+def unpack_kernel(table_ref, packed_ref, out_ref):
+    out_ref[...] = dot(table_ref[...], packed_ref[...]).astype(BF16)
 
 
 def squares(values):
@@ -161,13 +174,13 @@
 
 def wide_stats(values, same):
     rows = values.shape[0]
-    pick = ((iota((16, rows), 1) >> 4) == iota((16, rows), 0)).astype(BF16)
+    pick = ((iota((32, rows), 1) >> 4) == iota((32, rows), 0)).astype(BF16)
     high, low = squares(values)
     both = jnp.concatenate([dot(pick, values), dot(pick, high) + dot(pick, low)], axis=0)
     both = both[:, :CH] + both[:, CH:]
     total = dot(jnp.concatenate(three(both), axis=0), same)
-    total = total[0:32] + total[32:64] + total[64:96]
-    return moments(total[0:16], total[16:32])
+    total = total[0:64] + total[64:128] + total[128:192]
+    return moments(total[0:32], total[32:64])
 
 
 def own_stats(values, same):
@@ -236,38 +249,24 @@
 
 
 def main_kernel(
-    keep_ref, table_ref, packed_ref, wide_ref, own_ref, same_wide_ref, same_own_ref, select_ref, raw_ref,
-    act_ref, rest_ref, head_ref, weight_ref, rows_ref, taps_ref,
+    keep_ref, parts_ref, wide_ref, own_ref, same_wide_ref, same_own_ref, select_ref, raw_ref,
+    act_ref, rest_ref, rows_ref, taps_ref, weight_ref,
 ):
-    rows_ref[...] = dot(table_ref[...], packed_ref[...]).astype(BF16)
+    rows_ref[...] = (parts_ref[0:HELD, :].astype(F32) + parts_ref[HELD:, :].astype(F32)).astype(BF16)
     side_by_side(raw_ref, weight_ref)
     norm_first(rows_ref, wide_ref, same_wide_ref[...], taps_ref)
-    rest_ref[...] = dot_nt(rows_ref[...], select_ref[...]).astype(BF16)
-    for b in range(3):
-        head_ref[b] = taps_ref[b, 0:32, :]
-    hidden = convolve(taps_ref, with_weights(weight_ref), INNER, keep_ref[EDGE:, :]) + own_ref[0:1]
+    rest_ref[...] = dot_nt(rows_ref[EDGE:, :], select_ref[...]).astype(BF16)
+    hidden = convolve(taps_ref, with_weights(weight_ref), OUT, keep_ref[...]) + own_ref[0:1]
     act_ref[...] = norm_second(hidden.astype(BF16), own_ref, same_own_ref[...])
 
 
-def halo_kernel(
-    keep_ref, earlier_ref, head_ref, wide_ref, own_ref, same_wide_ref, same_own_ref, weight_ref, main_ref,
-    act_ref, taps_ref,
-):
-    norm_first(earlier_ref, wide_ref, same_wide_ref[...], taps_ref)
-    for b in range(3):
-        taps_ref[b, EDGE : EDGE + 32, :] = head_ref[b]
-    hidden = convolve(taps_ref, with_weights(weight_ref), EDGE, keep_ref[0:EDGE, :]) + own_ref[0:1]
-    act_ref[0:CUT, :] = norm_second(hidden.astype(BF16), own_ref, same_own_ref[...])
-    act_ref[CUT:FOLDED, :] = main_ref[...]
-
-
-def unfolded(ref, h, base, frames, f):
-    half = frames // 2
-    low = base + frames * ROWS + (f % half) * ROWS
+def unfolded(ref, h, f):
+    half = OUT // ROWS // 2
+    low = OUT + (f % half) * ROWS
     lane = 64 * (f // half)
     return jnp.concatenate(
         [
-            ref[h, base + f * ROWS : base + (f + 1) * ROWS, :].astype(F32),
+            ref[h, f * ROWS : (f + 1) * ROWS, :].astype(F32),
             ref[h, low : low + ROWS, :].astype(F32)[:, lane : lane + 64],
         ],
         axis=1,
@@ -276,9 +275,7 @@
 
 def last_kernel(keep_ref, act_ref, rest_ref, own_ref, weight_ref, out_ref, taps_ref):
     for f in range(F_DEV + 2):
-        parts = [
-            unfolded(act_ref, h, 0, 4, f) if f < 4 else unfolded(act_ref, h, CUT, 14, f - 4) for h in range(4)
-        ]
+        parts = [unfolded(act_ref, h, f) for h in range(4)]
         whole = jnp.concatenate([p[:, OWN:] for p in parts] + [p[:, :OWN] for p in parts], axis=1)
         store_taps(taps_ref, f * ROWS, whole)
     total = convolve(taps_ref, with_weights(weight_ref), BLOCK, keep_ref[2 * ROWS :, :])
@@ -341,20 +338,20 @@
 
     [packed] = call(
         pack_kernel,
-        [vmem((256, WIDE), BF16)],
+        [vmem((32 * PLACES, WIDE), BF16)],
         [hbm] * 2,
         [pltpu.VMEM((32, 128), I32), pltpu.VMEM((SLOTS, WIDE), BF16)] + [pltpu.SemaphoreType.DMA] * 2,
         flops=10**7,
     )(plan, decoder_feature_rows)
     arrived = lax.all_to_all(
-        packed.reshape(32, CAP, WIDE), ("ta", "ha"), 0, 0, axis_index_groups=same_core, tiled=True
-    ).reshape(256, WIDE)
+        packed.reshape(32, PLACES, WIDE), ("ta", "ha"), 0, 0, axis_index_groups=same_core, tiled=True
+    ).reshape(32 * PLACES, WIDE)
     weight, raw = (9, PAIR, WIDE), (9, 3 * OWN, CH)
     table, keep, wide, own, same_wide, same_own, select, second = call(
         prepare_kernel,
         [
-            vmem((BLOCK, 512), BF16),
-            vmem((EDGE + INNER, 2), BF16),
+            vmem((HELD, 512), BF16),
+            vmem((OUT, 2), BF16),
             vmem((2, CH), F32),
             vmem((4, PAIR), F32),
             vmem((CH, CH), BF16),
@@ -376,30 +373,21 @@
         second_convolution_bias,
         second_convolution_weight.reshape(raw),
     )
-    both = lax.all_gather(arrived, "ha", axis=0, axis_index_groups=chips, tiled=True)
-    [tail] = call(tail_kernel, [((EDGE, WIDE), BF16)], [vmem] * 2, flops=10**8)(table, both)
-    earlier = lax.ppermute(tail, "ta", [(i, i + 1) for i in range(n_ta - 1)])
-    act, rest, head, near = call(
+    [part] = call(unpack_kernel, [((HELD, WIDE), BF16)], [vmem] * 2, flops=10**8)(table, arrived)
+    parts = lax.all_gather(part, "ha", axis=0, axis_index_groups=chips, tiled=True)
+    act, rest = call(
         main_kernel,
-        [
-            vmem((FOLDED - CUT, 128), BF16),
-            vmem((BLOCK, PAIR), BF16),
-            vmem((3, 32, WIDE), BF16),
-            vmem(weight, BF16),
-        ],
-        [vmem] * 9,
-        [vmem((BLOCK, WIDE), BF16), vmem((3, BLOCK, WIDE), BF16)],
+        [((FOLDED, 128), BF16), vmem((BLOCK, PAIR), BF16)],
+        [vmem] * 8,
+        [vmem((HELD, WIDE), BF16), vmem((3, HELD, WIDE), BF16), vmem(weight, BF16)],
         flops=2 * 10**9,
-    )(keep, table, both, wide, own, same_wide, same_own, select, first_convolution_weight.reshape(raw))
-    [act] = call(
-        halo_kernel, [((FOLDED, 128), BF16)], [vmem] * 9, [vmem((3, EDGE + 32, WIDE), BF16)], flops=10**9
-    )(keep, earlier, head, wide, own, same_wide, same_own, near, act)
+    )(keep, parts, wide, own, same_wide, same_own, select, first_convolution_weight.reshape(raw))
     acts = lax.all_gather(act, "ha", axis=0, tiled=False)
     [out] = call(
         last_kernel,
         [((4, 96, 128), BF16)],
         [vmem] * 5,
-        [pltpu.VMEM((3, EDGE + INNER, WIDE), BF16)],
+        [vmem((3, OUT, WIDE), BF16)],
         flops=2 * 10**9,
     )(keep, acts, rest, own, second)
     parts = lax.all_to_all(out, "ha", 0, 0, tiled=True)

time: 68.8 us -> 70.8 us (1.029)
  the two profiles are of different devices: /device:TPU:72 before, /device:TPU:96 now
where the time goes in v6:
time: 70.8 us; the launch traced here: 70.5 us
  blocking collectives  26.3 us (37%)
  waiting for transfers between devices  18.4 us (26%)
  starting transfers between devices  12.6 us (18%)
  Pallas kernels  11.9 us (17%)
  local copies, waits for them, and re-layouts  1.35 us (2%)
    all_to_all x1, waiting for transfers between devices, local(): lax.all_to_all(packed.reshape(32, PLACES, WIDE), ('ta', 'ha'), 0, 0, axis...  18.4 us
    all_to_all x1, starting transfers between devices, local(): lax.all_to_all(packed.reshape(32, PLACES, WIDE), ('ta', 'ha'), 0, 0, axis...  12.6 us
    all_to_all x1, blocking collectives, local(): parts = lax.all_to_all(out, 'ha', 0, 0, tiled=True)  12.2 us
    pallas_call x6, Pallas kernels, pinned(): run(*(pltpu.with_memory_space_constraint(a, pltpu.HBM) if m is pltpu.HBM...  11.9 us
    all_gather x1, blocking collectives, local(): acts = lax.all_gather(act, 'ha', axis=0, tiled=False)  11.5 us
    all_gather x1, blocking collectives, local(): lax.all_gather(part, 'ha', axis=0, axis_index_groups=chips, tiled=True)  2.51 us
  transfers between devices with their start and end apart: 1, of which 1 were waited for; matrix products, arithmetic and copies ran while one was open for 0% of the time, Pallas kernels for 6%

profile of v6, /device:TPU:96, one launch (start us, length us, event | category | flops | bytes accessed | tf_op | source)
XLA Modules:
  0.0 70.5 jit_solution(13850028427710643491)
XLA Ops:
  0.0 0.0 copy-start.1
  0.0 2.2 %shard_map.110 = bf16[512,768]{1,0:T(8,128)(2,1)} custom-call(s32[32,128]{1,0:T(8,128)} %bitcast.9, bf16[64,768]{1,0:T(8,128)(2,1)} %rows_hbm.1), custom_call_target="tpu_custom_call" | custom-call | flops 10000000 | bytes 1048576 | tf_op jit(solution)/shard_map/pallas_call | solution.py:313
  2.2 12.6 %all-to-all-start = ((bf16[32,16,768]{2,1,0:T(8,128)(2,1)}), bf16[32,16,768]{2,1,0:T(8,128)(2,1)S(1)}, u32[]{:S(2)}, u32[]{:S(2)}) async-start(bf16[32,16,768]{2,1,0:T(8,128)(2,1)} %bitcast.2), calls=%async_computation | async-start | bytes 1572864 | tf_op jit(solution)/shard_map/all_to_all | solution.py:346
  14.8 0.0 copy-done.1
  14.8 4.0 %shard_map.109 = (bf16[320,512]{1,0:T(8,128)(2,1)S(1)}, bf16[288,2]{1,0:T(8,128)(2,1)S(1)}, f32[2,384]{1,0:T(2,128)S(1)}, f32[4,192]{1,0:T(4,128)S(1)}, bf16[384...) custom-call(s32[6]{0:T(128)S(1)} %copy-done.1, ...), custom_call_target="tpu_custom_call" | custom-call | flops 2000000000 | bytes 1048576 | tf_op jit(solution)/shard_map/pallas_call | solution.py:313
  18.8 0.0 copy-start.3
  18.8 0.7 copy-done.3
  19.5 0.0 copy-start.5
  19.5 0.6 copy-done.5
  20.2 0.0 copy-start
  20.2 18.4 %all-to-all-done = bf16[32,16,768]{2,1,0:T(8,128)(2,1)S(1)} async-done(((bf16[32,16,768]{2,1,0:T(8,128)(2,1)}), bf16[32,16,768]{2,1,0:T(8,128)(2,1)S(1)}, u32[]{:S(2)}, u32[]{:S(2)}) %all-to-all-start) | async-done | bytes 786464 | tf_op jit(solution)/shard_map/all_to_all | solution.py:346
  38.5 0.0 copy-start.4
  38.5 0.0 copy-start.6
  38.5 0.4 shard_map.111
  39.0 2.5 %all_gather.9.parts_ref = bf16[640,768]{1,0:T(8,128)(2,1)S(1)} all-gather(bf16[320,768]{1,0:T(8,128)(2,1)S(1)} %shard_map.111), channel_id=1, replica_groups={{0,1},{2,3},{4,5},{6,7},{8,9},{10,11},{12,13},{14,15},{16,17},{18,19},{..., dimensions={0}, use_global_device_ids=true | all-gather | bytes 1474560 | tf_op jit(solution)/shard_map/all_gather | solution.py:377
  41.5 0.0 copy-done
  41.5 0.0 copy-done.4
  41.5 0.0 copy-done.6
  41.5 0.0 copy-start.2
  41.5 2.8 %shard_map.112 = (bf16[432,128]{1,0:T(8,128)(2,1)S(1)}, bf16[256,192]{1,0:T(8,128)(2,1)S(1)}) custom-call(bf16[288,2]{1,0:T(8,128)(2,1)S(1)} %copy-done.6, bf16[640,768]{1,0:T(8,128)(2,1)S(1)} %all_gather.9.parts_ref, f32[2,384]{1,0:T(2,128)S(1)} %get-tuple-element.17.wide_ref, f32[4,192]{1,0:T(4,128)S(1)} %get-tuple-element.18.own_ref, ...), custom_call_target="tpu_custom_call" | custom-call | flops 2000000000 | bytes 1048576 | tf_op jit(solution)/shard_map/pallas_call | solution.py:313
  44.3 11.5 %all-gather = bf16[1728,128]{1,0:T(8,128)(2,1)S(1)} all-gather(bf16[432,128]{1,0:T(8,128)(2,1)S(1)} %get-tuple-element.22), channel_id=2, replica_groups=mesh['dp'=8,'ta'=16,'ha'=4] {'ha'}, dimensions={0}, use_global_device_ids=true | all-gather | bytes 552960 | tf_op jit(solution)/shard_map/all_gather | solution.py:385
  55.8 0.0 copy-done.2
  55.8 1.6 %shard_map.113 = bf16[4,96,128]{2,1,0:T(8,128)(2,1)S(1)} custom-call(bf16[288,2]{1,0:T(8,128)(2,1)S(1)} %copy-done.6, bf16[4,432,128]{2,1,0:T(8,128)(2,1)S(1)} %bitcast.7, bf16[256,192]{1,0:T(8,128)(2,1)S(1)} %get-tuple-element.23.rest_ref, f32[4,192]{1,0:T(4,128)S(1)} %get-tuple-element.18.own_ref, bf16[9,192,768]{2,1,0:T(8,128)(2,1)S(1)} %copy-done.2), custom_call_target="tpu_custom_call" | custom-call | flops 2000000000 | bytes 1048576 | tf_op jit(solution)/shard_map/pallas_call | solution.py:313
  57.4 12.2 %all_to_all.10.parts_ref = bf16[4,96,128]{2,1,0:T(8,128)(2,1)S(1)} all-to-all(bf16[4,96,128]{2,1,0:T(8,128)(2,1)S(1)} %shard_map.113), channel_id=1, replica_groups=mesh['dp'=8,'ta'=16,'ha'=4] {'ha'}, dimensions={0} | all-to-all | bytes 196608 | tf_op jit(solution)/shard_map/all_to_all | solution.py:393
  69.6 0.9 %shard_map.114 = bf16[16,4,2,384]{3,2,1,0:T(2,128)(2,1)} custom-call(bf16[4,96,128]{2,1,0:T(8,128)(2,1)S(1)} %all_to_all.10.parts_ref), custom_call_target="tpu_custom_call" | custom-call | bytes 1048576 | tf_op jit(solution)/shard_map/pallas_call | solution.py:313
Async XLA Ops:
  0.0 14.8 %copy-start.1 = (s32[6]{0:T(128)S(1)}, s32[6]{0:T(128)}, u32[]{:S(2)}) copy-start(s32[6]{0:T(128)} %count_ref.1) | copy-start | bytes 76
  2.2 36.3 %all-to-all-start = ((bf16[32,16,768]{2,1,0:T(8,128)(2,1)}), bf16[32,16,768]{2,1,0:T(8,128)(2,1)S(1)}, u32[]{:S(2)}, u32[]{:S(2)}) async-start(bf16[32,16,768]{2,1,0:T(8,128)(2,1)} %bitcast.2), calls=%async_computation | async-start | bytes 1572864 | tf_op jit(solution)/shard_map/all_to_all | solution.py:346
  18.8 0.7 %copy-start.3 = (bf16[192,768]{1,0:T(8,128)(2,1)}, bf16[192,768]{1,0:T(8,128)(2,1)S(1)}, u32[]{:S(2)}) copy-start(bf16[192,768]{1,0:T(8,128)(2,1)S(1)} %get-tuple-element.21.select_ref) | copy-start | bytes 884740
  19.5 0.6 copy-start.5
  20.2 21.3 %copy-start = (bf16[3,3,3,96,384]{4,3,2,1,0:T(8,128)(2,1)S(1)}, bf16[3,3,3,96,384]{4,3,2,1,0:T(8,128)(2,1)}, u32[]{:S(2)}) copy-start(bf16[3,3,3,96,384]{4,3,2,1,0:T(8,128)(2,1)} %param.16) | copy-start | bytes 5971972
  38.5 2.9 %copy-start.4 = (bf16[192,768]{1,0:T(8,128)(2,1)S(1)}, bf16[192,768]{1,0:T(8,128)(2,1)}, u32[]{:S(2)}) copy-start(bf16[192,768]{1,0:T(8,128)(2,1)} %copy-done.3) | copy-start | bytes 884740
  38.5 2.9 %copy-start.6 = (bf16[288,2]{1,0:T(8,128)(2,1)S(1)}, bf16[288,2]{1,0:T(8,128)(2,1)}, u32[]{:S(2)}) copy-start(bf16[288,2]{1,0:T(8,128)(2,1)} %copy-done.5) | copy-start | bytes 3460
  41.5 14.3 %copy-start.2 = (bf16[9,192,768]{2,1,0:T(8,128)(2,1)S(1)}, bf16[9,192,768]{2,1,0:T(8,128)(2,1)}, u32[]{:S(2)}) copy-start(bf16[9,192,768]{2,1,0:T(8,128)(2,1)} %get-tuple-element.24.weight_ref) | copy-start | bytes 7962628

commit v7 on v5

--- a/solution.py
+++ b/solution.py
@@ -90,7 +90,7 @@
 
 def prepare_kernel(
     count_ref, plan_hbm, gain_hbm, bias_hbm, b1_hbm, g2_hbm, n2_hbm, b2_hbm, w2_hbm,
-    table_ref, keep_ref, wide_ref, own_ref, same_wide_ref, same_own_ref, select_ref, second_ref,
+    table_ref, edge_ref, keep_ref, wide_ref, own_ref, same_wide_ref, same_own_ref, select_ref, second_ref,
     plan_ref, gain_ref, bias_ref, b1_ref, g2_ref, n2_ref, b2_ref, w2_ref, sems,
 ):
     pairs = (
@@ -128,6 +128,8 @@
     want = (q + 1).astype(F32)
     table_ref[:, 0:256] = (held[0:1] == want).astype(BF16)
     table_ref[:, 256:512] = (held[1:2] == want).astype(BF16)
+    here = jnp.where(ha % 2 == 0, held[0:1], held[1:2])
+    edge_ref[...] = (here == want[BLOCK - EDGE :]).astype(BF16)
     for copy in copies[2:]:
         copy.wait()
     wide_ref[0:1] = gain_ref[...].reshape(1, CH)
@@ -143,7 +145,7 @@
 
 
 def tail_kernel(table_ref, packed_ref, tail_ref):
-    tail_ref[...] = dot(table_ref[BLOCK - EDGE :, :], packed_ref[...]).astype(BF16)
+    tail_ref[...] = dot(table_ref[...], packed_ref[...]).astype(BF16)
 
 
 def squares(values):
@@ -156,7 +158,7 @@
 def moments(total, total_squares):
     entries = ROWS * 2 * GROUP
     mean = total / entries
-    return mean, lax.rsqrt(total_squares / entries - mean * mean + 1e-06)
+    return mean, lax.rsqrt(jnp.maximum(total_squares / entries - mean * mean, 0.0) + 1e-06)
 
 
 def wide_stats(values, same):
@@ -251,9 +253,10 @@
 
 def halo_kernel(
     keep_ref, earlier_ref, head_ref, wide_ref, own_ref, same_wide_ref, same_own_ref, weight_ref, main_ref,
-    act_ref, taps_ref,
+    act_ref, taps_ref, rows_ref,
 ):
-    norm_first(earlier_ref, wide_ref, same_wide_ref[...], taps_ref)
+    rows_ref[...] = (earlier_ref[0:EDGE, :].astype(F32) + earlier_ref[EDGE:, :].astype(F32)).astype(BF16)
+    norm_first(rows_ref, wide_ref, same_wide_ref[...], taps_ref)
     for b in range(3):
         taps_ref[b, EDGE : EDGE + 32, :] = head_ref[b]
     hidden = convolve(taps_ref, with_weights(weight_ref), EDGE, keep_ref[0:EDGE, :]) + own_ref[0:1]
@@ -350,10 +353,11 @@
         packed.reshape(32, CAP, WIDE), ("ta", "ha"), 0, 0, axis_index_groups=same_core, tiled=True
     ).reshape(256, WIDE)
     weight, raw = (9, PAIR, WIDE), (9, 3 * OWN, CH)
-    table, keep, wide, own, same_wide, same_own, select, second = call(
+    table, edge, keep, wide, own, same_wide, same_own, select, second = call(
         prepare_kernel,
         [
             vmem((BLOCK, 512), BF16),
+            vmem((EDGE, BLOCK), BF16),
             vmem((EDGE + INNER, 2), BF16),
             vmem((2, CH), F32),
             vmem((4, PAIR), F32),
@@ -376,9 +380,10 @@
         second_convolution_bias,
         second_convolution_weight.reshape(raw),
     )
+    [tail] = call(tail_kernel, [((EDGE, WIDE), BF16)], [vmem] * 2, flops=10**8)(edge, arrived)
+    tail, arrived = lax.optimization_barrier((tail, arrived))
+    earlier = lax.ppermute(tail, "ta", [(i, i + 1) for i in range(n_ta - 1)])
     both = lax.all_gather(arrived, "ha", axis=0, axis_index_groups=chips, tiled=True)
-    [tail] = call(tail_kernel, [((EDGE, WIDE), BF16)], [vmem] * 2, flops=10**8)(table, both)
-    earlier = lax.ppermute(tail, "ta", [(i, i + 1) for i in range(n_ta - 1)])
     act, rest, head, near = call(
         main_kernel,
         [
@@ -389,10 +394,11 @@
         ],
         [vmem] * 9,
         [vmem((BLOCK, WIDE), BF16), vmem((3, BLOCK, WIDE), BF16)],
-        flops=2 * 10**9,
+        flops=10**6,
     )(keep, table, both, wide, own, same_wide, same_own, select, first_convolution_weight.reshape(raw))
+    earlier = lax.all_gather(earlier, "ha", axis=0, axis_index_groups=chips, tiled=True)
     [act] = call(
-        halo_kernel, [((FOLDED, 128), BF16)], [vmem] * 9, [vmem((3, EDGE + 32, WIDE), BF16)], flops=10**9
+        halo_kernel, [((FOLDED, 128), BF16)], [vmem] * 9, [vmem((3, EDGE + 32, WIDE), BF16), vmem((EDGE, WIDE), BF16)], flops=10**9
     )(keep, earlier, head, wide, own, same_wide, same_own, near, act)
     acts = lax.all_gather(act, "ha", axis=0, tiled=False)
     [out] = call(

time: 68.8 us -> 69.8 us (1.015)
  the two profiles are of different devices: /device:TPU:72 before, /device:TPU:62 now
where the time goes in v7:
time: 69.8 us; the launch traced here: 69.4 us
  blocking collectives  28.3 us (41%)
  starting transfers between devices  17.9 us (26%)
  Pallas kernels  12.9 us (18%)
  waiting for transfers between devices  9.6 us (14%)
    all_to_all x1, starting transfers between devices, local(): lax.all_to_all(packed.reshape(32, CAP, WIDE), ('ta', 'ha'), 0, 0, axis_in...  13.4 us
    pallas_call x7, Pallas kernels, pinned(): run(*(pltpu.with_memory_space_constraint(a, pltpu.HBM) if m is pltpu.HBM...  12.9 us
    all_gather x1, blocking collectives, local(): acts = lax.all_gather(act, 'ha', axis=0, tiled=False)  12.7 us
    all_to_all x1, blocking collectives, local(): parts = lax.all_to_all(out, 'ha', 0, 0, tiled=True)  11.1 us
    all_to_all x1, waiting for transfers between devices, local(): lax.all_to_all(packed.reshape(32, CAP, WIDE), ('ta', 'ha'), 0, 0, axis_in...  9.59 us
    ppermute x1, starting transfers between devices, local(): earlier = lax.ppermute(tail, 'ta', [(i, i + 1) for i in range(n_ta - 1)])  4.48 us
    all_gather x1, blocking collectives, local(): lax.all_gather(arrived, 'ha', axis=0, axis_index_groups=chips, tiled=True)  2.37 us
    all_gather x1, blocking collectives, local(): lax.all_gather(earlier, 'ha', axis=0, axis_index_groups=chips, tiled=True)  2.08 us
  transfers between devices with their start and end apart: 2, of which 1 were waited for; matrix products, arithmetic and copies ran while one was open for 0% of the time, Pallas kernels for 10%

profile of v7, /device:TPU:62, one launch (start us, length us, event | category | flops | bytes accessed | tf_op | source)
XLA Modules:
  0.0 69.4 jit_solution(6527540185743824313)
XLA Ops:
  0.0 2.0 %shard_map.110 = bf16[256,768]{1,0:T(8,128)(2,1)} custom-call(s32[32,128]{1,0:T(8,128)} %bitcast.10, bf16[64,768]{1,0:T(8,128)(2,1)} %rows_hbm.1), custom_call_target="tpu_custom_call" | custom-call | flops 10000000 | bytes 1048576 | tf_op jit(solution)/shard_map/pallas_call | solution.py:319
  2.0 13.4 %all-to-all-start = ((bf16[32,8,768]{2,1,0:T(8,128)(2,1)}), bf16[32,8,768]{2,1,0:T(8,128)(2,1)S(1)}, u32[]{:S(2)}, u32[]{:S(2)}) async-start(bf16[32,8,768]{2,1,0:T(8,128)(2,1)} %bitcast.2), calls=%async_computation | async-start | bytes 786432 | tf_op jit(solution)/shard_map/all_to_all | solution.py:352
  15.4 0.0 copy-start.1
  15.4 0.6 copy-done.1
  16.1 0.0 copy-start
  16.1 4.0 %shard_map.109 = (bf16[256,512]{1,0:T(8,128)(2,1)S(1)}, bf16[64,256]{1,0:T(8,128)(2,1)S(1)}, bf16[288,2]{1,0:T(8,128)(2,1)S(1)}, f32[2,384]{1,0:T(2,128)S(1)}, f...) custom-call(s32[6]{0:T(128)S(1)} %copy-done.1, ...), custom_call_target="tpu_custom_call" | custom-call | flops 2000000000 | bytes 1048576 | tf_op jit(solution)/shard_map/pallas_call | solution.py:319
  20.1 9.6 %all-to-all-done = bf16[32,8,768]{2,1,0:T(8,128)(2,1)S(1)} async-done(((bf16[32,8,768]{2,1,0:T(8,128)(2,1)}), bf16[32,8,768]{2,1,0:T(8,128)(2,1)S(1)}, u32[]{:S(2)}, u32[]{:S(2)}) %all-to-all-start) | async-done | bytes 393248 | tf_op jit(solution)/shard_map/all_to_all | solution.py:352
  29.7 0.2 shard_map.111
  29.9 4.5 %collective-permute-start = (bf16[64,768]{1,0:T(8,128)(2,1)S(1)}, bf16[64,768]{1,0:T(8,128)(2,1)S(1)}, u32[]{:S(2)}, u32[]{:S(2)}) collective-permute-start(bf16[64,768]{1,0:T(8,128)(2,1)S(1)} %shard_map.111), channel_id=1, source_target_pairs={{0,4},{4,8},{8,12},{12,16},{16,20},{20,24},{24,28},{28,32},{32,36}... | collective-permute-start | bytes 294920 | tf_op jit(solution)/shard_map/ppermute | solution.py:385
  34.4 2.4 %all_gather.13.packed_ref = bf16[512,768]{1,0:T(8,128)(2,1)S(1)} all-gather(bf16[256,768]{1,0:T(8,128)(2,1)S(1)} %bitcast.7), channel_id=1, replica_groups={{0,1},{2,3},{4,5},{6,7},{8,9},{10,11},{12,13},{14,15},{16,17},{18,19},{..., dimensions={0}, use_global_device_ids=true | all-gather | bytes 1179648 | tf_op jit(solution)/shard_map/all_gather | solution.py:386
  36.7 0.0 copy-done
  36.7 2.7 %shard_map.112 = (bf16[336,128]{1,0:T(8,128)(2,1)S(1)}, bf16[256,192]{1,0:T(8,128)(2,1)S(1)}, bf16[3,32,768]{2,1,0:T(8,128)(2,1)S(1)}, bf16[9,192,768]{2,1,0:T(8,128)(2,1)S(1)}) custom-call(bf16[288,2]{1,0:T(8,128)(2,1)S(1)} %get-tuple-element.20.keep_ref, bf16[256,512]{1,0:T(8,128)(2,1)S(1)} %get-tuple-element.23.table_ref, ...), custom_call_target="tpu_custom_call" | custom-call | flops 1000000 | bytes 1048576 | tf_op jit(solution)/shard_map/pallas_call | solution.py:319
  39.4 0.0 copy-start.2
  39.4 0.0 collective-permute-done
  39.4 2.1 %all_gather.12.earlier_ref = bf16[128,768]{1,0:T(8,128)(2,1)S(1)} all-gather(bf16[64,768]{1,0:T(8,128)(2,1)S(1)} %collective-permute-done), channel_id=1, replica_groups={{0,1},{2,3},{4,5},{6,7},{8,9},{10,11},{12,13},{14,15},{16,17},{18,19},{..., dimensions={0}, use_global_device_ids=true | all-gather | bytes 294912 | tf_op jit(solution)/shard_map/all_gather | solution.py:399
  41.5 1.6 %shard_map.113 = bf16[432,128]{1,0:T(8,128)(2,1)S(1)} custom-call(bf16[288,2]{1,0:T(8,128)(2,1)S(1)} %get-tuple-element.20.keep_ref, bf16[128,768]{1,0:T(8,128)(2,1)S(1)} %all_gather.12.earlier_ref, bf16[3,32,768]{2,1,0:T(8,128)(2,1)S(1)} %get-tuple-element.30.head_ref, f32[2,384]{1,0:T(2,128)S(1)} %get-tuple-element.25.wide_ref, ...), custom_call_target="tpu_custom_call" | custom-call | flops 1000000000 | bytes 1048576 | tf_op jit(solution)/shard_map/pallas_call | solution.py:319
  43.1 12.7 %all-gather = bf16[1728,128]{1,0:T(8,128)(2,1)S(1)} all-gather(bf16[432,128]{1,0:T(8,128)(2,1)S(1)} %shard_map.113), channel_id=2, replica_groups=mesh['dp'=8,'ta'=16,'ha'=4] {'ha'}, dimensions={0}, use_global_device_ids=true | all-gather | bytes 552960 | tf_op jit(solution)/shard_map/all_gather | solution.py:403
  55.8 0.0 copy-done.2
  55.8 1.6 %shard_map.114 = bf16[4,96,128]{2,1,0:T(8,128)(2,1)S(1)} custom-call(bf16[288,2]{1,0:T(8,128)(2,1)S(1)} %get-tuple-element.20.keep_ref, bf16[4,432,128]{2,1,0:T(8,128)(2,1)S(1)} %bitcast.9, bf16[256,192]{1,0:T(8,128)(2,1)S(1)} %get-tuple-element.33.rest_ref, f32[4,192]{1,0:T(4,128)S(1)} %get-tuple-element.26.own_ref, bf16[9,192,768]{2,1,0:T(8,128)(2,1)S(1)} %copy-done.2), custom_call_target="tpu_custom_call" | custom-call | flops 2000000000 | bytes 1048576 | tf_op jit(solution)/shard_map/pallas_call | solution.py:319
  57.4 11.1 %all_to_all.10.parts_ref = bf16[4,96,128]{2,1,0:T(8,128)(2,1)S(1)} all-to-all(bf16[4,96,128]{2,1,0:T(8,128)(2,1)S(1)} %shard_map.114), channel_id=1, replica_groups=mesh['dp'=8,'ta'=16,'ha'=4] {'ha'}, dimensions={0} | all-to-all | bytes 196608 | tf_op jit(solution)/shard_map/all_to_all | solution.py:411
  68.5 0.9 %shard_map.115 = bf16[16,4,2,384]{3,2,1,0:T(2,128)(2,1)} custom-call(bf16[4,96,128]{2,1,0:T(8,128)(2,1)S(1)} %all_to_all.10.parts_ref), custom_call_target="tpu_custom_call" | custom-call | bytes 1048576 | tf_op jit(solution)/shard_map/pallas_call | solution.py:319
Async XLA Ops:
  2.0 27.7 %all-to-all-start = ((bf16[32,8,768]{2,1,0:T(8,128)(2,1)}), bf16[32,8,768]{2,1,0:T(8,128)(2,1)S(1)}, u32[]{:S(2)}, u32[]{:S(2)}) async-start(bf16[32,8,768]{2,1,0:T(8,128)(2,1)} %bitcast.2), calls=%async_computation | async-start | bytes 786432 | tf_op jit(solution)/shard_map/all_to_all | solution.py:352
  15.4 0.7 copy-start.1
  16.1 20.7 %copy-start = (bf16[3,3,3,96,384]{4,3,2,1,0:T(8,128)(2,1)S(1)}, bf16[3,3,3,96,384]{4,3,2,1,0:T(8,128)(2,1)}, u32[]{:S(2)}) copy-start(bf16[3,3,3,96,384]{4,3,2,1,0:T(8,128)(2,1)} %param.16) | copy-start | bytes 5971972
  29.9 9.6 %collective-permute-start = (bf16[64,768]{1,0:T(8,128)(2,1)S(1)}, bf16[64,768]{1,0:T(8,128)(2,1)S(1)}, u32[]{:S(2)}, u32[]{:S(2)}) collective-permute-start(bf16[64,768]{1,0:T(8,128)(2,1)S(1)} %shard_map.111), channel_id=1, source_target_pairs={{0,4},{4,8},{8,12},{12,16},{16,20},{20,24},{24,28},{28,32},{32,36}... | collective-permute-start | bytes 294920 | tf_op jit(solution)/shard_map/ppermute | solution.py:385
  39.4 16.4 %copy-start.2 = (bf16[9,192,768]{2,1,0:T(8,128)(2,1)S(1)}, bf16[9,192,768]{2,1,0:T(8,128)(2,1)}, u32[]{:S(2)}) copy-start(bf16[9,192,768]{2,1,0:T(8,128)(2,1)} %get-tuple-element.34.weight_ref) | copy-start | bytes 7962628

commit v8 on v5

--- a/solution.py
+++ b/solution.py
@@ -156,7 +156,7 @@
 def moments(total, total_squares):
     entries = ROWS * 2 * GROUP
     mean = total / entries
-    return mean, lax.rsqrt(total_squares / entries - mean * mean + 1e-06)
+    return mean, lax.rsqrt(jnp.maximum(total_squares / entries - mean * mean, 0.0) + 1e-06)
 
 
 def wide_stats(values, same):

time: 68.8 us -> 68.8 us (level)
  no operation moved by 1% of the time
where the time goes in v8:
time: 68.8 us; the launch traced here: 68.4 us
  blocking collectives  25.3 us (37%)
  starting transfers between devices  15.1 us (22%)
  waiting for transfers between devices  14.3 us (21%)
  Pallas kernels  13 us (19%)
    pallas_call x7, Pallas kernels, pinned(): run(*(pltpu.with_memory_space_constraint(a, pltpu.HBM) if m is pltpu.HBM...  13 us
    all_to_all x1, starting transfers between devices, local(): lax.all_to_all(packed.reshape(32, CAP, WIDE), ('ta', 'ha'), 0, 0, axis_in...  12.6 us
    all_gather x1, blocking collectives, local(): acts = lax.all_gather(act, 'ha', axis=0, tiled=False)  11.6 us
    all_to_all x1, blocking collectives, local(): parts = lax.all_to_all(out, 'ha', 0, 0, tiled=True)  11.4 us
    all_to_all x1, waiting for transfers between devices, local(): lax.all_to_all(packed.reshape(32, CAP, WIDE), ('ta', 'ha'), 0, 0, axis_in...  10.7 us
    ppermute x1, waiting for transfers between devices, local(): earlier = lax.ppermute(tail, 'ta', [(i, i + 1) for i in range(n_ta - 1)])  3.63 us
    ppermute x1, starting transfers between devices, local(): earlier = lax.ppermute(tail, 'ta', [(i, i + 1) for i in range(n_ta - 1)])  2.5 us
    all_gather x1, blocking collectives, local(): lax.all_gather(arrived, 'ha', axis=0, axis_index_groups=chips, tiled=True)  2.36 us
  transfers between devices with their start and end apart: 2, of which 2 were waited for; matrix products, arithmetic and copies ran while one was open for 0% of the time, Pallas kernels for 10%

profile of v8, /device:TPU:72, one launch (start us, length us, event | category | flops | bytes accessed | tf_op | source)
XLA Modules:
  0.0 68.4 jit_solution(15475526932542380634)
XLA Ops:
  0.0 2.0 %shard_map.110 = bf16[256,768]{1,0:T(8,128)(2,1)} custom-call(s32[32,128]{1,0:T(8,128)} %bitcast.9, bf16[64,768]{1,0:T(8,128)(2,1)} %rows_hbm.1), custom_call_target="tpu_custom_call" | custom-call | flops 10000000 | bytes 1048576 | tf_op jit(solution)/shard_map/pallas_call | solution.py:316
  2.0 12.6 %all-to-all-start = ((bf16[32,8,768]{2,1,0:T(8,128)(2,1)}), bf16[32,8,768]{2,1,0:T(8,128)(2,1)S(1)}, u32[]{:S(2)}, u32[]{:S(2)}) async-start(bf16[32,8,768]{2,1,0:T(8,128)(2,1)} %bitcast.2), calls=%async_computation | async-start | bytes 786432 | tf_op jit(solution)/shard_map/all_to_all | solution.py:349
  14.6 0.0 copy-start.1
  14.6 0.6 copy-done.1
  15.2 0.0 copy-start
  15.2 4.0 %shard_map.109 = (bf16[256,512]{1,0:T(8,128)(2,1)S(1)}, bf16[288,2]{1,0:T(8,128)(2,1)S(1)}, f32[2,384]{1,0:T(2,128)S(1)}, f32[4,192]{1,0:T(4,128)S(1)}, bf16[384...) custom-call(s32[6]{0:T(128)S(1)} %copy-done.1, ...), custom_call_target="tpu_custom_call" | custom-call | flops 2000000000 | bytes 1048576 | tf_op jit(solution)/shard_map/pallas_call | solution.py:316
  19.2 10.7 %all-to-all-done = bf16[32,8,768]{2,1,0:T(8,128)(2,1)S(1)} async-done(((bf16[32,8,768]{2,1,0:T(8,128)(2,1)}), bf16[32,8,768]{2,1,0:T(8,128)(2,1)S(1)}, u32[]{:S(2)}, u32[]{:S(2)}) %all-to-all-start) | async-done | bytes 393248 | tf_op jit(solution)/shard_map/all_to_all | solution.py:349
  30.0 2.4 %all_gather.9.packed_ref = bf16[512,768]{1,0:T(8,128)(2,1)S(1)} all-gather(bf16[256,768]{1,0:T(8,128)(2,1)S(1)} %bitcast.8), channel_id=1, replica_groups={{0,1},{2,3},{4,5},{6,7},{8,9},{10,11},{12,13},{14,15},{16,17},{18,19},{..., dimensions={0}, use_global_device_ids=true | all-gather | bytes 1179648 | tf_op jit(solution)/shard_map/all_gather | solution.py:379
  32.3 0.3 shard_map.111
  32.6 2.5 %collective-permute-start = (bf16[64,768]{1,0:T(8,128)(2,1)S(1)}, bf16[64,768]{1,0:T(8,128)(2,1)S(1)}, u32[]{:S(2)}, u32[]{:S(2)}) collective-permute-start(bf16[64,768]{1,0:T(8,128)(2,1)S(1)} %shard_map.111), channel_id=1, source_target_pairs={{0,4},{4,8},{8,12},{12,16},{16,20},{20,24},{24,28},{28,32},{32,36}... | collective-permute-start | bytes 294920 | tf_op jit(solution)/shard_map/ppermute | solution.py:381
  35.1 0.0 copy-done
  35.1 2.7 %shard_map.112 = (bf16[336,128]{1,0:T(8,128)(2,1)S(1)}, bf16[256,192]{1,0:T(8,128)(2,1)S(1)}, bf16[3,32,768]{2,1,0:T(8,128)(2,1)S(1)}, bf16[9,192,768]{2,1,0:T(8,128)(2,1)S(1)}) custom-call(bf16[288,2]{1,0:T(8,128)(2,1)S(1)} %get-tuple-element.17.keep_ref, bf16[256,512]{1,0:T(8,128)(2,1)S(1)} %get-tuple-element.18.table_ref, ...), custom_call_target="tpu_custom_call" | custom-call | flops 2000000000 | bytes 1048576 | tf_op jit(solution)/shard_map/pallas_call | solution.py:316
  37.8 0.0 copy-start.2
  37.8 3.6 %collective-permute-done.earlier_ref = bf16[64,768]{1,0:T(8,128)(2,1)S(1)} collective-permute-done((bf16[64,768]{1,0:T(8,128)(2,1)S(1)}, bf16[64,768]{1,0:T(8,128)(2,1)S(1)}, u32[]{:S(2)}, u32[]{:S(2)}) %collective-permute-start) | collective-permute-done | bytes 98336 | tf_op jit(solution)/shard_map/ppermute | solution.py:381
  41.4 1.6 %shard_map.113 = bf16[432,128]{1,0:T(8,128)(2,1)S(1)} custom-call(bf16[288,2]{1,0:T(8,128)(2,1)S(1)} %get-tuple-element.17.keep_ref, bf16[64,768]{1,0:T(8,128)(2,1)S(1)} %collective-permute-done.earlier_ref, bf16[3,32,768]{2,1,0:T(8,128)(2,1)S(1)} %get-tuple-element.24.head_ref, f32[2,384]{1,0:T(2,128)S(1)} %get-tuple-element.19.wide_ref, ...), custom_call_target="tpu_custom_call" | custom-call | flops 1000000000 | bytes 1048576 | tf_op jit(solution)/shard_map/pallas_call | solution.py:316
  43.0 11.6 %all-gather = bf16[1728,128]{1,0:T(8,128)(2,1)S(1)} all-gather(bf16[432,128]{1,0:T(8,128)(2,1)S(1)} %shard_map.113), channel_id=2, replica_groups=mesh['dp'=8,'ta'=16,'ha'=4] {'ha'}, dimensions={0}, use_global_device_ids=true | all-gather | bytes 552960 | tf_op jit(solution)/shard_map/all_gather | solution.py:397
  54.5 0.0 copy-done.2
  54.5 1.6 %shard_map.114 = bf16[4,96,128]{2,1,0:T(8,128)(2,1)S(1)} custom-call(bf16[288,2]{1,0:T(8,128)(2,1)S(1)} %get-tuple-element.17.keep_ref, bf16[4,432,128]{2,1,0:T(8,128)(2,1)S(1)} %bitcast.6, bf16[256,192]{1,0:T(8,128)(2,1)S(1)} %get-tuple-element.27.rest_ref, f32[4,192]{1,0:T(4,128)S(1)} %get-tuple-element.20.own_ref, bf16[9,192,768]{2,1,0:T(8,128)(2,1)S(1)} %copy-done.2), custom_call_target="tpu_custom_call" | custom-call | flops 2000000000 | bytes 1048576 | tf_op jit(solution)/shard_map/pallas_call | solution.py:316
  56.1 11.4 %all_to_all.10.parts_ref = bf16[4,96,128]{2,1,0:T(8,128)(2,1)S(1)} all-to-all(bf16[4,96,128]{2,1,0:T(8,128)(2,1)S(1)} %shard_map.114), channel_id=1, replica_groups=mesh['dp'=8,'ta'=16,'ha'=4] {'ha'}, dimensions={0} | all-to-all | bytes 196608 | tf_op jit(solution)/shard_map/all_to_all | solution.py:405
  67.5 0.9 %shard_map.115 = bf16[16,4,2,384]{3,2,1,0:T(2,128)(2,1)} custom-call(bf16[4,96,128]{2,1,0:T(8,128)(2,1)S(1)} %all_to_all.10.parts_ref), custom_call_target="tpu_custom_call" | custom-call | bytes 1048576 | tf_op jit(solution)/shard_map/pallas_call | solution.py:316
Async XLA Ops:
  2.0 28.0 %all-to-all-start = ((bf16[32,8,768]{2,1,0:T(8,128)(2,1)}), bf16[32,8,768]{2,1,0:T(8,128)(2,1)S(1)}, u32[]{:S(2)}, u32[]{:S(2)}) async-start(bf16[32,8,768]{2,1,0:T(8,128)(2,1)} %bitcast.2), calls=%async_computation | async-start | bytes 786432 | tf_op jit(solution)/shard_map/all_to_all | solution.py:349
  14.6 0.7 copy-start.1
  15.2 19.9 %copy-start = (bf16[3,3,3,96,384]{4,3,2,1,0:T(8,128)(2,1)S(1)}, bf16[3,3,3,96,384]{4,3,2,1,0:T(8,128)(2,1)}, u32[]{:S(2)}) copy-start(bf16[3,3,3,96,384]{4,3,2,1,0:T(8,128)(2,1)} %param.16) | copy-start | bytes 5971972
  32.6 8.8 %collective-permute-start = (bf16[64,768]{1,0:T(8,128)(2,1)S(1)}, bf16[64,768]{1,0:T(8,128)(2,1)S(1)}, u32[]{:S(2)}, u32[]{:S(2)}) collective-permute-start(bf16[64,768]{1,0:T(8,128)(2,1)S(1)} %shard_map.111), channel_id=1, source_target_pairs={{0,4},{4,8},{8,12},{12,16},{16,20},{20,24},{24,28},{28,32},{32,36}... | collective-permute-start | bytes 294920 | tf_op jit(solution)/shard_map/ppermute | solution.py:381
  37.8 16.8 %copy-start.2 = (bf16[9,192,768]{2,1,0:T(8,128)(2,1)S(1)}, bf16[9,192,768]{2,1,0:T(8,128)(2,1)}, u32[]{:S(2)}) copy-start(bf16[9,192,768]{2,1,0:T(8,128)(2,1)} %get-tuple-element.28.weight_ref) | copy-start | bytes 7962628

commit v9 on v8

--- a/solution.py
+++ b/solution.py
@@ -89,12 +89,12 @@
 
 
 def prepare_kernel(
-    count_ref, plan_hbm, gain_hbm, bias_hbm, b1_hbm, g2_hbm, n2_hbm, b2_hbm, w2_hbm,
-    table_ref, keep_ref, wide_ref, own_ref, same_wide_ref, same_own_ref, select_ref, second_ref,
-    plan_ref, gain_ref, bias_ref, b1_ref, g2_ref, n2_ref, b2_ref, w2_ref, sems,
+    count_ref, plan_hbm, gain_hbm, bias_hbm, b1_hbm, g2_hbm, n2_hbm, b2_hbm, w1_hbm, w2_hbm,
+    table_ref, keep_ref, wide_ref, own_ref, same_wide_ref, same_own_ref, select_ref, first_ref, second_ref,
+    plan_ref, gain_ref, bias_ref, b1_ref, g2_ref, n2_ref, b2_ref, w1_ref, w2_ref, sems,
 ):
     pairs = (
-        (plan_hbm, plan_ref), (w2_hbm, w2_ref), (gain_hbm, gain_ref), (bias_hbm, bias_ref),
+        (plan_hbm, plan_ref), (w1_hbm, w1_ref), (w2_hbm, w2_ref), (gain_hbm, gain_ref), (bias_hbm, bias_ref),
         (b1_hbm, b1_ref), (g2_hbm, g2_ref), (n2_hbm, n2_ref), (b2_hbm, b2_ref),
     )
     copies = [pltpu.make_async_copy(source, to, sems.at[k]) for k, (source, to) in enumerate(pairs)]
@@ -128,7 +128,7 @@
     want = (q + 1).astype(F32)
     table_ref[:, 0:256] = (held[0:1] == want).astype(BF16)
     table_ref[:, 256:512] = (held[1:2] == want).astype(BF16)
-    for copy in copies[2:]:
+    for copy in copies[3:]:
         copy.wait()
     wide_ref[0:1] = gain_ref[...].reshape(1, CH)
     wide_ref[1:2] = bias_ref[...].reshape(1, CH)
@@ -139,6 +139,8 @@
             part = jnp.where(ha == h, value[:, h * OWN : (h + 1) * OWN], part)
         own_ref[k : k + 1] = jnp.concatenate([part, part], axis=1)
     copies[1].wait()
+    side_by_side(w1_ref, first_ref)
+    copies[2].wait()
     side_by_side(w2_ref, second_ref)
 
 
@@ -236,12 +238,14 @@
 
 
 def main_kernel(
-    keep_ref, table_ref, packed_ref, wide_ref, own_ref, same_wide_ref, same_own_ref, select_ref, raw_ref,
-    act_ref, rest_ref, head_ref, weight_ref, rows_ref, taps_ref,
+    keep_ref, table_ref, packed_ref, wide_ref, own_ref, same_wide_ref, same_own_ref, select_hbm, weight_ref,
+    act_ref, rest_ref, head_ref, rows_ref, taps_ref, select_ref, sem,
 ):
+    copy = pltpu.make_async_copy(select_hbm, select_ref, sem)
+    copy.start()
     rows_ref[...] = dot(table_ref[...], packed_ref[...]).astype(BF16)
-    side_by_side(raw_ref, weight_ref)
     norm_first(rows_ref, wide_ref, same_wide_ref[...], taps_ref)
+    copy.wait()
     rest_ref[...] = dot_nt(rows_ref[...], select_ref[...]).astype(BF16)
     for b in range(3):
         head_ref[b] = taps_ref[b, 0:32, :]
@@ -350,7 +354,7 @@
         packed.reshape(32, CAP, WIDE), ("ta", "ha"), 0, 0, axis_index_groups=same_core, tiled=True
     ).reshape(256, WIDE)
     weight, raw = (9, PAIR, WIDE), (9, 3 * OWN, CH)
-    table, keep, wide, own, same_wide, same_own, select, second = call(
+    table, keep, wide, own, same_wide, same_own, select, first, second = call(
         prepare_kernel,
         [
             vmem((BLOCK, 512), BF16),
@@ -359,11 +363,12 @@
             vmem((4, PAIR), F32),
             vmem((CH, CH), BF16),
             vmem((PAIR, PAIR), BF16),
-            vmem((PAIR, WIDE), BF16),
+            hbm((PAIR, WIDE), BF16),
+            vmem(weight, BF16),
             hbm(weight, BF16),
         ],
-        [smem] + [hbm] * 8,
-        [vmem((32, 128), I32)] + [vmem((CH,), F32)] * 6 + [vmem(raw, BF16), pltpu.SemaphoreType.DMA((8,))],
+        [smem] + [hbm] * 9,
+        [vmem((32, 128), I32)] + [vmem((CH,), F32)] * 6 + [vmem(raw, BF16)] * 2 + [pltpu.SemaphoreType.DMA((9,))],
         flops=2 * 10**9,
     )(
         latent_frame_count,
@@ -374,26 +379,26 @@
         second_norm_gain,
         second_norm_bias,
         second_convolution_bias,
+        first_convolution_weight.reshape(raw),
         second_convolution_weight.reshape(raw),
     )
     both = lax.all_gather(arrived, "ha", axis=0, axis_index_groups=chips, tiled=True)
     [tail] = call(tail_kernel, [((EDGE, WIDE), BF16)], [vmem] * 2, flops=10**8)(table, both)
     earlier = lax.ppermute(tail, "ta", [(i, i + 1) for i in range(n_ta - 1)])
-    act, rest, head, near = call(
+    act, rest, head = call(
         main_kernel,
         [
             vmem((FOLDED - CUT, 128), BF16),
             vmem((BLOCK, PAIR), BF16),
             vmem((3, 32, WIDE), BF16),
-            vmem(weight, BF16),
         ],
-        [vmem] * 9,
-        [vmem((BLOCK, WIDE), BF16), vmem((3, BLOCK, WIDE), BF16)],
+        [vmem] * 7 + [hbm, vmem],
+        [vmem((BLOCK, WIDE), BF16), vmem((3, BLOCK, WIDE), BF16), vmem((PAIR, WIDE), BF16), pltpu.SemaphoreType.DMA],
         flops=2 * 10**9,
-    )(keep, table, both, wide, own, same_wide, same_own, select, first_convolution_weight.reshape(raw))
+    )(keep, table, both, wide, own, same_wide, same_own, select, first)
     [act] = call(
         halo_kernel, [((FOLDED, 128), BF16)], [vmem] * 9, [vmem((3, EDGE + 32, WIDE), BF16)], flops=10**9
-    )(keep, earlier, head, wide, own, same_wide, same_own, near, act)
+    )(keep, earlier, head, wide, own, same_wide, same_own, first, act)
     acts = lax.all_gather(act, "ha", axis=0, tiled=False)
     [out] = call(
         last_kernel,

time: 68.8 us -> 69.2 us (level)
  the two profiles are of different devices: /device:TPU:72 before, /device:TPU:80 now
where the time goes in v9:
time: 69.2 us; the launch traced here: 68.7 us
  blocking collectives  25.5 us (37%)
  starting transfers between devices  15.2 us (22%)
  Pallas kernels  14.5 us (21%)
  waiting for transfers between devices  12.9 us (19%)
    pallas_call x7, Pallas kernels, pinned(): run(*(pltpu.with_memory_space_constraint(a, pltpu.HBM) if m is pltpu.HBM...  14.5 us
    all_to_all x1, starting transfers between devices, local(): lax.all_to_all(packed.reshape(32, CAP, WIDE), ('ta', 'ha'), 0, 0, axis_in...  12.6 us
    all_gather x1, blocking collectives, local(): acts = lax.all_gather(act, 'ha', axis=0, tiled=False)  11.6 us
    all_to_all x1, blocking collectives, local(): parts = lax.all_to_all(out, 'ha', 0, 0, tiled=True)  11.4 us
    all_to_all x1, waiting for transfers between devices, local(): lax.all_to_all(packed.reshape(32, CAP, WIDE), ('ta', 'ha'), 0, 0, axis_in...  9.98 us
    ppermute x1, waiting for transfers between devices, local(): earlier = lax.ppermute(tail, 'ta', [(i, i + 1) for i in range(n_ta - 1)])  2.91 us
    all_gather x1, blocking collectives, local(): lax.all_gather(arrived, 'ha', axis=0, axis_index_groups=chips, tiled=True)  2.57 us
    ppermute x1, starting transfers between devices, local(): earlier = lax.ppermute(tail, 'ta', [(i, i + 1) for i in range(n_ta - 1)])  2.51 us
  transfers between devices with their start and end apart: 2, of which 2 were waited for; matrix products, arithmetic and copies ran while one was open for 0% of the time, Pallas kernels for 12%

profile of v9, /device:TPU:80, one launch (start us, length us, event | category | flops | bytes accessed | tf_op | source)
XLA Modules:
  0.0 68.7 jit_solution(8117387582985992749)
XLA Ops:
  0.0 1.9 %shard_map.110 = bf16[256,768]{1,0:T(8,128)(2,1)} custom-call(s32[32,128]{1,0:T(8,128)} %bitcast.7, bf16[64,768]{1,0:T(8,128)(2,1)} %rows_hbm.1), custom_call_target="tpu_custom_call" | custom-call | flops 10000000 | bytes 1048576 | tf_op jit(solution)/shard_map/pallas_call | solution.py:320
  2.0 12.6 %all-to-all-start = ((bf16[32,8,768]{2,1,0:T(8,128)(2,1)}), bf16[32,8,768]{2,1,0:T(8,128)(2,1)}, u32[]{:S(2)}, u32[]{:S(2)}) async-start(bf16[32,8,768]{2,1,0:T(8,128)(2,1)} %bitcast.3), calls=%async_computation | async-start | bytes 786432 | tf_op jit(solution)/shard_map/all_to_all | solution.py:353
  14.6 0.0 copy-start
  14.6 0.6 copy-done
  15.3 4.8 %shard_map.109 = (bf16[256,512]{1,0:T(8,128)(2,1)S(1)}, bf16[288,2]{1,0:T(8,128)(2,1)S(1)}, f32[2,384]{1,0:T(2,128)S(1)}, f32[4,192]{1,0:T(4,128)S(1)}, bf16[384...) custom-call(s32[6]{0:T(128)S(1)} %copy-done, ...), custom_call_target="tpu_custom_call" | custom-call | flops 2000000000 | bytes 1048576 | tf_op jit(solution)/shard_map/pallas_call | solution.py:320
  20.1 10.0 %all-to-all-done = bf16[32,8,768]{2,1,0:T(8,128)(2,1)} async-done(((bf16[32,8,768]{2,1,0:T(8,128)(2,1)}), bf16[32,8,768]{2,1,0:T(8,128)(2,1)}, u32[]{:S(2)}, u32[]{:S(2)}) %all-to-all-start) | async-done | bytes 393248 | tf_op jit(solution)/shard_map/all_to_all | solution.py:353
  30.1 2.6 %all_gather.9.packed_ref = bf16[512,768]{1,0:T(8,128)(2,1)S(1)} all-gather(bf16[256,768]{1,0:T(8,128)(2,1)} %bitcast.4), channel_id=1, replica_groups={{0,1},{2,3},{4,5},{6,7},{8,9},{10,11},{12,13},{14,15},{16,17},{18,19},{..., dimensions={0}, use_global_device_ids=true | all-gather | bytes 1179648 | tf_op jit(solution)/shard_map/all_gather | solution.py:385
  32.6 0.3 shard_map.111
  32.9 2.5 %collective-permute-start = (bf16[64,768]{1,0:T(8,128)(2,1)S(1)}, bf16[64,768]{1,0:T(8,128)(2,1)S(1)}, u32[]{:S(2)}, u32[]{:S(2)}) collective-permute-start(bf16[64,768]{1,0:T(8,128)(2,1)S(1)} %shard_map.111), channel_id=1, source_target_pairs={{0,4},{4,8},{8,12},{12,16},{16,20},{20,24},{24,28},{28,32},{32,36}... | collective-permute-start | bytes 294920 | tf_op jit(solution)/shard_map/ppermute | solution.py:387
  35.4 3.4 %shard_map.112 = (bf16[336,128]{1,0:T(8,128)(2,1)S(1)}, bf16[256,192]{1,0:T(8,128)(2,1)S(1)}, bf16[3,32,768]{2,1,0:T(8,128)(2,1)S(1)}) custom-call(bf16[288,2]{1,0:T(8,128)(2,1)S(1)} %get-tuple-element.17.keep_ref, bf16[256,512]{1,0:T(8,128)(2,1)S(1)} %get-tuple-element.18.table_ref, bf16[512,768]{1,0:T(8,128)(2,1)S(1)} %all_gather.9.packed_ref, ...), custom_call_target="tpu_custom_call" | custom-call | flops 2000000000 | bytes 1048576 | tf_op jit(solution)/shard_map/pallas_call | solution.py:320
  38.8 0.0 copy-start.1
  38.8 2.9 %collective-permute-done.earlier_ref = bf16[64,768]{1,0:T(8,128)(2,1)S(1)} collective-permute-done((bf16[64,768]{1,0:T(8,128)(2,1)S(1)}, bf16[64,768]{1,0:T(8,128)(2,1)S(1)}, u32[]{:S(2)}, u32[]{:S(2)}) %collective-permute-start) | collective-permute-done | bytes 98336 | tf_op jit(solution)/shard_map/ppermute | solution.py:387
  41.7 1.6 %shard_map.113 = bf16[432,128]{1,0:T(8,128)(2,1)S(1)} custom-call(bf16[288,2]{1,0:T(8,128)(2,1)S(1)} %get-tuple-element.17.keep_ref, bf16[64,768]{1,0:T(8,128)(2,1)S(1)} %collective-permute-done.earlier_ref, bf16[3,32,768]{2,1,0:T(8,128)(2,1)S(1)} %get-tuple-element.25.head_ref, f32[2,384]{1,0:T(2,128)S(1)} %get-tuple-element.19.wide_ref, ...), custom_call_target="tpu_custom_call" | custom-call | flops 1000000000 | bytes 1048576 | tf_op jit(solution)/shard_map/pallas_call | solution.py:320
  43.3 11.6 %all-gather = bf16[1728,128]{1,0:T(8,128)(2,1)S(1)} all-gather(bf16[432,128]{1,0:T(8,128)(2,1)S(1)} %shard_map.113), channel_id=2, replica_groups=mesh['dp'=8,'ta'=16,'ha'=4] {'ha'}, dimensions={0}, use_global_device_ids=true | all-gather | bytes 552960 | tf_op jit(solution)/shard_map/all_gather | solution.py:402
  54.9 0.0 copy-done.1
  54.9 1.6 %shard_map.114 = bf16[4,96,128]{2,1,0:T(8,128)(2,1)S(1)} custom-call(bf16[288,2]{1,0:T(8,128)(2,1)S(1)} %get-tuple-element.17.keep_ref, bf16[4,432,128]{2,1,0:T(8,128)(2,1)S(1)} %bitcast.6, bf16[256,192]{1,0:T(8,128)(2,1)S(1)} %get-tuple-element.27.rest_ref, f32[4,192]{1,0:T(4,128)S(1)} %get-tuple-element.20.own_ref, bf16[9,192,768]{2,1,0:T(8,128)(2,1)S(1)} %copy-done.1), custom_call_target="tpu_custom_call" | custom-call | flops 2000000000 | bytes 1048576 | tf_op jit(solution)/shard_map/pallas_call | solution.py:320
  56.5 11.4 %all_to_all.10.parts_ref = bf16[4,96,128]{2,1,0:T(8,128)(2,1)S(1)} all-to-all(bf16[4,96,128]{2,1,0:T(8,128)(2,1)S(1)} %shard_map.114), channel_id=1, replica_groups=mesh['dp'=8,'ta'=16,'ha'=4] {'ha'}, dimensions={0} | all-to-all | bytes 196608 | tf_op jit(solution)/shard_map/all_to_all | solution.py:410
  67.8 0.9 %shard_map.115 = bf16[16,4,2,384]{3,2,1,0:T(2,128)(2,1)} custom-call(bf16[4,96,128]{2,1,0:T(8,128)(2,1)S(1)} %all_to_all.10.parts_ref), custom_call_target="tpu_custom_call" | custom-call | bytes 1048576 | tf_op jit(solution)/shard_map/pallas_call | solution.py:320
Async XLA Ops:
  2.0 28.1 %all-to-all-start = ((bf16[32,8,768]{2,1,0:T(8,128)(2,1)}), bf16[32,8,768]{2,1,0:T(8,128)(2,1)}, u32[]{:S(2)}, u32[]{:S(2)}) async-start(bf16[32,8,768]{2,1,0:T(8,128)(2,1)} %bitcast.3), calls=%async_computation | async-start | bytes 786432 | tf_op jit(solution)/shard_map/all_to_all | solution.py:353
  14.6 0.7 copy-start
  32.9 8.8 %collective-permute-start = (bf16[64,768]{1,0:T(8,128)(2,1)S(1)}, bf16[64,768]{1,0:T(8,128)(2,1)S(1)}, u32[]{:S(2)}, u32[]{:S(2)}) collective-permute-start(bf16[64,768]{1,0:T(8,128)(2,1)S(1)} %shard_map.111), channel_id=1, source_target_pairs={{0,4},{4,8},{8,12},{12,16},{16,20},{20,24},{24,28},{28,32},{32,36}... | collective-permute-start | bytes 294920 | tf_op jit(solution)/shard_map/ppermute | solution.py:387
  38.8 16.1 %copy-start.1 = (bf16[9,192,768]{2,1,0:T(8,128)(2,1)S(1)}, bf16[9,192,768]{2,1,0:T(8,128)(2,1)}, u32[]{:S(2)}) copy-start(bf16[9,192,768]{2,1,0:T(8,128)(2,1)} %get-tuple-element.28.weight_ref) | copy-start | bytes 7962628

commit v10 on v9

--- a/solution.py
+++ b/solution.py
@@ -245,12 +245,12 @@
     copy.start()
     rows_ref[...] = dot(table_ref[...], packed_ref[...]).astype(BF16)
     norm_first(rows_ref, wide_ref, same_wide_ref[...], taps_ref)
-    copy.wait()
-    rest_ref[...] = dot_nt(rows_ref[...], select_ref[...]).astype(BF16)
     for b in range(3):
         head_ref[b] = taps_ref[b, 0:32, :]
     hidden = convolve(taps_ref, with_weights(weight_ref), INNER, keep_ref[EDGE:, :]) + own_ref[0:1]
     act_ref[...] = norm_second(hidden.astype(BF16), own_ref, same_own_ref[...])
+    copy.wait()
+    rest_ref[...] = dot_nt(rows_ref[...], select_ref[...]).astype(BF16)
 
 
 def halo_kernel(

time: 69.2 us -> 69.2 us (level)
  the two profiles are of different devices: /device:TPU:80 before, /device:TPU:72 now
where the time goes in v10:
time: 69.2 us; the launch traced here: 68.7 us
  blocking collectives  25.5 us (37%)
  starting transfers between devices  15.1 us (22%)
  Pallas kernels  14 us (20%)
  waiting for transfers between devices  13.4 us (19%)
    pallas_call x7, Pallas kernels, pinned(): run(*(pltpu.with_memory_space_constraint(a, pltpu.HBM) if m is pltpu.HBM...  14 us
    all_to_all x1, starting transfers between devices, local(): lax.all_to_all(packed.reshape(32, CAP, WIDE), ('ta', 'ha'), 0, 0, axis_in...  12.6 us
    all_gather x1, blocking collectives, local(): acts = lax.all_gather(act, 'ha', axis=0, tiled=False)  11.6 us
    all_to_all x1, blocking collectives, local(): parts = lax.all_to_all(out, 'ha', 0, 0, tiled=True)  11.4 us
    all_to_all x1, waiting for transfers between devices, local(): lax.all_to_all(packed.reshape(32, CAP, WIDE), ('ta', 'ha'), 0, 0, axis_in...  9.99 us
    ppermute x1, waiting for transfers between devices, local(): earlier = lax.ppermute(tail, 'ta', [(i, i + 1) for i in range(n_ta - 1)])  3.38 us
    all_gather x1, blocking collectives, local(): lax.all_gather(arrived, 'ha', axis=0, axis_index_groups=chips, tiled=True)  2.57 us
    ppermute x1, starting transfers between devices, local(): earlier = lax.ppermute(tail, 'ta', [(i, i + 1) for i in range(n_ta - 1)])  2.51 us
  transfers between devices with their start and end apart: 2, of which 2 were waited for; matrix products, arithmetic and copies ran while one was open for 0% of the time, Pallas kernels for 11%

profile of v10, /device:TPU:72, one launch (start us, length us, event | category | flops | bytes accessed | tf_op | source)
XLA Modules:
  0.0 68.7 jit_solution(3416928068043774189)
XLA Ops:
  0.0 2.0 %shard_map.110 = bf16[256,768]{1,0:T(8,128)(2,1)} custom-call(s32[32,128]{1,0:T(8,128)} %bitcast.7, bf16[64,768]{1,0:T(8,128)(2,1)} %rows_hbm.1), custom_call_target="tpu_custom_call" | custom-call | flops 10000000 | bytes 1048576 | tf_op jit(solution)/shard_map/pallas_call | solution.py:320
  2.0 12.6 %all-to-all-start = ((bf16[32,8,768]{2,1,0:T(8,128)(2,1)}), bf16[32,8,768]{2,1,0:T(8,128)(2,1)}, u32[]{:S(2)}, u32[]{:S(2)}) async-start(bf16[32,8,768]{2,1,0:T(8,128)(2,1)} %bitcast.3), calls=%async_computation | async-start | bytes 786432 | tf_op jit(solution)/shard_map/all_to_all | solution.py:353
  14.6 0.0 copy-start
  14.6 0.6 copy-done
  15.3 4.8 %shard_map.109 = (bf16[256,512]{1,0:T(8,128)(2,1)S(1)}, bf16[288,2]{1,0:T(8,128)(2,1)S(1)}, f32[2,384]{1,0:T(2,128)S(1)}, f32[4,192]{1,0:T(4,128)S(1)}, bf16[384...) custom-call(s32[6]{0:T(128)S(1)} %copy-done, ...), custom_call_target="tpu_custom_call" | custom-call | flops 2000000000 | bytes 1048576 | tf_op jit(solution)/shard_map/pallas_call | solution.py:320
  20.1 10.0 %all-to-all-done = bf16[32,8,768]{2,1,0:T(8,128)(2,1)} async-done(((bf16[32,8,768]{2,1,0:T(8,128)(2,1)}), bf16[32,8,768]{2,1,0:T(8,128)(2,1)}, u32[]{:S(2)}, u32[]{:S(2)}) %all-to-all-start) | async-done | bytes 393248 | tf_op jit(solution)/shard_map/all_to_all | solution.py:353
  30.1 2.6 %all_gather.9.packed_ref = bf16[512,768]{1,0:T(8,128)(2,1)S(1)} all-gather(bf16[256,768]{1,0:T(8,128)(2,1)} %bitcast.4), channel_id=1, replica_groups={{0,1},{2,3},{4,5},{6,7},{8,9},{10,11},{12,13},{14,15},{16,17},{18,19},{..., dimensions={0}, use_global_device_ids=true | all-gather | bytes 1179648 | tf_op jit(solution)/shard_map/all_gather | solution.py:385
  32.6 0.3 shard_map.111
  32.9 2.5 %collective-permute-start = (bf16[64,768]{1,0:T(8,128)(2,1)S(1)}, bf16[64,768]{1,0:T(8,128)(2,1)S(1)}, u32[]{:S(2)}, u32[]{:S(2)}) collective-permute-start(bf16[64,768]{1,0:T(8,128)(2,1)S(1)} %shard_map.111), channel_id=1, source_target_pairs={{0,4},{4,8},{8,12},{12,16},{16,20},{20,24},{24,28},{28,32},{32,36}... | collective-permute-start | bytes 294920 | tf_op jit(solution)/shard_map/ppermute | solution.py:387
  35.4 2.9 %shard_map.112 = (bf16[336,128]{1,0:T(8,128)(2,1)S(1)}, bf16[256,192]{1,0:T(8,128)(2,1)S(1)}, bf16[3,32,768]{2,1,0:T(8,128)(2,1)S(1)}) custom-call(bf16[288,2]{1,0:T(8,128)(2,1)S(1)} %get-tuple-element.17.keep_ref, bf16[256,512]{1,0:T(8,128)(2,1)S(1)} %get-tuple-element.18.table_ref, bf16[512,768]{1,0:T(8,128)(2,1)S(1)} %all_gather.9.packed_ref, ...), custom_call_target="tpu_custom_call" | custom-call | flops 2000000000 | bytes 1048576 | tf_op jit(solution)/shard_map/pallas_call | solution.py:320
  38.3 0.0 copy-start.1
  38.3 3.4 %collective-permute-done.earlier_ref = bf16[64,768]{1,0:T(8,128)(2,1)S(1)} collective-permute-done((bf16[64,768]{1,0:T(8,128)(2,1)S(1)}, bf16[64,768]{1,0:T(8,128)(2,1)S(1)}, u32[]{:S(2)}, u32[]{:S(2)}) %collective-permute-start) | collective-permute-done | bytes 98336 | tf_op jit(solution)/shard_map/ppermute | solution.py:387
  41.7 1.6 %shard_map.113 = bf16[432,128]{1,0:T(8,128)(2,1)S(1)} custom-call(bf16[288,2]{1,0:T(8,128)(2,1)S(1)} %get-tuple-element.17.keep_ref, bf16[64,768]{1,0:T(8,128)(2,1)S(1)} %collective-permute-done.earlier_ref, bf16[3,32,768]{2,1,0:T(8,128)(2,1)S(1)} %get-tuple-element.25.head_ref, f32[2,384]{1,0:T(2,128)S(1)} %get-tuple-element.19.wide_ref, ...), custom_call_target="tpu_custom_call" | custom-call | flops 1000000000 | bytes 1048576 | tf_op jit(solution)/shard_map/pallas_call | solution.py:320
  43.3 11.6 %all-gather = bf16[1728,128]{1,0:T(8,128)(2,1)S(1)} all-gather(bf16[432,128]{1,0:T(8,128)(2,1)S(1)} %shard_map.113), channel_id=2, replica_groups=mesh['dp'=8,'ta'=16,'ha'=4] {'ha'}, dimensions={0}, use_global_device_ids=true | all-gather | bytes 552960 | tf_op jit(solution)/shard_map/all_gather | solution.py:402
  54.9 0.0 copy-done.1
  54.9 1.6 %shard_map.114 = bf16[4,96,128]{2,1,0:T(8,128)(2,1)S(1)} custom-call(bf16[288,2]{1,0:T(8,128)(2,1)S(1)} %get-tuple-element.17.keep_ref, bf16[4,432,128]{2,1,0:T(8,128)(2,1)S(1)} %bitcast.6, bf16[256,192]{1,0:T(8,128)(2,1)S(1)} %get-tuple-element.27.rest_ref, f32[4,192]{1,0:T(4,128)S(1)} %get-tuple-element.20.own_ref, bf16[9,192,768]{2,1,0:T(8,128)(2,1)S(1)} %copy-done.1), custom_call_target="tpu_custom_call" | custom-call | flops 2000000000 | bytes 1048576 | tf_op jit(solution)/shard_map/pallas_call | solution.py:320
  56.5 11.4 %all_to_all.10.parts_ref = bf16[4,96,128]{2,1,0:T(8,128)(2,1)S(1)} all-to-all(bf16[4,96,128]{2,1,0:T(8,128)(2,1)S(1)} %shard_map.114), channel_id=1, replica_groups=mesh['dp'=8,'ta'=16,'ha'=4] {'ha'}, dimensions={0} | all-to-all | bytes 196608 | tf_op jit(solution)/shard_map/all_to_all | solution.py:410
  67.8 0.9 %shard_map.115 = bf16[16,4,2,384]{3,2,1,0:T(2,128)(2,1)} custom-call(bf16[4,96,128]{2,1,0:T(8,128)(2,1)S(1)} %all_to_all.10.parts_ref), custom_call_target="tpu_custom_call" | custom-call | bytes 1048576 | tf_op jit(solution)/shard_map/pallas_call | solution.py:320
Async XLA Ops:
  2.0 28.1 %all-to-all-start = ((bf16[32,8,768]{2,1,0:T(8,128)(2,1)}), bf16[32,8,768]{2,1,0:T(8,128)(2,1)}, u32[]{:S(2)}, u32[]{:S(2)}) async-start(bf16[32,8,768]{2,1,0:T(8,128)(2,1)} %bitcast.3), calls=%async_computation | async-start | bytes 786432 | tf_op jit(solution)/shard_map/all_to_all | solution.py:353
  14.6 0.7 copy-start
  32.9 8.8 %collective-permute-start = (bf16[64,768]{1,0:T(8,128)(2,1)S(1)}, bf16[64,768]{1,0:T(8,128)(2,1)S(1)}, u32[]{:S(2)}, u32[]{:S(2)}) collective-permute-start(bf16[64,768]{1,0:T(8,128)(2,1)S(1)} %shard_map.111), channel_id=1, source_target_pairs={{0,4},{4,8},{8,12},{12,16},{16,20},{20,24},{24,28},{28,32},{32,36}... | collective-permute-start | bytes 294920 | tf_op jit(solution)/shard_map/ppermute | solution.py:387
  38.3 16.5 %copy-start.1 = (bf16[9,192,768]{2,1,0:T(8,128)(2,1)S(1)}, bf16[9,192,768]{2,1,0:T(8,128)(2,1)}, u32[]{:S(2)}) copy-start(bf16[9,192,768]{2,1,0:T(8,128)(2,1)} %get-tuple-element.28.weight_ref) | copy-start | bytes 7962628
